TPU v7x, 128 devices: a whole 4x4x4 slice. The times are simulated.
128 devices in a mesh: cast: 8 (over x_lo, z), width: 8 (over y, x_hi), thick: 2 (over core).
Axes of the slice: x: 4 (x_hi: 2, x_lo: 2; x = x_hi * 2 + x_lo), y: 4, z: 4, core: 2. Of those that a mesh axis runs over, the one named last changes fastest.
Arguments:
- velocity: float32 [3, 512, 256, 512], P(None, 'cast', ('width', 'thick')), may hold values from -6 to 6
- magnetic: float32 [3, 512, 256, 512], P(None, 'cast', ('width', 'thick')), may hold values from -6 to 6
- labels: int32 [512, 256, 512], P('cast', ('width', 'thick')), may hold values from 0 to 2
- viscosity: float32 [512, 256, 512], P('cast', ('width', 'thick')), may hold values from 0.05 to 0.5
Outputs:
- velocity_next: float32 [3, 512, 256, 512], P(None, 'cast', ('width', 'thick'))
- potential: float32 [512, 256, 512], P('cast', ('width', 'thick'))
All inputs are finite; a program needn't handle non-finite values.
Results may differ from a plain program's by a relative error of at most 0.00002.
Values sent between devices are 32-bit elements; how exact they have to be, the bound alone decides.
No kernel may reach another device: no remote copies, remote signals or barrier semaphores. Data moves between devices by JAX's collectives and lax.ppermute only.
A program may use at most 192 MiB of HBM per device.

v0:
```python
import math

import jax
import jax.numpy as jnp
from jax import lax
from jax.sharding import PartitionSpec as P

ITERS = 4


time_step = 0.1
force_gain = 0.3


def with_halo(block, sides, width):
    for axis, dim in sides:
        count = lax.axis_size(axis)
        forward = [(i, i + 1) for i in range(count - 1)]
        backward = [(target, source) for source, target in forward]
        low = lax.ppermute(
            lax.slice_in_dim(block, block.shape[dim] - width, None, axis=dim), axis, forward
        )
        high = lax.ppermute(lax.slice_in_dim(block, 0, width, axis=dim), axis, backward)
        block = jnp.concatenate([low, block, high], axis=dim)
    return block


def conductivity(labels):
    return jnp.where(labels == 0, 1.0, jnp.where(labels == 1, 0.7, 4.0)).astype(jnp.float32)


def neighbour(padded, dim, step):
    leading = padded.ndim - 3
    count = padded.shape[leading + dim]
    index = [slice(None)] * leading + [slice(1, -1)] * 3
    index[leading + dim] = slice(1 + step, count - 1 + step)
    return padded[tuple(index)]


def center(padded):
    leading = padded.ndim - 3
    return padded[tuple([slice(None)] * leading + [slice(1, -1)] * 3)]


def cross(left, right):
    return jnp.stack(
        [
            left[1] * right[2] - left[2] * right[1],
            left[2] * right[0] - left[0] * right[2],
            left[0] * right[1] - left[1] * right[0],
        ]
    )


def sweep_weight(k):
    return 2.0 / (2.15 + 1.75 * math.cos(math.pi * (2 * k + 1) / (2 * ITERS)))


def pad_depth(field):
    return jnp.pad(field, [(0, 0)] * (field.ndim - 1) + [(1, 1)])


def potential_pad(potential):
    extended = with_halo(potential, (("cast", 0), (("width", "thick"), 1)), 1)
    return pad_depth(extended)


def prepare(sig_pad, field_pad):
    sig_c = center(sig_pad)
    field_c = center(field_pad)
    faces = []
    source = jnp.zeros_like(sig_c)
    diag = 0.05 * sig_c
    for dim in range(3):
        for step in (1, -1):
            sig_n = neighbour(sig_pad, dim, step)
            face = 2.0 * sig_c * sig_n / (sig_c + sig_n)
            faces.append((dim, step, face))
            source = (
                source + step * face * (field_c[dim] + neighbour(field_pad[dim], dim, step)) * 0.5
            )
            diag = diag + face
    return (faces, source, diag)


def relax(phi_pad, faces, source, diag, omega):
    phi = center(phi_pad)
    total = jnp.zeros_like(phi)
    for dim, step, face in faces:
        total = total + face * neighbour(phi_pad, dim, step)
    return phi + omega * ((total - source) / diag - phi)


def lorentz(phi_pad, sigma, field, magnetic):
    grads = [0.5 * (neighbour(phi_pad, d, 1) - neighbour(phi_pad, d, -1)) for d in range(3)]
    current = jnp.stack([sigma * (field[d] - grads[d]) for d in range(3)])
    return cross(current, magnetic)


def predict(vel_pad, visc_pad, force):
    vel = center(vel_pad)
    visc = center(visc_pad)
    result = []
    for comp in range(3):
        advect = jnp.zeros_like(visc)
        spread = jnp.zeros_like(visc)
        for dim in range(3):
            upper = neighbour(vel_pad[comp], dim, 1)
            lower = neighbour(vel_pad[comp], dim, -1)
            advect = advect + vel[dim] * (upper - lower) * 0.5
            spread = spread + 0.5 * (visc + neighbour(visc_pad, dim, 1)) * (upper - vel[comp])
            spread = spread + 0.5 * (visc + neighbour(visc_pad, dim, -1)) * (lower - vel[comp])
        result.append(vel[comp] + time_step * (spread - advect) + force_gain * force[comp])
    return jnp.stack(result)


def local(velocity, magnetic, labels, viscosity):
    sigma = conductivity(labels)
    field = cross(velocity, magnetic)
    stacked = jnp.concatenate([sigma[None], field], axis=0)
    stacked_pad = pad_depth(with_halo(stacked, (("cast", 1), (("width", "thick"), 2)), 1))
    faces, source, diag = prepare(stacked_pad[0], stacked_pad[1:])
    potential = jnp.zeros_like(sigma)
    for k in range(ITERS):
        potential = relax(potential_pad(potential), faces, source, diag, sweep_weight(k))
    force = lorentz(potential_pad(potential), sigma, field, magnetic)
    flow = jnp.concatenate([velocity, viscosity[None]], axis=0)
    flow_pad = pad_depth(with_halo(flow, (("cast", 1), (("width", "thick"), 2)), 1))
    velocity_next = predict(flow_pad[:3], flow_pad[3], force)
    return (velocity_next, potential)


def solution(mesh):
    placed = (
        P(None, "cast", ("width", "thick"), None),
        P(None, "cast", ("width", "thick"), None),
        P("cast", ("width", "thick"), None),
        P("cast", ("width", "thick"), None),
    )
    return jax.shard_map(
        local,
        mesh=mesh,
        in_specs=placed,
        out_specs=(P(None, "cast", ("width", "thick"), None), P("cast", ("width", "thick"), None)),
        check_vma=False,
    )
```

profile of v0, /device:TPU:15, one launch (start us, length us, event | category | flops | bytes accessed | tf_op | source)
XLA Modules:
  0.0 326.2 jit_solution(17320938540843167707)
XLA Ops:
  0.6 5.9 %collective-permute-start.8 = (f32[1,16,512]{2,1,0:T(8,128)S(1)}, f32[1,16,512]{2,1,0:T(8,128)S(1)}, u32[]{:S(2)}, u32[]{:S(2)}) collective-permute-start(f32[1,16,512]{2,1,0:T(8,128)S(1)} %broadcast.39), channel_id=1, source_target_pairs={{16,0},{32,16},{48,32},{64,48},{80,64},{96,80},{112,96},{17,1},{33... | collective-permute-start | bytes 98312 | tf_op jit(solution)/shard_map/ppermute | solution.py:23
  11.7 6.2 %multiply_subtract_fusion.2 = (f32[1,64,16,512]{3,2,1,0:T(8,128)S(1)}, f32[1,64,16,512]{3,2,1,0:T(8,128)S(1)}, f32[1,64,16,512]{3,2,1,0:T(8,128)S(1)}) fusion(f32[3,64,16,512]{3,2,1,0:T(8,128)} %param.5, f32[3,64,16,512]{3,2,1,0:T(8,128)} %param.4), kind=kLoop, calls=%fused_computation.302 | loop fusion | flops 4718592 | bytes 18874368 | tf_op jit(solution)/shard_map/sub | solution.py:48
  19.9 5.5 %collective-permute-start.5 = (f32[4,1,16,512]{3,2,1,0:T(8,128)S(1)}, f32[4,1,16,512]{3,2,1,0:T(8,128)S(1)}, u32[]{:S(2)}, u32[]{:S(2)}) collective-permute-start(f32[4,1,16,512]{3,2,1,0:T(8,128)S(1)} %get-tuple-element.32), channel_id=1, source_target_pairs={{16,0},{32,16},{48,32},{64,48},{80,64},{96,80},{112,96},{17,1},{33... | collective-permute-start | bytes 393224 | tf_op jit(solution)/shard_map/ppermute | solution.py:23
  26.0 3.4 %collective-permute-start.10 = (f32[66,1,512]{2,1,0:T(1,128)S(1)}, f32[66,1,512]{2,1,0:T(1,128)S(1)}, u32[]{:S(2)}, u32[]{:S(2)}) collective-permute-start(f32[66,1,512]{2,1,0:T(1,128)S(1)} %get-tuple-element.44), channel_id=1, source_target_pairs={{1,0},{2,1},{3,2},{4,3},{5,4},{6,5},{7,6},{8,7},{9,8},{10,9},{11,1... | collective-permute-start | bytes 405512 | tf_op jit(solution)/shard_map/ppermute | solution.py:23
  29.4 4.5 %collective-permute-start.11 = (f32[66,1,512]{2,1,0:T(1,128)S(1)}, f32[66,1,512]{2,1,0:T(1,128)S(1)}, u32[]{:S(2)}, u32[]{:S(2)}) collective-permute-start(f32[66,1,512]{2,1,0:T(1,128)S(1)} %get-tuple-element.43), channel_id=1, source_target_pairs={{0,1},{1,2},{2,3},{3,4},{4,5},{5,6},{6,7},{7,8},{8,9},{9,10},{10,1... | collective-permute-start | bytes 405512 | tf_op jit(solution)/shard_map/ppermute | solution.py:20
  40.6 5.4 %select_maximum_fusion.21 = f32[66,18,514]{2,1,0:T(8,128)} fusion(f32[66,1,512]{2,1,0:T(1,128)S(1)} %collective-permute-done.10, f32[66,1,512]{2,1,0:T(1,128)S(1)} %collective-permute-done.11, f32[1,16,512]{2,1,0:T(8,128)S(1)} %collective-permute-done.8, f32[64,16,512]{2,1,0:T(8,128)S(1)} %broadcast_in_dim.26, f32[1,16,512]{2,1,0:T(8,128)S(1)} %collective-permute-done.9), kind=kLoop, calls=%fused_computation.38 | loop fusion | flops 7327584 | bytes 4875552 | tf_op jit(solution)/shard_map/concatenate | solution.py:24
  46.5 5.5 %collective-permute-done.7 = f32[4,66,1,512]{3,2,1,0:T(1,128)S(1)} collective-permute-done((f32[4,66,1,512]{3,2,1,0:T(1,128)S(1)}, f32[4,66,1,512]{3,2,1,0:T(1,128)S(1)}, u32[]{:S(2)}, u32[]{:S(2)}) %collective-permute-start.7) | collective-permute-done | bytes 540704 | tf_op jit(solution)/shard_map/ppermute | solution.py:23
  51.9 6.4 %pad_maximum_fusion = f32[4,66,18,512]{3,2,1,0:T(8,128)} fusion(f32[4,66,1,512]{3,2,1,0:T(1,128)S(1)} %collective-permute-done.7, f32[4,1,16,512]{3,2,1,0:T(8,128)S(1)} %collective-permute-done.5, f32[1,64,16,512]{3,2,1,0:T(8,128)S(1)} %get-tuple-element.26, f32[1,64,16,512]{3,2,1,0:T(8,128)S(1)} %get-tuple-element.25, ...), kind=kLoop, calls=%fused_computation.12 | loop fusion | flops 17031168 | bytes 19464192 | tf_op jit(solution)/shard_map/concatenate | solution.py:24
  58.3 9.8 %fusion.2 = (f32[66,18,514]{2,1,0:T(8,128)}, f32[66,18,514]{2,1,0:T(8,128)}, f32[66,18,514]{2,1,0:T(8,128)}, f32[66,18,514]{2,1,0:T(8,128)S(1)}) fusion(f32[4,66,18,512]{3,2,1,0:T(8,128)} %pad_maximum_fusion), kind=kLoop, calls=%fused_computation.17 | loop fusion | bytes 19502208 | tf_op jit(solution)/shard_map/squeeze | solution.py:80
  68.1 20.0 %fusion.154 = (f32[64,16,512]{2,1,0:T(8,128)S(1)}, f32[64,16,512]{2,1,0:T(8,128)S(1)}, f32[64,16,512]{2,1,0:T(8,128)}, f32[64,16,512]{2,1,0:T(8,128)}, f32[64,16...) fusion(f32[66,18,514]{2,1,0:T(8,128)} %select_maximum_fusion.21, ...), kind=kLoop, calls=%fused_computation.305 | loop fusion | flops 35127296 | bytes 56958976 | tf_op jit(solution)/shard_map/mul | solution.py:91
  88.2 3.7 %collective-permute-start.12 = (f32[1,16,512]{2,1,0:T(8,128)S(1)}, f32[1,16,512]{2,1,0:T(8,128)S(1)}, u32[]{:S(2)}, u32[]{:S(2)}) collective-permute-start(f32[1,16,512]{2,1,0:T(8,128)S(1)} %get-tuple-element.52), channel_id=1, source_target_pairs={{16,0},{32,16},{48,32},{64,48},{80,64},{96,80},{112,96},{17,1},{33... | collective-permute-start | bytes 98312 | tf_op jit(solution)/shard_map/ppermute | solution.py:23
  93.9 4.8 %collective-permute-done.13 = f32[1,16,512]{2,1,0:T(8,128)S(1)} collective-permute-done((f32[1,16,512]{2,1,0:T(8,128)S(1)}, f32[1,16,512]{2,1,0:T(8,128)S(1)}, u32[]{:S(2)}, u32[]{:S(2)}) %collective-permute-start.13) | collective-permute-done | bytes 32800 | tf_op jit(solution)/shard_map/ppermute | solution.py:20
  100.9 6.5 %collective-permute-start.15 = (f32[66,1,512]{2,1,0:T(1,128)S(1)}, f32[66,1,512]{2,1,0:T(1,128)S(1)}, u32[]{:S(2)}, u32[]{:S(2)}) collective-permute-start(f32[66,1,512]{2,1,0:T(1,128)S(1)} %get-tuple-element.41), channel_id=1, source_target_pairs={{0,1},{1,2},{2,3},{3,4},{4,5},{5,6},{6,7},{7,8},{8,9},{9,10},{10,1... | collective-permute-start | bytes 405512 | tf_op jit(solution)/shard_map/ppermute | solution.py:20
  109.2 5.4 %select_maximum_fusion.17 = f32[66,18,514]{2,1,0:T(8,128)} fusion(f32[66,1,512]{2,1,0:T(1,128)S(1)} %collective-permute-done.14, f32[66,1,512]{2,1,0:T(1,128)S(1)} %collective-permute-done.15, f32[1,16,512]{2,1,0:T(8,128)S(1)} %collective-permute-done.12, f32[64,16,512]{2,1,0:T(8,128)S(1)} %get-tuple-element.5, f32[1,16,512]{2,1,0:T(8,128)S(1)} %collective-permute-done.13), kind=kLoop, calls=%fused_computation.34 | loop fusion | flops 7327584 | bytes 4875552 | tf_op jit(solution)/shard_map/concatenate | solution.py:24
  114.6 9.5 %fusion.59 = f32[64,16,512]{2,1,0:T(8,128)S(1)} fusion(f32[64,16,512]{2,1,0:T(8,128)S(1)} %get-tuple-element.5, f32[64,16,512]{2,1,0:T(8,128)S(1)} %get-tuple-element.6, f32[64,16,512]{2,1,0:T(8,128)} %get-tuple-element.12, f32[66,18,514]{2,1,0:T(8,128)} %select_maximum_fusion.17, f32[64,16,512]{2,1,0:T(8,128)} %get-tuple-element.11, ...), kind=kLoop, calls=%fused_computation.130 | loop fusion | flops 16252928 | bytes 25501696 | tf_op jit(solution)/shard_map/add | solution.py:91
  133.1 4.7 %collective-permute-start.18 = (f32[66,1,512]{2,1,0:T(1,128)S(1)}, f32[66,1,512]{2,1,0:T(1,128)S(1)}, u32[]{:S(2)}, u32[]{:S(2)}) collective-permute-start(f32[66,1,512]{2,1,0:T(1,128)S(1)} %get-tuple-element.40), channel_id=1, source_target_pairs={{1,0},{2,1},{3,2},{4,3},{5,4},{6,5},{7,6},{8,7},{9,8},{10,9},{11,1... | collective-permute-start | bytes 405512 | tf_op jit(solution)/shard_map/ppermute | solution.py:23
  137.8 5.8 %collective-permute-start.19 = (f32[66,1,512]{2,1,0:T(1,128)S(1)}, f32[66,1,512]{2,1,0:T(1,128)S(1)}, u32[]{:S(2)}, u32[]{:S(2)}) collective-permute-start(f32[66,1,512]{2,1,0:T(1,128)S(1)} %get-tuple-element.39), channel_id=1, source_target_pairs={{0,1},{1,2},{2,3},{3,4},{4,5},{5,6},{6,7},{7,8},{8,9},{9,10},{10,1... | collective-permute-start | bytes 405512 | tf_op jit(solution)/shard_map/ppermute | solution.py:20
  145.6 5.4 %select_maximum_fusion.13 = f32[66,18,514]{2,1,0:T(8,128)} fusion(f32[66,1,512]{2,1,0:T(1,128)S(1)} %collective-permute-done.18, f32[66,1,512]{2,1,0:T(1,128)S(1)} %collective-permute-done.19, f32[1,16,512]{2,1,0:T(8,128)S(1)} %collective-permute-done.16, f32[64,16,512]{2,1,0:T(8,128)S(1)} %fusion.59, f32[1,16,512]{2,1,0:T(8,128)S(1)} %collective-permute-done.17), kind=kLoop, calls=%fused_computation.30 | loop fusion | flops 7327584 | bytes 4875552 | tf_op jit(solution)/shard_map/concatenate | solution.py:24
  151.1 14.4 %fusion.45 = f32[64,16,512]{2,1,0:T(8,128)S(1)} fusion(f32[64,16,512]{2,1,0:T(8,128)} %copy-done.1, f32[64,16,512]{2,1,0:T(8,128)S(1)} %copy-done.3, f32[64,16,512]{2,1,0:T(8,128)} %get-tuple-element.12, f32[66,18,514]{2,1,0:T(8,128)} %select_maximum_fusion.13, f32[64,16,512]{2,1,0:T(8,128)} %get-tuple-element.11, f32[64,16,512]{2,1,0:T(8,128)} %get-tuple-element.10, ...), kind=kLoop, calls=%fused_computation.106 | loop fusion | flops 16252928 | bytes 25501696 | tf_op jit(solution)/shard_map/add | solution.py:91
  173.7 5.5 %collective-permute-start.1 = (f32[4,1,16,512]{3,2,1,0:T(8,128)S(1)}, f32[4,1,16,512]{3,2,1,0:T(8,128)S(1)}, u32[]{:S(2)}, u32[]{:S(2)}) collective-permute-start(f32[4,1,16,512]{3,2,1,0:T(8,128)S(1)} %get-tuple-element.34), channel_id=1, source_target_pairs={{16,0},{32,16},{48,32},{64,48},{80,64},{96,80},{112,96},{17,1},{33... | collective-permute-start | bytes 393224 | tf_op jit(solution)/shard_map/ppermute | solution.py:23
  182.7 6.6 %collective-permute-start.23 = (f32[66,1,512]{2,1,0:T(1,128)S(1)}, f32[66,1,512]{2,1,0:T(1,128)S(1)}, u32[]{:S(2)}, u32[]{:S(2)}) collective-permute-start(f32[66,1,512]{2,1,0:T(1,128)S(1)} %get-tuple-element.37), channel_id=1, source_target_pairs={{0,1},{1,2},{2,3},{3,4},{4,5},{5,6},{6,7},{7,8},{8,9},{9,10},{10,1... | collective-permute-start | bytes 405512 | tf_op jit(solution)/shard_map/ppermute | solution.py:20
  195.7 5.4 %select_maximum_fusion.9 = f32[66,18,514]{2,1,0:T(8,128)} fusion(f32[66,1,512]{2,1,0:T(1,128)S(1)} %collective-permute-done.22, f32[66,1,512]{2,1,0:T(1,128)S(1)} %collective-permute-done.23, f32[1,16,512]{2,1,0:T(8,128)S(1)} %collective-permute-done.20, f32[64,16,512]{2,1,0:T(8,128)S(1)} %fusion.45, f32[1,16,512]{2,1,0:T(8,128)S(1)} %collective-permute-done.21), kind=kLoop, calls=%fused_computation.26 | loop fusion | flops 7327584 | bytes 4875552 | tf_op jit(solution)/shard_map/concatenate | solution.py:24
  201.2 10.3 %fusion.31 = f32[64,16,512]{2,1,0:T(8,128)S(1)} fusion(f32[64,16,512]{2,1,0:T(8,128)S(1)} %fusion.45, f32[64,16,512]{2,1,0:T(8,128)} %copy-done.2, f32[64,16,512]{2,1,0:T(8,128)} %get-tuple-element.12, f32[66,18,514]{2,1,0:T(8,128)} %select_maximum_fusion.9, f32[64,16,512]{2,1,0:T(8,128)} %get-tuple-element.11, f32[64,16,512]{2,1,0:T(8,128)} %get-tuple-element.10, ...), kind=kLoop, calls=%fused_computation.82 | loop fusion | flops 16252928 | bytes 25501696 | tf_op jit(solution)/shard_map/add | solution.py:91
  213.5 5.5 %collective-permute-start.25 = (f32[1,16,512]{2,1,0:T(8,128)S(1)}, f32[1,16,512]{2,1,0:T(8,128)S(1)}, u32[]{:S(2)}, u32[]{:S(2)}) collective-permute-start(f32[1,16,512]{2,1,0:T(8,128)S(1)} %get-tuple-element.46), channel_id=1, source_target_pairs={{16,0},{32,16},{48,32},{64,48},{80,64},{96,80},{112,96},{17,1},{33... | collective-permute-start | bytes 98312 | tf_op jit(solution)/shard_map/ppermute | solution.py:23
  219.0 20.8 %select_maximum_fusion = f32[4,66,18,514]{3,2,1,0:T(8,128)} fusion(f32[4,66,1,512]{3,2,1,0:T(1,128)S(1)} %collective-permute-done.3, f32[4,66,1,512]{3,2,1,0:T(1,128)S(1)} %collective-permute-done.2, f32[4,1,16,512]{3,2,1,0:T(8,128)} %copy-done.12, f32[4,1,16,512]{3,2,1,0:T(8,128)S(1)} %collective-permute-done, f32[1,64,16,512]{3,2,1,0:T(8,128)} %bitcast.321, ...), kind=kLoop, calls=%fused_computation.6 | loop fusion | flops 34195392 | bytes 19502208 | tf_op jit(solution)/shard_map/concatenate | solution.py:24
  242.6 6.3 %collective-permute-start.27 = (f32[66,1,512]{2,1,0:T(1,128)S(1)}, f32[66,1,512]{2,1,0:T(1,128)S(1)}, u32[]{:S(2)}, u32[]{:S(2)}) collective-permute-start(f32[66,1,512]{2,1,0:T(1,128)S(1)} %get-tuple-element.35), channel_id=1, source_target_pairs={{0,1},{1,2},{2,3},{3,4},{4,5},{5,6},{6,7},{7,8},{8,9},{9,10},{10,1... | collective-permute-start | bytes 405512 | tf_op jit(solution)/shard_map/ppermute | solution.py:20
  248.9 10.7 %slice_bitcast_fusion.1 = (f32[66,18,514]{2,1,0:T(8,128)}, f32[66,18,514]{2,1,0:T(8,128)}, f32[66,18,514]{2,1,0:T(8,128)S(1)}, f32[66,18,514]{2,1,0:T(8,128)}) fusion(f32[4,66,18,514]{3,2,1,0:T(8,128)} %select_maximum_fusion), kind=kLoop, calls=%fused_computation.21 | loop fusion | bytes 19540224 | tf_op jit(solution)/shard_map/squeeze | solution.py:108
  259.6 5.5 %select_maximum_fusion.5 = f32[66,18,514]{2,1,0:T(8,128)} fusion(f32[66,1,512]{2,1,0:T(1,128)S(1)} %collective-permute-done.26, f32[66,1,512]{2,1,0:T(1,128)S(1)} %collective-permute-done.27, f32[1,16,512]{2,1,0:T(8,128)S(1)} %collective-permute-done.25, f32[64,16,512]{2,1,0:T(8,128)S(1)} %fusion.31, f32[1,16,512]{2,1,0:T(8,128)S(1)} %collective-permute-done.24), kind=kLoop, calls=%fused_computation.22 | loop fusion | flops 7327584 | bytes 4875552 | tf_op jit(solution)/shard_map/concatenate | solution.py:24
  265.1 19.8 %fusion.92 = (f32[1,64,16,512]{3,2,1,0:T(8,128)}, f32[64,16,512]{2,1,0:T(8,128)}, f32[64,16,512]{2,1,0:T(8,128)S(1)}) fusion(f32[66,18,514]{2,1,0:T(8,128)} %get-tuple-element.17, f32[3,64,16,512]{3,2,1,0:T(8,128)} %param.5, f32[3,64,16,512]{3,2,1,0:T(8,128)S(1)} %bitcast.317, f32[66,18,514]{2,1,0:T(8,128)S(1)} %get-tuple-element.18, ...), kind=kLoop, calls=%fused_computation.196 | loop fusion | flops 35651584 | bytes 53813248 | tf_op jit(solution)/shard_map/stack | solution.py:114
  284.9 17.1 %fusion.102 = f32[1,64,16,512]{3,2,1,0:T(8,128)} fusion(f32[64,16,512]{2,1,0:T(8,128)} %get-tuple-element.3, f32[66,18,514]{2,1,0:T(8,128)} %get-tuple-element.16, f32[64,16,512]{2,1,0:T(8,128)S(1)} %fusion.31, f32[1,16,512]{2,1,0:T(8,128)S(1)} %collective-permute-done.24, f32[1,16,512]{2,1,0:T(8,128)S(1)} %collective-permute-done.25, ...), kind=kLoop, calls=%fused_computation.210 | loop fusion | flops 29884416 | bytes 47251456 | tf_op jit(solution)/shard_map/stack | solution.py:114
  302.0 16.8 %fusion.97 = f32[1,64,16,512]{3,2,1,0:T(8,128)} fusion(f32[64,16,512]{2,1,0:T(8,128)S(1)} %get-tuple-element.4, f32[66,18,514]{2,1,0:T(8,128)} %get-tuple-element.19, f32[64,16,512]{2,1,0:T(8,128)S(1)} %fusion.31, f32[1,16,512]{2,1,0:T(8,128)S(1)} %collective-permute-done.24, f32[1,16,512]{2,1,0:T(8,128)S(1)} %collective-permute-done.25, ...), kind=kLoop, calls=%fused_computation.201 | loop fusion | flops 29884416 | bytes 47251456 | tf_op jit(solution)/shard_map/stack | solution.py:114
  318.8 6.9 %pad_maximum_fusion.1 = f32[3,64,16,512]{3,2,1,0:T(8,128)} fusion(f32[1,64,16,512]{3,2,1,0:T(8,128)} %fusion.97, f32[1,64,16,512]{3,2,1,0:T(8,128)} %fusion.102, f32[1,64,16,512]{3,2,1,0:T(8,128)} %get-tuple-element.2), kind=kLoop, calls=%fused_computation.13 | loop fusion | flops 3145728 | bytes 12582912 | tf_op jit(solution)/shard_map/stack | solution.py:114
  (94 shorter events, 54.2 us)
Async XLA Ops:
  0.6 24.8 %collective-permute-start.8 = (f32[1,16,512]{2,1,0:T(8,128)S(1)}, f32[1,16,512]{2,1,0:T(8,128)S(1)}, u32[]{:S(2)}, u32[]{:S(2)}) collective-permute-start(f32[1,16,512]{2,1,0:T(8,128)S(1)} %broadcast.39), channel_id=1, source_target_pairs={{16,0},{32,16},{48,32},{64,48},{80,64},{96,80},{112,96},{17,1},{33... | collective-permute-start | bytes 98312 | tf_op jit(solution)/shard_map/ppermute | solution.py:23
  6.6 18.9 %collective-permute-start.9 = (f32[1,16,512]{2,1,0:T(8,128)S(1)}, f32[1,16,512]{2,1,0:T(8,128)S(1)}, u32[]{:S(2)}, u32[]{:S(2)}) collective-permute-start(f32[1,16,512]{2,1,0:T(8,128)S(1)} %broadcast.39), channel_id=1, source_target_pairs={{0,16},{16,32},{32,48},{48,64},{64,80},{80,96},{96,112},{1,17},{17... | collective-permute-start | bytes 98312 | tf_op jit(solution)/shard_map/ppermute | solution.py:20
  18.0 15.9 %collective-permute-start.4 = (f32[4,1,16,512]{3,2,1,0:T(8,128)S(1)}, f32[4,1,16,512]{3,2,1,0:T(8,128)S(1)}, u32[]{:S(2)}, u32[]{:S(2)}) collective-permute-start(f32[4,1,16,512]{3,2,1,0:T(8,128)S(1)} %get-tuple-element.31), channel_id=1, source_target_pairs={{0,16},{16,32},{32,48},{48,64},{64,80},{80,96},{96,112},{1,17},{17... | collective-permute-start | bytes 393224 | tf_op jit(solution)/shard_map/ppermute | solution.py:20
  19.9 14.0 %collective-permute-start.5 = (f32[4,1,16,512]{3,2,1,0:T(8,128)S(1)}, f32[4,1,16,512]{3,2,1,0:T(8,128)S(1)}, u32[]{:S(2)}, u32[]{:S(2)}) collective-permute-start(f32[4,1,16,512]{3,2,1,0:T(8,128)S(1)} %get-tuple-element.32), channel_id=1, source_target_pairs={{16,0},{32,16},{48,32},{64,48},{80,64},{96,80},{112,96},{17,1},{33... | collective-permute-start | bytes 393224 | tf_op jit(solution)/shard_map/ppermute | solution.py:23
  26.0 14.6 %collective-permute-start.10 = (f32[66,1,512]{2,1,0:T(1,128)S(1)}, f32[66,1,512]{2,1,0:T(1,128)S(1)}, u32[]{:S(2)}, u32[]{:S(2)}) collective-permute-start(f32[66,1,512]{2,1,0:T(1,128)S(1)} %get-tuple-element.44), channel_id=1, source_target_pairs={{1,0},{2,1},{3,2},{4,3},{5,4},{6,5},{7,6},{8,7},{9,8},{10,9},{11,1... | collective-permute-start | bytes 405512 | tf_op jit(solution)/shard_map/ppermute | solution.py:23
  29.4 11.2 %collective-permute-start.11 = (f32[66,1,512]{2,1,0:T(1,128)S(1)}, f32[66,1,512]{2,1,0:T(1,128)S(1)}, u32[]{:S(2)}, u32[]{:S(2)}) collective-permute-start(f32[66,1,512]{2,1,0:T(1,128)S(1)} %get-tuple-element.43), channel_id=1, source_target_pairs={{0,1},{1,2},{2,3},{3,4},{4,5},{5,6},{6,7},{7,8},{8,9},{9,10},{10,1... | collective-permute-start | bytes 405512 | tf_op jit(solution)/shard_map/ppermute | solution.py:20
  35.7 10.7 %collective-permute-start.6 = (f32[4,66,1,512]{3,2,1,0:T(1,128)S(1)}, f32[4,66,1,512]{3,2,1,0:T(1,128)S(1)}, u32[]{:S(2)}, u32[]{:S(2)}) collective-permute-start(f32[4,66,1,512]{3,2,1,0:T(1,128)S(1)} %get-tuple-element.27), channel_id=1, source_target_pairs={{0,1},{1,2},{2,3},{3,4},{4,5},{5,6},{6,7},{7,8},{8,9},{9,10},{10,1... | collective-permute-start | bytes 1622024 | tf_op jit(solution)/shard_map/ppermute | solution.py:20
  37.7 14.2 %collective-permute-start.7 = (f32[4,66,1,512]{3,2,1,0:T(1,128)S(1)}, f32[4,66,1,512]{3,2,1,0:T(1,128)S(1)}, u32[]{:S(2)}, u32[]{:S(2)}) collective-permute-start(f32[4,66,1,512]{3,2,1,0:T(1,128)S(1)} %get-tuple-element.28), channel_id=1, source_target_pairs={{1,0},{2,1},{3,2},{4,3},{5,4},{6,5},{7,6},{8,7},{9,8},{10,9},{11,1... | collective-permute-start | bytes 1622024 | tf_op jit(solution)/shard_map/ppermute | solution.py:23
  88.2 26.5 %copy-start.2 = (f32[64,16,512]{2,1,0:T(8,128)}, f32[64,16,512]{2,1,0:T(8,128)S(1)}, u32[]{:S(2)}) copy-start(f32[64,16,512]{2,1,0:T(8,128)S(1)} %get-tuple-element.6) | copy-start | bytes 6291460
  88.2 5.7 %collective-permute-start.12 = (f32[1,16,512]{2,1,0:T(8,128)S(1)}, f32[1,16,512]{2,1,0:T(8,128)S(1)}, u32[]{:S(2)}, u32[]{:S(2)}) collective-permute-start(f32[1,16,512]{2,1,0:T(8,128)S(1)} %get-tuple-element.52), channel_id=1, source_target_pairs={{16,0},{32,16},{48,32},{64,48},{80,64},{96,80},{112,96},{17,1},{33... | collective-permute-start | bytes 98312 | tf_op jit(solution)/shard_map/ppermute | solution.py:23
  91.9 6.8 %collective-permute-start.13 = (f32[1,16,512]{2,1,0:T(8,128)S(1)}, f32[1,16,512]{2,1,0:T(8,128)S(1)}, u32[]{:S(2)}, u32[]{:S(2)}) collective-permute-start(f32[1,16,512]{2,1,0:T(8,128)S(1)} %get-tuple-element.51), channel_id=1, source_target_pairs={{0,16},{16,32},{32,48},{48,64},{64,80},{80,96},{96,112},{1,17},{17... | collective-permute-start | bytes 98312 | tf_op jit(solution)/shard_map/ppermute | solution.py:20
  99.0 8.7 %collective-permute-start.14 = (f32[66,1,512]{2,1,0:T(1,128)S(1)}, f32[66,1,512]{2,1,0:T(1,128)S(1)}, u32[]{:S(2)}, u32[]{:S(2)}) collective-permute-start(f32[66,1,512]{2,1,0:T(1,128)S(1)} %get-tuple-element.42), channel_id=1, source_target_pairs={{1,0},{2,1},{3,2},{4,3},{5,4},{6,5},{7,6},{8,7},{9,8},{10,9},{11,1... | collective-permute-start | bytes 405512 | tf_op jit(solution)/shard_map/ppermute | solution.py:23
  100.9 8.3 %collective-permute-start.15 = (f32[66,1,512]{2,1,0:T(1,128)S(1)}, f32[66,1,512]{2,1,0:T(1,128)S(1)}, u32[]{:S(2)}, u32[]{:S(2)}) collective-permute-start(f32[66,1,512]{2,1,0:T(1,128)S(1)} %get-tuple-element.41), channel_id=1, source_target_pairs={{0,1},{1,2},{2,3},{3,4},{4,5},{5,6},{6,7},{7,8},{8,9},{9,10},{10,1... | collective-permute-start | bytes 405512 | tf_op jit(solution)/shard_map/ppermute | solution.py:20
  124.1 21.5 %copy-start.1 = (f32[64,16,512]{2,1,0:T(8,128)}, f32[64,16,512]{2,1,0:T(8,128)S(1)}, u32[]{:S(2)}) copy-start(f32[64,16,512]{2,1,0:T(8,128)S(1)} %fusion.59) | copy-start | bytes 6291460
  124.1 5.3 %collective-permute-start.16 = (f32[1,16,512]{2,1,0:T(8,128)S(1)}, f32[1,16,512]{2,1,0:T(8,128)S(1)}, u32[]{:S(2)}, u32[]{:S(2)}) collective-permute-start(f32[1,16,512]{2,1,0:T(8,128)S(1)} %get-tuple-element.50), channel_id=1, source_target_pairs={{16,0},{32,16},{48,32},{64,48},{80,64},{96,80},{112,96},{17,1},{33... | collective-permute-start | bytes 98312 | tf_op jit(solution)/shard_map/ppermute | solution.py:23
  126.1 6.8 %collective-permute-start.17 = (f32[1,16,512]{2,1,0:T(8,128)S(1)}, f32[1,16,512]{2,1,0:T(8,128)S(1)}, u32[]{:S(2)}, u32[]{:S(2)}) collective-permute-start(f32[1,16,512]{2,1,0:T(8,128)S(1)} %get-tuple-element.49), channel_id=1, source_target_pairs={{0,16},{16,32},{32,48},{48,64},{64,80},{80,96},{96,112},{1,17},{17... | collective-permute-start | bytes 98312 | tf_op jit(solution)/shard_map/ppermute | solution.py:20
  133.1 11.2 %collective-permute-start.18 = (f32[66,1,512]{2,1,0:T(1,128)S(1)}, f32[66,1,512]{2,1,0:T(1,128)S(1)}, u32[]{:S(2)}, u32[]{:S(2)}) collective-permute-start(f32[66,1,512]{2,1,0:T(1,128)S(1)} %get-tuple-element.40), channel_id=1, source_target_pairs={{1,0},{2,1},{3,2},{4,3},{5,4},{6,5},{7,6},{8,7},{9,8},{10,9},{11,1... | collective-permute-start | bytes 405512 | tf_op jit(solution)/shard_map/ppermute | solution.py:23
  137.8 7.8 %collective-permute-start.19 = (f32[66,1,512]{2,1,0:T(1,128)S(1)}, f32[66,1,512]{2,1,0:T(1,128)S(1)}, u32[]{:S(2)}, u32[]{:S(2)}) collective-permute-start(f32[66,1,512]{2,1,0:T(1,128)S(1)} %get-tuple-element.39), channel_id=1, source_target_pairs={{0,1},{1,2},{2,3},{3,4},{4,5},{5,6},{6,7},{7,8},{8,9},{9,10},{10,1... | collective-permute-start | bytes 405512 | tf_op jit(solution)/shard_map/ppermute | solution.py:20
  145.6 25.1 %slice-start = ((s8[6291456]{0:T(1024)(128)(4,1)}), s8[4194304]{0:T(1024)(128)(4,1)S(1)}, s32[]{:S(2)}) async-start(s8[6291456]{0:T(1024)(128)(4,1)} %bitcast.316), calls=%async_computation | async-start | bytes 8388608
  165.5 13.7 %collective-permute-start.20 = (f32[1,16,512]{2,1,0:T(8,128)S(1)}, f32[1,16,512]{2,1,0:T(8,128)S(1)}, u32[]{:S(2)}, u32[]{:S(2)}) collective-permute-start(f32[1,16,512]{2,1,0:T(8,128)S(1)} %get-tuple-element.48), channel_id=1, source_target_pairs={{16,0},{32,16},{48,32},{64,48},{80,64},{96,80},{112,96},{17,1},{33... | collective-permute-start | bytes 98312 | tf_op jit(solution)/shard_map/ppermute | solution.py:23
  167.4 11.8 %collective-permute-start.21 = (f32[1,16,512]{2,1,0:T(8,128)S(1)}, f32[1,16,512]{2,1,0:T(8,128)S(1)}, u32[]{:S(2)}, u32[]{:S(2)}) collective-permute-start(f32[1,16,512]{2,1,0:T(8,128)S(1)} %get-tuple-element.47), channel_id=1, source_target_pairs={{0,16},{16,32},{32,48},{48,64},{64,80},{80,96},{96,112},{1,17},{17... | collective-permute-start | bytes 98312 | tf_op jit(solution)/shard_map/ppermute | solution.py:20
  171.6 17.6 %collective-permute-start = (f32[4,1,16,512]{3,2,1,0:T(8,128)S(1)}, f32[4,1,16,512]{3,2,1,0:T(8,128)S(1)}, u32[]{:S(2)}, u32[]{:S(2)}) collective-permute-start(f32[4,1,16,512]{3,2,1,0:T(8,128)S(1)} %get-tuple-element.33), channel_id=1, source_target_pairs={{0,16},{16,32},{32,48},{48,64},{64,80},{80,96},{96,112},{1,17},{17... | collective-permute-start | bytes 393224 | tf_op jit(solution)/shard_map/ppermute | solution.py:20
  173.7 15.6 %collective-permute-start.1 = (f32[4,1,16,512]{3,2,1,0:T(8,128)S(1)}, f32[4,1,16,512]{3,2,1,0:T(8,128)S(1)}, u32[]{:S(2)}, u32[]{:S(2)}) collective-permute-start(f32[4,1,16,512]{3,2,1,0:T(8,128)S(1)} %get-tuple-element.34), channel_id=1, source_target_pairs={{16,0},{32,16},{48,32},{64,48},{80,64},{96,80},{112,96},{17,1},{33... | collective-permute-start | bytes 393224 | tf_op jit(solution)/shard_map/ppermute | solution.py:23
  179.4 16.3 %collective-permute-start.22 = (f32[66,1,512]{2,1,0:T(1,128)S(1)}, f32[66,1,512]{2,1,0:T(1,128)S(1)}, u32[]{:S(2)}, u32[]{:S(2)}) collective-permute-start(f32[66,1,512]{2,1,0:T(1,128)S(1)} %get-tuple-element.38), channel_id=1, source_target_pairs={{1,0},{2,1},{3,2},{4,3},{5,4},{6,5},{7,6},{8,7},{9,8},{10,9},{11,1... | collective-permute-start | bytes 405512 | tf_op jit(solution)/shard_map/ppermute | solution.py:23
  182.7 13.0 %collective-permute-start.23 = (f32[66,1,512]{2,1,0:T(1,128)S(1)}, f32[66,1,512]{2,1,0:T(1,128)S(1)}, u32[]{:S(2)}, u32[]{:S(2)}) collective-permute-start(f32[66,1,512]{2,1,0:T(1,128)S(1)} %get-tuple-element.37), channel_id=1, source_target_pairs={{0,1},{1,2},{2,3},{3,4},{4,5},{5,6},{6,7},{7,8},{8,9},{9,10},{10,1... | collective-permute-start | bytes 405512 | tf_op jit(solution)/shard_map/ppermute | solution.py:20
  191.2 27.8 %collective-permute-start.2 = (f32[4,66,1,512]{3,2,1,0:T(1,128)}, f32[4,66,1,512]{3,2,1,0:T(1,128)S(1)}, u32[]{:S(2)}, u32[]{:S(2)}) collective-permute-start(f32[4,66,1,512]{3,2,1,0:T(1,128)} %get-tuple-element.29), channel_id=1, source_target_pairs={{0,1},{1,2},{2,3},{3,4},{4,5},{5,6},{6,7},{7,8},{8,9},{9,10},{10,1... | collective-permute-start | bytes 1622024 | tf_op jit(solution)/shard_map/ppermute | solution.py:20
  193.8 25.2 %collective-permute-start.3 = (f32[4,66,1,512]{3,2,1,0:T(1,128)}, f32[4,66,1,512]{3,2,1,0:T(1,128)S(1)}, u32[]{:S(2)}, u32[]{:S(2)}) collective-permute-start(f32[4,66,1,512]{3,2,1,0:T(1,128)} %get-tuple-element.30), channel_id=1, source_target_pairs={{1,0},{2,1},{3,2},{4,3},{5,4},{6,5},{7,6},{8,7},{9,8},{10,9},{11,1... | collective-permute-start | bytes 1622024 | tf_op jit(solution)/shard_map/ppermute | solution.py:23
  211.5 90.5 %copy-start = (f32[64,16,512]{2,1,0:T(8,128)}, f32[64,16,512]{2,1,0:T(8,128)S(1)}, u32[]{:S(2)}) copy-start(f32[64,16,512]{2,1,0:T(8,128)S(1)} %fusion.31) | copy-start | bytes 6291460
  211.5 28.3 %collective-permute-start.24 = (f32[1,16,512]{2,1,0:T(8,128)S(1)}, f32[1,16,512]{2,1,0:T(8,128)S(1)}, u32[]{:S(2)}, u32[]{:S(2)}) collective-permute-start(f32[1,16,512]{2,1,0:T(8,128)S(1)} %get-tuple-element.45), channel_id=1, source_target_pairs={{0,16},{16,32},{32,48},{48,64},{64,80},{80,96},{96,112},{1,17},{17... | collective-permute-start | bytes 98312 | tf_op jit(solution)/shard_map/ppermute | solution.py:20
  213.5 26.4 %collective-permute-start.25 = (f32[1,16,512]{2,1,0:T(8,128)S(1)}, f32[1,16,512]{2,1,0:T(8,128)S(1)}, u32[]{:S(2)}, u32[]{:S(2)}) collective-permute-start(f32[1,16,512]{2,1,0:T(8,128)S(1)} %get-tuple-element.46), channel_id=1, source_target_pairs={{16,0},{32,16},{48,32},{64,48},{80,64},{96,80},{112,96},{17,1},{33... | collective-permute-start | bytes 98312 | tf_op jit(solution)/shard_map/ppermute | solution.py:23
  240.1 19.5 %collective-permute-start.26 = (f32[66,1,512]{2,1,0:T(1,128)S(1)}, f32[66,1,512]{2,1,0:T(1,128)S(1)}, u32[]{:S(2)}, u32[]{:S(2)}) collective-permute-start(f32[66,1,512]{2,1,0:T(1,128)S(1)} %get-tuple-element.36), channel_id=1, source_target_pairs={{1,0},{2,1},{3,2},{4,3},{5,4},{6,5},{7,6},{8,7},{9,8},{10,9},{11,1... | collective-permute-start | bytes 405512 | tf_op jit(solution)/shard_map/ppermute | solution.py:23
  242.6 17.0 %collective-permute-start.27 = (f32[66,1,512]{2,1,0:T(1,128)S(1)}, f32[66,1,512]{2,1,0:T(1,128)S(1)}, u32[]{:S(2)}, u32[]{:S(2)}) collective-permute-start(f32[66,1,512]{2,1,0:T(1,128)S(1)} %get-tuple-element.35), channel_id=1, source_target_pairs={{0,1},{1,2},{2,3},{3,4},{4,5},{5,6},{6,7},{7,8},{8,9},{9,10},{10,1... | collective-permute-start | bytes 405512 | tf_op jit(solution)/shard_map/ppermute | solution.py:20
  (13 other events, 151.2 us)
where the time goes:
time: 331 us; the launch traced here: 326 us
  other arithmetic  185 us (56%)
  starting transfers between devices  101 us (31%)
  local copies, waits for them, and re-layouts  20.8 us (6%)
  waiting for transfers between devices  17.9 us (5%)
    another operation x4, other arithmetic, predict(): return jnp.stack(result)  60.6 us
    concatenate x12, other arithmetic, with_halo(): block = jnp.concatenate([low, block, high], axis=dim)  55.8 us
    ppermute x14, starting transfers between devices, with_halo(): lax.ppermute(lax.slice_in_dim(block, block.shape[dim] - width, None, axis...  50.7 us
    ppermute x14, starting transfers between devices, with_halo(): lax.ppermute(lax.slice_in_dim(block, 0, width, axis=dim), axis, backward)  50.5 us
    add x3, other arithmetic, relax(): return phi + omega * ((total - source) / diag - phi)  34.2 us
    mul x1, other arithmetic, relax(): return phi + omega * ((total - source) / diag - phi)  20 us
    ppermute x14, waiting for transfers between devices, with_halo(): lax.ppermute(lax.slice_in_dim(block, block.shape[dim] - width, None, axis...  11.5 us
    squeeze x1, local copies, waits for them, and re-layouts, predict(): upper = neighbour(vel_pad[comp], dim, 1)  10.7 us
  transfers between devices with their start and end apart: 28, of which 8 were waited for; matrix products, arithmetic and copies ran while one was open for 21% of the time, Pallas kernels for 0%

commit v1 on v0

v1 whole, which is shorter than its diff:
```python
import functools
import math

import jax
import jax.numpy as jnp
from jax import lax
from jax.experimental import pallas as pl
from jax.experimental.pallas import tpu as pltpu
from jax.sharding import PartitionSpec as P

ITERS = 4
time_step = 0.1
force_gain = 0.3

NXL = 64
NYL = 16
NT = 4
PAD = 16
CELLS = NXL * NYL
ROWS = CELLS + 2 * PAD
F32 = jnp.float32
WIDTH = ("width", "thick")
MIB = 1024 * 1024


def sweep_weight(k):
    return 2.0 / (2.15 + 1.75 * math.cos(math.pi * (2 * k + 1) / (2 * ITERS)))


def lanes(shape):
    return lax.broadcasted_iota(jnp.int32, shape, 2)


def sublanes(shape):
    return lax.broadcasted_iota(jnp.int32, shape, 1)


def z_up(a):
    r = pltpu.roll(a, 127, 2)
    after = jnp.concatenate([r[1:], jnp.zeros_like(r[:1])], axis=0)
    return jnp.where(lanes(a.shape) == 127, after, r)


def z_down(a):
    r = pltpu.roll(a, 1, 2)
    before = jnp.concatenate([jnp.zeros_like(r[:1]), r[:-1]], axis=0)
    return jnp.where(lanes(a.shape) == 0, before, r)


def recip(d):
    y = pl.reciprocal(d, approx=True)
    return y * (2.0 - d * y)


def low_rows():
    return pl.ds(PAD, NXL, stride=NYL)


def high_rows():
    return pl.ds(PAD + NYL - 1, NXL, stride=NYL)


LOW_PLANE = pl.ds(PAD, NYL)
HIGH_PLANE = pl.ds(PAD + CELLS - NYL, NYL)


def edge_slices():
    return (low_rows(), high_rows(), LOW_PLANE, HIGH_PLANE)


def zero_pads(ref):
    shape = ref.shape[:-2] + (PAD, 128)
    lead = (slice(None),) * (len(ref.shape) - 2)
    ref[lead + (pl.ds(0, PAD),)] = jnp.zeros(shape, F32)
    ref[lead + (pl.ds(PAD + CELLS, PAD),)] = jnp.zeros(shape, F32)


def row_of(x):
    return pl.multiple_of(PAD + x * NYL, NYL)


CHUNKS = 4


def load_kernel(vel, mag, lab, v, b, sig, e, ylo, yhi, xlo, xhi, labv, sem):
    per = CELLS // CHUNKS
    for ch in range(CHUNKS):
        src = pl.ds(ch * per, per)
        dst = pl.ds(PAD + ch * per, per)
        for t in range(NT):
            col = pl.ds(128 * t, 128)
            for c in range(3):
                pltpu.make_async_copy(vel.at[c, src, col], v.at[c, t, dst], sem.at[ch, 0]).start()
                pltpu.make_async_copy(mag.at[c, src, col], b.at[c, t, dst], sem.at[ch, 1]).start()
            pltpu.make_async_copy(lab.at[src, col], labv.at[t, src], sem.at[ch, 2]).start()
    for ref in (v, sig, e):
        zero_pads(ref)
    for ch in range(CHUNKS):
        src = pl.ds(ch * per, per)
        dst = pl.ds(PAD + ch * per, per)
        pltpu.make_async_copy(v.at[:, :, dst], v.at[:, :, dst], sem.at[ch, 0]).wait()
        pltpu.make_async_copy(b.at[:, :, dst], b.at[:, :, dst], sem.at[ch, 1]).wait()
        pltpu.make_async_copy(labv.at[:, src], labv.at[:, src], sem.at[ch, 2]).wait()

        @pl.loop(0, per // 8, unroll=4)
        def _(i):
            raw = pl.ds(pl.multiple_of(ch * per + i * 8, 8), 8)
            at = pl.ds(pl.multiple_of(PAD + ch * per + i * 8, 8), 8)
            lb = labv[:, raw, :]
            sig[:, at, :] = jnp.where(lb == 0, 1.0, jnp.where(lb == 1, 0.7, 4.0)).astype(F32)
            v0, v1, v2 = (v[c, :, at, :] for c in range(3))
            b0, b1, b2 = (b[c, :, at, :] for c in range(3))
            e[0, :, at, :] = v1 * b2 - v2 * b1
            e[1, :, at, :] = v2 * b0 - v0 * b2
            e[2, :, at, :] = v0 * b1 - v1 * b0

    for out, rows, d in zip((ylo, yhi, xlo, xhi), edge_slices(), (1, 1, 0, 0)):
        out[0] = sig[:, rows, :]
        out[1] = e[d, :, rows, :]


def face_kernel(w0, sig, e, v, visc, f, src, inv, phi, nu, vylo, vyhi, vxlo, vxhi, sem):
    copies = [
        pltpu.make_async_copy(visc.at[:, pl.ds(128 * t, 128)], nu.at[t, pl.ds(PAD, CELLS)], sem.at[t])
        for t in range(NT)
    ]
    for copy in copies:
        copy.start()
    for ref in (f, phi, nu):
        zero_pads(ref)
    shape = (NT, 8, 128)
    zero = jnp.zeros(shape, F32)
    sub = sublanes(shape)

    def face(a, n):
        return (2.0 * a) * n * recip(a + n)

    def body(x, carry):
        fxm, qxm, sc, exc = carry
        r = row_of(x)
        fx, qx, sp, exp = [], [], [], []
        fy, qy, fz, qz = [], [], [], []
        for y in range(2):
            at = pl.ds(r + 8 * y, 8)
            up = pl.ds(r + 8 * y + 1, 8)
            ahead = pl.ds(r + NYL + 8 * y, 8)
            sp.append(sig[:, ahead, :])
            exp.append(e[0, :, ahead, :])
            fx.append(face(sc[y], sp[y]))
            qx.append(fx[y] * (exc[y] + exp[y]))
            g = face(sc[y], sig[:, up, :])
            if y == 1:
                g = jnp.where(sub == 7, 0.0, g)
            fy.append(g)
            qy.append(g * (e[1, :, at, :] + e[1, :, up, :]))
            g = face(sc[y], z_up(sc[y]))
            ez = e[2, :, at, :]
            fz.append(g)
            qz.append(g * (ez + z_up(ez)))
        rf = [pltpu.roll(a, 1, 1) for a in fy]
        rq = [pltpu.roll(a, 1, 1) for a in qy]
        for y in range(2):
            at = pl.ds(r + 8 * y, 8)
            fym = jnp.where(sub == 0, rf[1 - y], rf[y])
            qym = jnp.where(sub == 0, rq[1 - y], rq[y])
            source = 0.5 * (((qx[y] - qxm[y]) + (qy[y] - qym)) + (qz[y] - z_down(qz[y])))
            diag = ((fx[y] + fxm[y]) + (fy[y] + fym)) + (fz[y] + z_down(fz[y])) + 0.05 * sc[y]
            inverse = recip(diag)
            f[0, :, at, :] = fx[y]
            f[1, :, at, :] = fy[y]
            f[2, :, at, :] = fz[y]
            src[:, at, :] = source
            inv[:, at, :] = inverse
            phi[:, at, :] = (-w0) * (source * inverse)
        return (tuple(fx), tuple(qx), tuple(sp), tuple(exp))

    first = [pl.ds(PAD + 8 * y, 8) for y in range(2)]
    start = (
        (zero, zero),
        (zero, zero),
        tuple(sig[:, at, :] for at in first),
        tuple(e[0, :, at, :] for at in first),
    )
    lax.fori_loop(0, NXL, body, start, unroll=2)
    for copy in copies:
        copy.wait()
    for out, rows in zip((vylo, vyhi, vxlo, vxhi), edge_slices()):
        for c in range(3):
            out[c] = v[c, :, rows, :]
        out[3] = nu[:, rows, :]


def first_edge_kernel(w0, hyl, hyh, hxl, hxh, sig, e, src_in, inv_in, phi_in,
                      src, inv, phi, cyl, cyh, cxl, cxh, oyl, oyh, oxl, oxh):
    del src_in, inv_in, phi_in
    place = lax.axis_index("width") * 2 + lax.axis_index("thick")
    cast = lax.axis_index("cast")
    inside = (place > 0, place < lax.axis_size(WIDTH) - 1, cast > 0, cast < lax.axis_size("cast") - 1)
    sides = tuple(zip((hyl, hyh, hxl, hxh), (cyl, cyh, cxl, cxh), (oyl, oyh, oxl, oxh), edge_slices(),
                      (1, 1, 0, 0), (-0.5, 0.5, -0.5, 0.5), inside))
    for halo, coef, _, rows, d, sign, ok in sides:
        s = sig[:, rows, :]
        n = halo[0] * jnp.where(ok, 1.0, 0.0).astype(F32)
        g = (2.0 * s) * n * recip(s + n)
        coef[...] = g
        src[:, rows, :] = src[:, rows, :] + sign * (g * (e[d, :, rows, :] + halo[1]))
        inv[:, rows, :] = recip(recip(inv[:, rows, :]) + g)
    for _, coef, _, rows, _, _, _ in sides:
        i = inv[:, rows, :]
        coef[...] = coef[...] * i
        phi[:, rows, :] = (-w0) * (src[:, rows, :] * i)
    for _, _, out, rows, _, _, _ in sides:
        out[...] = phi[:, rows, :]


def predictor(v, nu, vnew, x0, x1):
    shape = (NT, 8, 128)
    sub = sublanes(shape)

    @pl.loop(x0, x1)
    def _(x):
        r = row_of(x)
        for y in range(2):
            base = r + 8 * y
            at = pl.ds(base, 8)
            ups = (pl.ds(base + NYL, 8), pl.ds(base + 1, 8))
            downs = (pl.ds(base - NYL, 8), pl.ds(base - 1, 8))
            n = nu[:, at, :]
            vc = [v[c, :, at, :] for c in range(3)]
            coefs = []
            total = None
            for d in range(3):
                above = nu[:, ups[d], :] if d < 2 else z_up(n)
                below = nu[:, downs[d], :] if d < 2 else z_down(n)
                up = (0.5 * time_step) * ((n + above) - vc[d])
                down = (0.5 * time_step) * ((n + below) + vc[d])
                if d == 1 and y == 1:
                    up = jnp.where(sub == 7, 0.0, up)
                if d == 1 and y == 0:
                    down = jnp.where(sub == 0, 0.0, down)
                coefs.append((up, down))
                both = up + down
                total = both if total is None else total + both
            keep = 1.0 - total
            for c in range(3):
                acc = keep * vc[c]
                for d in range(3):
                    above = v[c, :, ups[d], :] if d < 2 else z_up(vc[c])
                    below = v[c, :, downs[d], :] if d < 2 else z_down(vc[c])
                    acc = acc + coefs[d][0] * above + coefs[d][1] * below
                vnew[c, :, at, :] = acc


def sweep_kernel(w, x0, x1, phi, f, src, inv, v, nu, *rest):
    out, vnew = rest[-2:]
    zero_pads(out)
    shape = (NT, 8, 128)
    zero = jnp.zeros(shape, F32)

    def body(x, carry):
        pxm, pc = carry
        r = row_of(x)
        px, pn = [], []
        for y in range(2):
            base = r + 8 * y
            at = pl.ds(base, 8)
            pn.append(phi[:, pl.ds(base + NYL, 8), :])
            fx = f[0, :, at, :]
            c = pc[y]
            px.append(fx * c)
            t = fx * pn[y] + pxm[y]
            t = t + f[1, :, at, :] * phi[:, pl.ds(base + 1, 8), :]
            t = t + f[1, :, pl.ds(base - 1, 8), :] * phi[:, pl.ds(base - 1, 8), :]
            fz = f[2, :, at, :]
            t = t + fz * z_up(c)
            t = t + z_down(fz * c)
            out[:, at, :] = c + w * ((t - src[:, at, :]) * inv[:, at, :] - c)
        return tuple(px), tuple(pn)

    start = ((zero, zero), tuple(phi[:, pl.ds(PAD + 8 * y, 8), :] for y in range(2)))
    lax.fori_loop(0, NXL, body, start, unroll=4)
    predictor(v, nu, vnew, x0, x1)


def edge_kernel(w, phi_in, cyl, cyh, cxl, cxh, hyl, hyh, hxl, hxh, phi, oyl, oyh, oxl, oxh):
    del phi_in
    for coef, halo, rows in zip((cyl, cyh, cxl, cxh), (hyl, hyh, hxl, hxh), edge_slices()):
        phi[:, rows, :] = phi[:, rows, :] + w * (coef[...] * halo[...])
    for out, rows in zip((oyl, oyh, oxl, oxh), edge_slices()):
        out[...] = phi[:, rows, :]


def force_kernel(phi, sig, e, b, vnew_in, potential, vnew, sem):
    del vnew_in
    copies = [
        pltpu.make_async_copy(phi.at[t, pl.ds(PAD, CELLS)], potential.at[:, pl.ds(128 * t, 128)], sem.at[t])
        for t in range(NT)
    ]
    for copy in copies:
        copy.start()
    shape = (NT, 8, 128)
    sub = sublanes(shape)

    @pl.loop(0, NXL, unroll=2)
    def _(x):
        r = row_of(x)
        for y in range(2):
            base = r + 8 * y
            at = pl.ds(base, 8)
            p = phi[:, at, :]
            yu = phi[:, pl.ds(base + 1, 8), :]
            yd = phi[:, pl.ds(base - 1, 8), :]
            if y == 1:
                yu = jnp.where(sub == 7, 0.0, yu)
            else:
                yd = jnp.where(sub == 0, 0.0, yd)
            diffs = (
                phi[:, pl.ds(base + NYL, 8), :] - phi[:, pl.ds(base - NYL, 8), :],
                yu - yd,
                z_up(p) - z_down(p),
            )
            s = force_gain * sig[:, at, :]
            cur = [s * (e[d, :, at, :] - 0.5 * diffs[d]) for d in range(3)]
            bb = [b[d, :, at, :] for d in range(3)]
            vnew[0, :, at, :] = vnew[0, :, at, :] + (cur[1] * bb[2] - cur[2] * bb[1])
            vnew[1, :, at, :] = vnew[1, :, at, :] + (cur[2] * bb[0] - cur[0] * bb[2])
            vnew[2, :, at, :] = vnew[2, :, at, :] + (cur[0] * bb[1] - cur[1] * bb[0])

    for copy in copies:
        copy.wait()


def last_kernel(sig, b, v, nu, hyl, hyh, hxl, hxh, gyl, gyh, gxl, gxh, vnew_in, result, vnew, sem):
    del vnew_in
    place = lax.axis_index("width") * 2 + lax.axis_index("thick")
    cast = lax.axis_index("cast")
    inside = (place > 0, place < lax.axis_size(WIDTH) - 1, cast > 0, cast < lax.axis_size("cast") - 1)
    sides = zip((hyl, hyh, hxl, hxh), (gyl, gyh, gxl, gxh), edge_slices(), (1, 1, 0, 0), (1.0, -1.0, 1.0, -1.0), inside)
    for halo, flow, rows, d, sign, ok in sides:
        mask = jnp.where(ok, 1.0, 0.0).astype(F32)
        cur = (0.5 * force_gain * sign) * (mask * (sig[:, rows, :] * halo[...]))
        n1, n2 = (d + 1) % 3, (d + 2) % 3
        add = {n1: -cur * b[n2, :, rows, :], n2: cur * b[n1, :, rows, :]}
        hn = mask * flow[3]
        along = v[d, :, rows, :]
        coef = (0.5 * time_step) * ((nu[:, rows, :] + hn) + sign * along)
        gone = (0.5 * time_step) * hn if d == 0 else coef
        for c in range(3):
            new = vnew[c, :, rows, :] + (coef * (mask * flow[c]) - gone * v[c, :, rows, :])
            if c in add:
                new = new + add[c]
            vnew[c, :, rows, :] = new
    copies = [
        pltpu.make_async_copy(vnew.at[c, t, pl.ds(PAD, CELLS)], result.at[c, :, pl.ds(128 * t, 128)], sem.at[c, t])
        for c in range(3)
        for t in range(NT)
    ]
    for copy in copies:
        copy.start()
    for copy in copies:
        copy.wait()


def resident(*shape):
    return pltpu.VMEM(shape, F32)


def in_vmem(x):
    return pltpu.with_memory_space_constraint(x, pltpu.VMEM)


def in_hbm(x):
    return pltpu.with_memory_space_constraint(x, pltpu.HBM)


IN_VMEM = pl.BlockSpec(memory_space=pltpu.VMEM)
IN_HBM = pl.BlockSpec(memory_space=pl.ANY)

FIELD = (NT, ROWS, 128)
YP = (NT, NXL, 128)
XP = (NT, NYL, 128)


def run(kernel, name, ins, outs, aliases=None, scratch=(), flops=0, moved=0, limit=8 * MIB):
    args = [in_hbm(a) if hbm else in_vmem(a) for a, hbm in ins]
    return pl.pallas_call(
        kernel,
        out_shape=outs,
        in_specs=[IN_HBM if hbm else IN_VMEM for _, hbm in ins],
        out_specs=[IN_HBM if isinstance(o, jax.ShapeDtypeStruct) else IN_VMEM for o in outs],
        input_output_aliases=aliases or {},
        scratch_shapes=list(scratch),
        compiler_params=pltpu.CompilerParams(vmem_limit_bytes=limit),
        cost_estimate=pl.CostEstimate(flops=flops, bytes_accessed=moved, transcendentals=0),
        name=name,
    )(*args)


def vm(*arrays):
    return [(a, False) for a in arrays]


def ring(axis, step):
    n = lax.axis_size(axis)
    return [(i, (i + step) % n) for i in range(n)]


def exchange(ylo, yhi, xlo, xhi):
    hyl = lax.ppermute(yhi, WIDTH, ring(WIDTH, 1))
    hyh = lax.ppermute(ylo, WIDTH, ring(WIDTH, -1))
    hxl = lax.ppermute(xhi, "cast", ring("cast", 1))
    hxh = lax.ppermute(xlo, "cast", ring("cast", -1))
    return hyl, hyh, hxl, hxh


def local(velocity, magnetic, labels, viscosity):
    vel = velocity.reshape(3, CELLS, NT * 128)
    mag = magnetic.reshape(3, CELLS, NT * 128)
    lab = labels.reshape(CELLS, NT * 128)
    visc = viscosity.reshape(CELLS, NT * 128)
    dma = pltpu.SemaphoreType.DMA
    w = [sweep_weight(k) for k in range(ITERS)]

    pair = [resident(2, *YP)] * 2 + [resident(2, *XP)] * 2
    quad = [resident(4, *YP)] * 2 + [resident(4, *XP)] * 2
    plain = [resident(*YP)] * 2 + [resident(*XP)] * 2

    v, b, sig, e, *edges = run(
        load_kernel, "load", [(vel, True), (mag, True), (lab, True)],
        [resident(3, *FIELD), resident(3, *FIELD), resident(*FIELD), resident(3, *FIELD)] + pair,
        scratch=[pltpu.VMEM((NT, CELLS, 128), jnp.int32), dma((CHUNKS, 3))],
    )
    halos = exchange(*edges)
    f, src, inv, phi, nu, *flow = run(
        functools.partial(face_kernel, w[0]), "faces", vm(sig, e, v) + [(visc, True)],
        [resident(3, *FIELD), resident(*FIELD), resident(*FIELD), resident(*FIELD), resident(*FIELD)] + quad,
        scratch=[dma((NT,))], flops=10_000_000, moved=20 * MIB,
    )
    src, inv, phi, *rest = run(
        functools.partial(first_edge_kernel, w[0]), "edges1", vm(*halos, sig, e, src, inv, phi),
        [resident(*FIELD)] * 3 + plain + plain,
        aliases={6: 0, 7: 1, 8: 2},
    )
    coefs, edges = rest[:4], rest[4:]
    flow_halos = exchange(*flow)
    vnew = None
    cuts = (0, 22, 43, 64)
    for k in range(1, ITERS):
        halos = exchange(*edges)
        ins = vm(phi, f, src, inv, v, nu)
        aliases = {}
        if vnew is not None:
            ins = ins + vm(vnew)
            aliases = {6: 1}
        phi, vnew = run(
            functools.partial(sweep_kernel, w[k], cuts[k - 1], cuts[k]), f"sweep{k}", ins,
            [resident(*FIELD), resident(3, *FIELD)], aliases=aliases, flops=10_000_000, moved=16 * MIB,
        )
        phi, *edges = run(
            functools.partial(edge_kernel, w[k]), f"edges{k + 1}", vm(phi, *coefs, *halos),
            [resident(*FIELD)] + plain, aliases={0: 0},
        )
    halos = exchange(*edges)
    potential, vnew = run(
        force_kernel, "force", vm(phi, sig, e, b, vnew),
        [jax.ShapeDtypeStruct((CELLS, NT * 128), F32), resident(3, *FIELD)],
        aliases={4: 1}, scratch=[dma((NT,))], flops=10_000_000, moved=16 * MIB,
    )
    result, _ = run(
        last_kernel, "last", vm(sig, b, v, nu, *halos, *flow_halos, vnew),
        [jax.ShapeDtypeStruct((3, CELLS, NT * 128), F32), resident(3, *FIELD)],
        aliases={12: 1}, scratch=[dma((3, NT))],
    )
    return result.reshape(velocity.shape), potential.reshape(labels.shape)


def solution(mesh):
    fields = P(None, "cast", WIDTH, None)
    scalar = P("cast", WIDTH, None)
    return jax.shard_map(
        local,
        mesh=mesh,
        in_specs=(fields, fields, scalar, scalar),
        out_specs=(fields, scalar),
        check_vma=False,
    )
```

time: 331 us -> 110 us (0.33)
  the two profiles are of different devices: /device:TPU:15 before, /device:TPU:2 now
where the time goes in v1:
time: 110 us; the launch traced here: 109 us
  starting transfers between devices  47.4 us (43%)
  Pallas kernels  40.7 us (37%)
  waiting for transfers between devices  16.8 us (15%)
  local copies, waits for them, and re-layouts  2.75 us (2%)
  between operations  1.1 us (1%)
    pallas_call x11, Pallas kernels, run(): pl.pallas_call(kernel, out_shape=outs, in_specs=[IN_HBM if hbm else IN_VM...  40.7 us
    ppermute x6, starting transfers between devices, exchange(): hyh = lax.ppermute(ylo, WIDTH, ring(WIDTH, -1))  29 us
    ppermute x6, waiting for transfers between devices, exchange(): hxl = lax.ppermute(xhi, 'cast', ring('cast', 1))  15.9 us
    ppermute x6, starting transfers between devices, exchange(): hxh = lax.ppermute(xlo, 'cast', ring('cast', -1))  11.6 us
    ppermute x6, starting transfers between devices, exchange(): hxl = lax.ppermute(xhi, 'cast', ring('cast', 1))  6.55 us
    unnamed x14, local copies, waits for them, and re-layouts  2.75 us
  transfers between devices with their start and end apart: 24, of which 4 were waited for; matrix products, arithmetic and copies ran while one was open for 0% of the time, Pallas kernels for 26%

profile of v1, /device:TPU:2, one launch (start us, length us, event | category | flops | bytes accessed | tf_op | source)
XLA Modules:
  0.0 108.7 jit_solution(1737264551619867445)
XLA Ops:
  0.6 6.2 %load.1 = (f32[3,4,1056,128]{3,2,1,0:T(8,128)S(1)}, f32[3,4,1056,128]{3,2,1,0:T(8,128)S(1)}, f32[4,1056,128]{2,1,0:T(8,128)S(1)}, f32[3,4,1056,128]{3,2,1,0:T(8,...) custom-call(f32[3,1024,512]{2,1,0:T(8,128)} %bitcast.8, ...), custom_call_target="tpu_custom_call" | custom-call | tf_op jit(solution)/shard_map/load/pallas_call | solution.py:386
  6.8 2.7 %copy-done.4 = f32[3,4,1056,128]{3,2,1,0:T(8,128)} copy-done((f32[3,4,1056,128]{3,2,1,0:T(8,128)}, f32[3,4,1056,128]{3,2,1,0:T(8,128)S(1)}, u32[]{:S(2)}) %copy-start.4) | copy-done | bytes 6488088
  9.5 5.4 %collective-permute-start.1 = (f32[2,4,64,128]{3,2,1,0:T(8,128)S(1)}, f32[2,4,64,128]{3,2,1,0:T(8,128)S(1)}, u32[]{:S(2)}, u32[]{:S(2)}) collective-permute-start(f32[2,4,64,128]{3,2,1,0:T(8,128)S(1)} %get-tuple-element.60), channel_id=1, source_target_pairs={{0,15},{1,0},{2,1},{3,2},{4,3},{5,4},{6,5},{7,6},{8,7},{9,8},{10,9... | collective-permute-start | bytes 786440 | tf_op jit(solution)/shard_map/ppermute | solution.py:410
  14.9 1.9 %collective-permute-start.2 = (f32[2,4,16,128]{3,2,1,0:T(8,128)S(1)}, f32[2,4,16,128]{3,2,1,0:T(8,128)S(1)}, u32[]{:S(2)}, u32[]{:S(2)}) collective-permute-start(f32[2,4,16,128]{3,2,1,0:T(8,128)S(1)} %get-tuple-element.61), channel_id=1, source_target_pairs={{0,16},{16,32},{32,48},{48,64},{64,80},{80,96},{96,112},{112,0},{1... | collective-permute-start | bytes 196616 | tf_op jit(solution)/shard_map/ppermute | solution.py:411
  16.8 2.2 %collective-permute-start.3 = (f32[2,4,16,128]{3,2,1,0:T(8,128)S(1)}, f32[2,4,16,128]{3,2,1,0:T(8,128)S(1)}, u32[]{:S(2)}, u32[]{:S(2)}) collective-permute-start(f32[2,4,16,128]{3,2,1,0:T(8,128)S(1)} %get-tuple-element.62), channel_id=1, source_target_pairs={{0,112},{16,0},{32,16},{48,32},{64,48},{80,64},{96,80},{112,96},{1... | collective-permute-start | bytes 196616 | tf_op jit(solution)/shard_map/ppermute | solution.py:412
  19.0 6.8 %faces.1 = (f32[3,4,1056,128]{3,2,1,0:T(8,128)S(1)}, f32[4,1056,128]{2,1,0:T(8,128)S(1)}, f32[4,1056,128]{2,1,0:T(8,128)S(1)}, f32[4,1056,128]{2,1,0:T(8,128)S(1...) custom-call(f32[4,1056,128]{2,1,0:T(8,128)S(1)} %get-tuple-element.5, ...), custom_call_target="tpu_custom_call" | custom-call | flops 10000000 | bytes 20971520 | tf_op jit(solution)/shard_map/faces/pallas_call | solution.py:386
  25.9 1.5 %edges1.1 = (f32[4,1056,128]{2,1,0:T(8,128)S(1)}, f32[4,1056,128]{2,1,0:T(8,128)S(1)}, f32[4,1056,128]{2,1,0:T(8,128)S(1)}, f32[4,64,128]{2,1,0:T(8,128)S(1)}, f...) custom-call(f32[2,4,64,128]{3,2,1,0:T(8,128)S(1)} %collective-permut, ...), custom_call_target="tpu_custom_call", output_to_operand_aliasing={{0}: (6, {}), {1}: (7, {}), {2}: (8, {})} | custom-call | tf_op jit(solution)/shard_map/edges1/pallas_call | solution.py:386
  27.5 0.1 collective-permute-start.4
  27.6 5.3 %collective-permute-start.5 = (f32[4,64,128]{2,1,0:T(8,128)S(1)}, f32[4,64,128]{2,1,0:T(8,128)S(1)}, u32[]{:S(2)}, u32[]{:S(2)}) collective-permute-start(f32[4,64,128]{2,1,0:T(8,128)S(1)} %get-tuple-element.76), channel_id=1, source_target_pairs={{0,15},{1,0},{2,1},{3,2},{4,3},{5,4},{6,5},{7,6},{8,7},{9,8},{10,9... | collective-permute-start | bytes 393224 | tf_op jit(solution)/shard_map/ppermute | solution.py:410
  32.9 5.4 %collective-permute-start.21 = (f32[4,4,64,128]{3,2,1,0:T(8,128)S(1)}, f32[4,4,64,128]{3,2,1,0:T(8,128)S(1)}, u32[]{:S(2)}, u32[]{:S(2)}) collective-permute-start(f32[4,4,64,128]{3,2,1,0:T(8,128)S(1)} %get-tuple-element.98), channel_id=1, source_target_pairs={{0,15},{1,0},{2,1},{3,2},{4,3},{5,4},{6,5},{7,6},{8,7},{9,8},{10,9... | collective-permute-start | bytes 1572872 | tf_op jit(solution)/shard_map/ppermute | solution.py:410
  38.3 9.6 %collective-permute-done.6.hxl = f32[4,16,128]{2,1,0:T(8,128)S(1)} collective-permute-done((f32[4,16,128]{2,1,0:T(8,128)S(1)}, f32[4,16,128]{2,1,0:T(8,128)S(1)}, u32[]{:S(2)}, u32[]{:S(2)}) %collective-permute-start.6) | collective-permute-done | bytes 32800 | tf_op jit(solution)/shard_map/ppermute | solution.py:411
  47.9 5.7 %sweep1.1 = (f32[4,1056,128]{2,1,0:T(8,128)S(1)}, f32[3,4,1056,128]{3,2,1,0:T(8,128)S(1)}) custom-call(f32[4,1056,128]{2,1,0:T(8,128)S(1)} %get-tuple-element.66.phi, f32[3,4,1056,128]{3,2,1,0:T(8,128)S(1)} %get-tuple-element.67.f, f32[4,1056,128]{2,1,0:T(8,128)S(1)} %get-tuple-element.68.src, f32[4,1056,128]{2,1,0:T(8,128)S(1)} %get-tuple-element.69.inv, ...), custom_call_target="tpu_custom_call" | custom-call | flops 10000000 | bytes 16777216 | tf_op jit(solution)/shard_map/sweep1/pallas_call | solution.py:386
  53.6 0.4 edges2.1
  54.1 5.3 %collective-permute-start.9 = (f32[4,64,128]{2,1,0:T(8,128)S(1)}, f32[4,64,128]{2,1,0:T(8,128)S(1)}, u32[]{:S(2)}, u32[]{:S(2)}) collective-permute-start(f32[4,64,128]{2,1,0:T(8,128)S(1)} %get-tuple-element.83), channel_id=1, source_target_pairs={{0,15},{1,0},{2,1},{3,2},{4,3},{5,4},{6,5},{7,6},{8,7},{9,8},{10,9... | collective-permute-start | bytes 393224 | tf_op jit(solution)/shard_map/ppermute | solution.py:410
  59.5 2.0 %collective-permute-start.10 = (f32[4,16,128]{2,1,0:T(8,128)S(1)}, f32[4,16,128]{2,1,0:T(8,128)S(1)}, u32[]{:S(2)}, u32[]{:S(2)}) collective-permute-start(f32[4,16,128]{2,1,0:T(8,128)S(1)} %get-tuple-element.84), channel_id=1, source_target_pairs={{0,16},{16,32},{32,48},{48,64},{64,80},{80,96},{96,112},{112,0},{1... | collective-permute-start | bytes 98312 | tf_op jit(solution)/shard_map/ppermute | solution.py:411
  61.5 4.0 %collective-permute-done.10.hxl = f32[4,16,128]{2,1,0:T(8,128)S(1)} collective-permute-done((f32[4,16,128]{2,1,0:T(8,128)S(1)}, f32[4,16,128]{2,1,0:T(8,128)S(1)}, u32[]{:S(2)}, u32[]{:S(2)}) %collective-permute-start.10) | collective-permute-done | bytes 32800 | tf_op jit(solution)/shard_map/ppermute | solution.py:411
  65.5 5.5 %sweep2.1 = (f32[4,1056,128]{2,1,0:T(8,128)S(1)}, f32[3,4,1056,128]{3,2,1,0:T(8,128)S(1)}) custom-call(f32[4,1056,128]{2,1,0:T(8,128)S(1)} %get-tuple-element.79.phi, f32[3,4,1056,128]{3,2,1,0:T(8,128)S(1)} %get-tuple-element.67.f, f32[4,1056,128]{2,1,0:T(8,128)S(1)} %get-tuple-element.68.src, ...), custom_call_target="tpu_custom_call", output_to_operand_aliasing={{1}: (6, {})} | custom-call | flops 10000000 | bytes 16777216 | tf_op jit(solution)/shard_map/sweep2/pallas_call | solution.py:386
  71.0 0.4 edges3.1
  71.5 2.1 %collective-permute-start.14 = (f32[4,16,128]{2,1,0:T(8,128)S(1)}, f32[4,16,128]{2,1,0:T(8,128)S(1)}, u32[]{:S(2)}, u32[]{:S(2)}) collective-permute-start(f32[4,16,128]{2,1,0:T(8,128)S(1)} %get-tuple-element.91), channel_id=1, source_target_pairs={{0,16},{16,32},{32,48},{48,64},{64,80},{80,96},{96,112},{112,0},{1... | collective-permute-start | bytes 98312 | tf_op jit(solution)/shard_map/ppermute | solution.py:411
  73.6 2.1 %collective-permute-start.15 = (f32[4,16,128]{2,1,0:T(8,128)S(1)}, f32[4,16,128]{2,1,0:T(8,128)S(1)}, u32[]{:S(2)}, u32[]{:S(2)}) collective-permute-start(f32[4,16,128]{2,1,0:T(8,128)S(1)} %get-tuple-element.92), channel_id=1, source_target_pairs={{0,112},{16,0},{32,16},{48,32},{64,48},{80,64},{96,80},{112,96},{1... | collective-permute-start | bytes 98312 | tf_op jit(solution)/shard_map/ppermute | solution.py:412
  75.7 2.2 %collective-permute-done.14.hxl = f32[4,16,128]{2,1,0:T(8,128)S(1)} collective-permute-done((f32[4,16,128]{2,1,0:T(8,128)S(1)}, f32[4,16,128]{2,1,0:T(8,128)S(1)}, u32[]{:S(2)}, u32[]{:S(2)}) %collective-permute-start.14) | collective-permute-done | bytes 32800 | tf_op jit(solution)/shard_map/ppermute | solution.py:411
  77.9 2.3 %collective-permute-start.13 = (f32[4,64,128]{2,1,0:T(8,128)S(1)}, f32[4,64,128]{2,1,0:T(8,128)S(1)}, u32[]{:S(2)}, u32[]{:S(2)}) collective-permute-start(f32[4,64,128]{2,1,0:T(8,128)S(1)} %get-tuple-element.90), channel_id=1, source_target_pairs={{0,15},{1,0},{2,1},{3,2},{4,3},{5,4},{6,5},{7,6},{8,7},{9,8},{10,9... | collective-permute-start | bytes 393224 | tf_op jit(solution)/shard_map/ppermute | solution.py:410
  80.2 0.5 collective-permute-start.22
  80.7 0.9 collective-permute-done.12.hyl
  81.6 3.1 %collective-permute-start.23 = (f32[4,4,16,128]{3,2,1,0:T(8,128)S(1)}, f32[4,4,16,128]{3,2,1,0:T(8,128)S(1)}, u32[]{:S(2)}, u32[]{:S(2)}) collective-permute-start(f32[4,4,16,128]{3,2,1,0:T(8,128)S(1)} %get-tuple-element.100), channel_id=1, source_target_pairs={{0,112},{16,0},{32,16},{48,32},{64,48},{80,64},{96,80},{112,96},{1... | collective-permute-start | bytes 393224 | tf_op jit(solution)/shard_map/ppermute | solution.py:412
  84.7 5.5 %sweep3.1 = (f32[4,1056,128]{2,1,0:T(8,128)S(1)}, f32[3,4,1056,128]{3,2,1,0:T(8,128)S(1)}) custom-call(f32[4,1056,128]{2,1,0:T(8,128)S(1)} %get-tuple-element.86.phi, f32[3,4,1056,128]{3,2,1,0:T(8,128)S(1)} %get-tuple-element.67.f, f32[4,1056,128]{2,1,0:T(8,128)S(1)} %get-tuple-element.68.src, ...), custom_call_target="tpu_custom_call", output_to_operand_aliasing={{1}: (6, {})} | custom-call | flops 10000000 | bytes 16777216 | tf_op jit(solution)/shard_map/sweep3/pallas_call | solution.py:386
  90.2 0.4 edges4.1
  90.7 0.1 collective-permute-start.16
  90.8 5.3 %collective-permute-start.17 = (f32[4,64,128]{2,1,0:T(8,128)S(1)}, f32[4,64,128]{2,1,0:T(8,128)S(1)}, u32[]{:S(2)}, u32[]{:S(2)}) collective-permute-start(f32[4,64,128]{2,1,0:T(8,128)S(1)} %get-tuple-element.94), channel_id=1, source_target_pairs={{0,15},{1,0},{2,1},{3,2},{4,3},{5,4},{6,5},{7,6},{8,7},{9,8},{10,9... | collective-permute-start | bytes 393224 | tf_op jit(solution)/shard_map/ppermute | solution.py:410
  96.1 4.1 %collective-permute-start.19 = (f32[4,16,128]{2,1,0:T(8,128)S(1)}, f32[4,16,128]{2,1,0:T(8,128)S(1)}, u32[]{:S(2)}, u32[]{:S(2)}) collective-permute-start(f32[4,16,128]{2,1,0:T(8,128)S(1)} %get-tuple-element.96), channel_id=1, source_target_pairs={{0,112},{16,0},{32,16},{48,32},{64,48},{80,64},{96,80},{112,96},{1... | collective-permute-start | bytes 98312 | tf_op jit(solution)/shard_map/ppermute | solution.py:412
  100.3 3.6 %force.1 = (f32[1024,512]{1,0:T(8,128)}, f32[3,4,1056,128]{3,2,1,0:T(8,128)S(1)}) custom-call(f32[4,1056,128]{2,1,0:T(8,128)S(1)} %get-tuple-element.101.phi, f32[4,1056,128]{2,1,0:T(8,128)S(1)} %copy-done.1, f32[3,4,1056,128]{3,2,1,0:T(8,128)S(1)} %get-tuple-element.57.e, f32[3,4,1056,128]{3,2,1,0:T(8,128)S(1)} %bitcast.7, ...), custom_call_target="tpu_custom_call", output_to_operand_aliasing={{1}: (4, {})} | custom-call | flops 10000000 | bytes 16777216 | tf_op jit(solution)/shard_map/force/pallas_call | solution.py:386
  103.9 4.6 %last.1 = (f32[3,1024,512]{2,1,0:T(8,128)}, f32[3,4,1056,128]{3,2,1,0:T(8,128)S(1)}) custom-call(f32[4,1056,128]{2,1,0:T(8,128)S(1)} %copy-done.1, f32[3,4,1056,128]{3,2,1,0:T(8,128)S(1)} %bitcast.7, f32[3,4,1056,128]{3,2,1,0:T(8,128)S(1)} %get-tuple-element.56.v, f32[4,1056,128]{2,1,0:T(8,128)S(1)} %copy-done.3, ...), custom_call_target="tpu_custom_call", output_to_operand_aliasing={{1}: (12, {})} | custom-call | tf_op jit(solution)/shard_map/last/pallas_call | solution.py:386
  (42 shorter events, 0.2 us)
Async XLA Ops:
  6.8 2.7 %copy-start.4 = (f32[3,4,1056,128]{3,2,1,0:T(8,128)}, f32[3,4,1056,128]{3,2,1,0:T(8,128)S(1)}, u32[]{:S(2)}) copy-start(f32[3,4,1056,128]{3,2,1,0:T(8,128)S(1)} %get-tuple-element.55.b) | copy-start | bytes 19464196
  9.5 16.4 %copy-start = (f32[4,1056,128]{2,1,0:T(8,128)}, f32[4,1056,128]{2,1,0:T(8,128)S(1)}, u32[]{:S(2)}) copy-start(f32[4,1056,128]{2,1,0:T(8,128)S(1)} %get-tuple-element.54.sig) | copy-start | bytes 6488068
  9.5 16.4 %collective-permute-start = (f32[2,4,64,128]{3,2,1,0:T(8,128)S(1)}, f32[2,4,64,128]{3,2,1,0:T(8,128)S(1)}, u32[]{:S(2)}, u32[]{:S(2)}) collective-permute-start(f32[2,4,64,128]{3,2,1,0:T(8,128)S(1)} %get-tuple-element.59), channel_id=1, source_target_pairs={{0,1},{1,2},{2,3},{3,4},{4,5},{5,6},{6,7},{7,8},{8,9},{9,10},{10,1... | collective-permute-start | bytes 786440 | tf_op jit(solution)/shard_map/ppermute | solution.py:409
  9.5 16.4 %collective-permute-start.1 = (f32[2,4,64,128]{3,2,1,0:T(8,128)S(1)}, f32[2,4,64,128]{3,2,1,0:T(8,128)S(1)}, u32[]{:S(2)}, u32[]{:S(2)}) collective-permute-start(f32[2,4,64,128]{3,2,1,0:T(8,128)S(1)} %get-tuple-element.60), channel_id=1, source_target_pairs={{0,15},{1,0},{2,1},{3,2},{4,3},{5,4},{6,5},{7,6},{8,7},{9,8},{10,9... | collective-permute-start | bytes 786440 | tf_op jit(solution)/shard_map/ppermute | solution.py:410
  14.9 11.0 %collective-permute-start.2 = (f32[2,4,16,128]{3,2,1,0:T(8,128)S(1)}, f32[2,4,16,128]{3,2,1,0:T(8,128)S(1)}, u32[]{:S(2)}, u32[]{:S(2)}) collective-permute-start(f32[2,4,16,128]{3,2,1,0:T(8,128)S(1)} %get-tuple-element.61), channel_id=1, source_target_pairs={{0,16},{16,32},{32,48},{48,64},{64,80},{80,96},{96,112},{112,0},{1... | collective-permute-start | bytes 196616 | tf_op jit(solution)/shard_map/ppermute | solution.py:411
  16.8 9.1 %collective-permute-start.3 = (f32[2,4,16,128]{3,2,1,0:T(8,128)S(1)}, f32[2,4,16,128]{3,2,1,0:T(8,128)S(1)}, u32[]{:S(2)}, u32[]{:S(2)}) collective-permute-start(f32[2,4,16,128]{3,2,1,0:T(8,128)S(1)} %get-tuple-element.62), channel_id=1, source_target_pairs={{0,112},{16,0},{32,16},{48,32},{64,48},{80,64},{96,80},{112,96},{1... | collective-permute-start | bytes 196616 | tf_op jit(solution)/shard_map/ppermute | solution.py:412
  25.9 58.8 %copy-start.2 = (f32[4,1056,128]{2,1,0:T(8,128)}, f32[4,1056,128]{2,1,0:T(8,128)S(1)}, u32[]{:S(2)}) copy-start(f32[4,1056,128]{2,1,0:T(8,128)S(1)} %get-tuple-element.58.nu) | copy-start | bytes 6488068
  27.5 26.1 %collective-permute-start.4 = (f32[4,64,128]{2,1,0:T(8,128)S(1)}, f32[4,64,128]{2,1,0:T(8,128)S(1)}, u32[]{:S(2)}, u32[]{:S(2)}) collective-permute-start(f32[4,64,128]{2,1,0:T(8,128)S(1)} %get-tuple-element.75), channel_id=1, source_target_pairs={{0,1},{1,2},{2,3},{3,4},{4,5},{5,6},{6,7},{7,8},{8,9},{9,10},{10,1... | collective-permute-start | bytes 393224 | tf_op jit(solution)/shard_map/ppermute | solution.py:409
  27.6 26.0 %collective-permute-start.5 = (f32[4,64,128]{2,1,0:T(8,128)S(1)}, f32[4,64,128]{2,1,0:T(8,128)S(1)}, u32[]{:S(2)}, u32[]{:S(2)}) collective-permute-start(f32[4,64,128]{2,1,0:T(8,128)S(1)} %get-tuple-element.76), channel_id=1, source_target_pairs={{0,15},{1,0},{2,1},{3,2},{4,3},{5,4},{6,5},{7,6},{8,7},{9,8},{10,9... | collective-permute-start | bytes 393224 | tf_op jit(solution)/shard_map/ppermute | solution.py:410
  32.9 63.2 %collective-permute-start.20 = (f32[4,4,64,128]{3,2,1,0:T(8,128)S(1)}, f32[4,4,64,128]{3,2,1,0:T(8,128)S(1)}, u32[]{:S(2)}, u32[]{:S(2)}) collective-permute-start(f32[4,4,64,128]{3,2,1,0:T(8,128)S(1)} %get-tuple-element.97), channel_id=1, source_target_pairs={{0,1},{1,2},{2,3},{3,4},{4,5},{5,6},{6,7},{7,8},{8,9},{9,10},{10,1... | collective-permute-start | bytes 1572872 | tf_op jit(solution)/shard_map/ppermute | solution.py:409
  32.9 70.9 %collective-permute-start.21 = (f32[4,4,64,128]{3,2,1,0:T(8,128)S(1)}, f32[4,4,64,128]{3,2,1,0:T(8,128)S(1)}, u32[]{:S(2)}, u32[]{:S(2)}) collective-permute-start(f32[4,4,64,128]{3,2,1,0:T(8,128)S(1)} %get-tuple-element.98), channel_id=1, source_target_pairs={{0,15},{1,0},{2,1},{3,2},{4,3},{5,4},{6,5},{7,6},{8,7},{9,8},{10,9... | collective-permute-start | bytes 1572872 | tf_op jit(solution)/shard_map/ppermute | solution.py:410
  38.3 9.6 %collective-permute-start.6 = (f32[4,16,128]{2,1,0:T(8,128)S(1)}, f32[4,16,128]{2,1,0:T(8,128)S(1)}, u32[]{:S(2)}, u32[]{:S(2)}) collective-permute-start(f32[4,16,128]{2,1,0:T(8,128)S(1)} %get-tuple-element.77), channel_id=1, source_target_pairs={{0,16},{16,32},{32,48},{48,64},{64,80},{80,96},{96,112},{112,0},{1... | collective-permute-start | bytes 98312 | tf_op jit(solution)/shard_map/ppermute | solution.py:411
  47.9 5.7 %collective-permute-start.7 = (f32[4,16,128]{2,1,0:T(8,128)S(1)}, f32[4,16,128]{2,1,0:T(8,128)S(1)}, u32[]{:S(2)}, u32[]{:S(2)}) collective-permute-start(f32[4,16,128]{2,1,0:T(8,128)S(1)} %get-tuple-element.78), channel_id=1, source_target_pairs={{0,112},{16,0},{32,16},{48,32},{64,48},{80,64},{96,80},{112,96},{1... | collective-permute-start | bytes 98312 | tf_op jit(solution)/shard_map/ppermute | solution.py:412
  54.1 16.9 %collective-permute-start.8 = (f32[4,64,128]{2,1,0:T(8,128)S(1)}, f32[4,64,128]{2,1,0:T(8,128)S(1)}, u32[]{:S(2)}, u32[]{:S(2)}) collective-permute-start(f32[4,64,128]{2,1,0:T(8,128)S(1)} %get-tuple-element.82), channel_id=1, source_target_pairs={{0,1},{1,2},{2,3},{3,4},{4,5},{5,6},{6,7},{7,8},{8,9},{9,10},{10,1... | collective-permute-start | bytes 393224 | tf_op jit(solution)/shard_map/ppermute | solution.py:409
  54.1 16.9 %collective-permute-start.9 = (f32[4,64,128]{2,1,0:T(8,128)S(1)}, f32[4,64,128]{2,1,0:T(8,128)S(1)}, u32[]{:S(2)}, u32[]{:S(2)}) collective-permute-start(f32[4,64,128]{2,1,0:T(8,128)S(1)} %get-tuple-element.83), channel_id=1, source_target_pairs={{0,15},{1,0},{2,1},{3,2},{4,3},{5,4},{6,5},{7,6},{8,7},{9,8},{10,9... | collective-permute-start | bytes 393224 | tf_op jit(solution)/shard_map/ppermute | solution.py:410
  59.5 6.0 %collective-permute-start.10 = (f32[4,16,128]{2,1,0:T(8,128)S(1)}, f32[4,16,128]{2,1,0:T(8,128)S(1)}, u32[]{:S(2)}, u32[]{:S(2)}) collective-permute-start(f32[4,16,128]{2,1,0:T(8,128)S(1)} %get-tuple-element.84), channel_id=1, source_target_pairs={{0,16},{16,32},{32,48},{48,64},{64,80},{80,96},{96,112},{112,0},{1... | collective-permute-start | bytes 98312 | tf_op jit(solution)/shard_map/ppermute | solution.py:411
  65.5 5.5 %collective-permute-start.11 = (f32[4,16,128]{2,1,0:T(8,128)S(1)}, f32[4,16,128]{2,1,0:T(8,128)S(1)}, u32[]{:S(2)}, u32[]{:S(2)}) collective-permute-start(f32[4,16,128]{2,1,0:T(8,128)S(1)} %get-tuple-element.85), channel_id=1, source_target_pairs={{0,112},{16,0},{32,16},{48,32},{64,48},{80,64},{96,80},{112,96},{1... | collective-permute-start | bytes 98312 | tf_op jit(solution)/shard_map/ppermute | solution.py:412
  71.5 6.4 %collective-permute-start.14 = (f32[4,16,128]{2,1,0:T(8,128)S(1)}, f32[4,16,128]{2,1,0:T(8,128)S(1)}, u32[]{:S(2)}, u32[]{:S(2)}) collective-permute-start(f32[4,16,128]{2,1,0:T(8,128)S(1)} %get-tuple-element.91), channel_id=1, source_target_pairs={{0,16},{16,32},{32,48},{48,64},{64,80},{80,96},{96,112},{112,0},{1... | collective-permute-start | bytes 98312 | tf_op jit(solution)/shard_map/ppermute | solution.py:411
  73.6 8.0 %collective-permute-start.12 = (f32[4,64,128]{2,1,0:T(8,128)S(1)}, f32[4,64,128]{2,1,0:T(8,128)S(1)}, u32[]{:S(2)}, u32[]{:S(2)}) collective-permute-start(f32[4,64,128]{2,1,0:T(8,128)S(1)} %get-tuple-element.89), channel_id=1, source_target_pairs={{0,1},{1,2},{2,3},{3,4},{4,5},{5,6},{6,7},{7,8},{8,9},{9,10},{10,1... | collective-permute-start | bytes 393224 | tf_op jit(solution)/shard_map/ppermute | solution.py:409
  73.6 6.6 %collective-permute-start.15 = (f32[4,16,128]{2,1,0:T(8,128)S(1)}, f32[4,16,128]{2,1,0:T(8,128)S(1)}, u32[]{:S(2)}, u32[]{:S(2)}) collective-permute-start(f32[4,16,128]{2,1,0:T(8,128)S(1)} %get-tuple-element.92), channel_id=1, source_target_pairs={{0,112},{16,0},{32,16},{48,32},{64,48},{80,64},{96,80},{112,96},{1... | collective-permute-start | bytes 98312 | tf_op jit(solution)/shard_map/ppermute | solution.py:412
  77.9 12.4 %collective-permute-start.13 = (f32[4,64,128]{2,1,0:T(8,128)S(1)}, f32[4,64,128]{2,1,0:T(8,128)S(1)}, u32[]{:S(2)}, u32[]{:S(2)}) collective-permute-start(f32[4,64,128]{2,1,0:T(8,128)S(1)} %get-tuple-element.90), channel_id=1, source_target_pairs={{0,15},{1,0},{2,1},{3,2},{4,3},{5,4},{6,5},{7,6},{8,7},{9,8},{10,9... | collective-permute-start | bytes 393224 | tf_op jit(solution)/shard_map/ppermute | solution.py:410
  80.2 10.6 %collective-permute-start.22 = (f32[4,4,16,128]{3,2,1,0:T(8,128)S(1)}, f32[4,4,16,128]{3,2,1,0:T(8,128)S(1)}, u32[]{:S(2)}, u32[]{:S(2)}) collective-permute-start(f32[4,4,16,128]{3,2,1,0:T(8,128)S(1)} %get-tuple-element.99), channel_id=1, source_target_pairs={{0,16},{16,32},{32,48},{48,64},{64,80},{80,96},{96,112},{112,0},{1... | collective-permute-start | bytes 393224 | tf_op jit(solution)/shard_map/ppermute | solution.py:411
  81.6 14.5 %collective-permute-start.23 = (f32[4,4,16,128]{3,2,1,0:T(8,128)S(1)}, f32[4,4,16,128]{3,2,1,0:T(8,128)S(1)}, u32[]{:S(2)}, u32[]{:S(2)}) collective-permute-start(f32[4,4,16,128]{3,2,1,0:T(8,128)S(1)} %get-tuple-element.100), channel_id=1, source_target_pairs={{0,112},{16,0},{32,16},{48,32},{64,48},{80,64},{96,80},{112,96},{1... | collective-permute-start | bytes 393224 | tf_op jit(solution)/shard_map/ppermute | solution.py:412
  84.7 15.6 %slice-start = ((s8[6488064]{0:T(1024)(128)(4,1)}), s8[4194304]{0:T(1024)(128)(4,1)S(1)}, s32[]{:S(2)}) async-start(s8[6488064]{0:T(1024)(128)(4,1)} %bitcast.6), calls=%async_computation | async-start | bytes 8388608
  84.7 15.6 %slice-start.1 = ((s8[6488064]{0:T(1024)(128)(4,1)}), s8[2293760]{0:T(1024)(128)(4,1)S(1)}, s32[]{:S(2)}) async-start(s8[6488064]{0:T(1024)(128)(4,1)} %bitcast.6), calls=%async_computation.1 | async-start | bytes 4587520
  90.2 10.0 %copy-start.1 = (f32[4,1056,128]{2,1,0:T(8,128)S(1)}, f32[4,1056,128]{2,1,0:T(8,128)}, u32[]{:S(2)}) copy-start(f32[4,1056,128]{2,1,0:T(8,128)} %copy-done) | copy-start | bytes 6488068
  90.7 13.2 %collective-permute-start.16 = (f32[4,64,128]{2,1,0:T(8,128)S(1)}, f32[4,64,128]{2,1,0:T(8,128)S(1)}, u32[]{:S(2)}, u32[]{:S(2)}) collective-permute-start(f32[4,64,128]{2,1,0:T(8,128)S(1)} %get-tuple-element.93), channel_id=1, source_target_pairs={{0,1},{1,2},{2,3},{3,4},{4,5},{5,6},{6,7},{7,8},{8,9},{9,10},{10,1... | collective-permute-start | bytes 393224 | tf_op jit(solution)/shard_map/ppermute | solution.py:409
  90.8 13.1 %collective-permute-start.17 = (f32[4,64,128]{2,1,0:T(8,128)S(1)}, f32[4,64,128]{2,1,0:T(8,128)S(1)}, u32[]{:S(2)}, u32[]{:S(2)}) collective-permute-start(f32[4,64,128]{2,1,0:T(8,128)S(1)} %get-tuple-element.94), channel_id=1, source_target_pairs={{0,15},{1,0},{2,1},{3,2},{4,3},{5,4},{6,5},{7,6},{8,7},{9,8},{10,9... | collective-permute-start | bytes 393224 | tf_op jit(solution)/shard_map/ppermute | solution.py:410
  96.1 7.8 %collective-permute-start.18 = (f32[4,16,128]{2,1,0:T(8,128)S(1)}, f32[4,16,128]{2,1,0:T(8,128)S(1)}, u32[]{:S(2)}, u32[]{:S(2)}) collective-permute-start(f32[4,16,128]{2,1,0:T(8,128)S(1)} %get-tuple-element.95), channel_id=1, source_target_pairs={{0,16},{16,32},{32,48},{48,64},{64,80},{80,96},{96,112},{112,0},{1... | collective-permute-start | bytes 98312 | tf_op jit(solution)/shard_map/ppermute | solution.py:411
  96.1 7.8 %collective-permute-start.19 = (f32[4,16,128]{2,1,0:T(8,128)S(1)}, f32[4,16,128]{2,1,0:T(8,128)S(1)}, u32[]{:S(2)}, u32[]{:S(2)}) collective-permute-start(f32[4,16,128]{2,1,0:T(8,128)S(1)} %get-tuple-element.96), channel_id=1, source_target_pairs={{0,112},{16,0},{32,16},{48,32},{64,48},{80,64},{96,80},{112,96},{1... | collective-permute-start | bytes 98312 | tf_op jit(solution)/shard_map/ppermute | solution.py:412
  100.3 3.6 %copy-start.3 = (f32[4,1056,128]{2,1,0:T(8,128)S(1)}, f32[4,1056,128]{2,1,0:T(8,128)}, u32[]{:S(2)}) copy-start(f32[4,1056,128]{2,1,0:T(8,128)} %copy-done.2) | copy-start | bytes 6488068

commit v2 on v1

v2 whole, which is shorter than its diff:
```python
import functools
import math

import jax
import jax.numpy as jnp
from jax import lax
from jax.experimental import pallas as pl
from jax.experimental.pallas import tpu as pltpu
from jax.sharding import PartitionSpec as P

ITERS = 4
time_step = 0.1
force_gain = 0.3

NXL = 64
NYL = 16
NT = 4
PAD = 16
CELLS = NXL * NYL
ROWS = CELLS + 2 * PAD
F32 = jnp.float32
WIDTH = ("width", "thick")
MIB = 1024 * 1024
SHAPE = (NT, 8, 128)
OUTSIDE = 1e30


def sweep_weight(k):
    return 2.0 / (2.15 + 1.75 * math.cos(math.pi * (2 * k + 1) / (2 * ITERS)))


def z_up(a, fill=0.0):
    r = pltpu.roll(a, 127, 2)
    after = jnp.concatenate([r[1:], jnp.full_like(r[:1], fill)], axis=0)
    return jnp.where(lax.broadcasted_iota(jnp.int32, a.shape, 2) == 127, after, r)


def z_down(a):
    r = pltpu.roll(a, 1, 2)
    before = jnp.concatenate([jnp.zeros_like(r[:1]), r[:-1]], axis=0)
    return jnp.where(lax.broadcasted_iota(jnp.int32, a.shape, 2) == 0, before, r)


def recip(d):
    return pltpu.reciprocal(d, approx=True)


def sublanes():
    return lax.broadcasted_iota(jnp.int32, SHAPE, 1)


def row_of(x):
    return pl.multiple_of(PAD + x * NYL, NYL)


def fill_pads(ref, value=0.0):
    lead = (slice(None),) * (len(ref.shape) - 2)
    block = jnp.full(ref.shape[:-2] + (PAD, 128), value, F32)
    ref[lead + (pl.ds(0, PAD),)] = block
    ref[lead + (pl.ds(PAD + CELLS, PAD),)] = block


class Sides:
    def __init__(self, x0=0, planes=NXL):
        thick = lax.axis_index("thick")
        place = lax.axis_index("width") * 2 + thick
        cast = lax.axis_index("cast")
        last = lax.axis_size("width") * 2 - 1
        near = (NYL - 1) * (1 - thick)
        far = (NYL - 1) * thick

        def rows(pad):
            start = pad + x0 * NYL
            return (
                pl.ds(start + near, planes, stride=NYL),
                pl.ds(start + far, planes, stride=NYL),
                pl.ds(pad, NYL),
                pl.ds(pad + CELLS - NYL, NYL),
            )

        self.rows = rows(PAD)
        self.inner = rows(0)
        self.dims = (1, 1, 0, 0)
        high = jnp.where(thick == 0, 1.0, -1.0).astype(F32)
        self.signs = (high, -high, -1.0, 1.0)

        def inside(ok):
            return jnp.where(ok, 1.0, 0.0).astype(F32)

        self.masks = (
            1.0,
            inside(((thick == 0) & (place > 0)) | ((thick == 1) & (place < last))),
            inside(cast > 0),
            inside(cast < lax.axis_size("cast") - 1),
        )


CHUNKS = 4


def load_kernel(vel, mag, lab, v, hat, e, oa, ob, ol, oh, braw, lraw, sem):
    per = CELLS // CHUNKS
    for ch in range(CHUNKS):
        src = pl.ds(ch * per, per)
        dst = pl.ds(PAD + ch * per, per)
        for t in range(NT):
            pltpu.make_async_copy(vel.at[:, src, pl.ds(128 * t, 128)], v.at[:, t, dst], sem.at[ch, t]).start()
        pltpu.make_async_copy(mag.at[:, src], braw.at[:, src], sem.at[ch, NT]).start()
        pltpu.make_async_copy(lab.at[src], lraw.at[src], sem.at[ch, NT + 1]).start()
    fill_pads(v)
    fill_pads(e)
    fill_pads(hat, OUTSIDE)
    for ch in range(CHUNKS):
        src = pl.ds(ch * per, per)
        dst = pl.ds(PAD + ch * per, per)
        for t in range(NT):
            pltpu.make_async_copy(vel.at[:, src, pl.ds(128 * t, 128)], v.at[:, t, dst], sem.at[ch, t]).wait()
        pltpu.make_async_copy(mag.at[:, src], braw.at[:, src], sem.at[ch, NT]).wait()
        pltpu.make_async_copy(lab.at[src], lraw.at[src], sem.at[ch, NT + 1]).wait()

        @pl.loop(0, per // 8, unroll=8)
        def _(i):
            raw = pl.ds(pl.multiple_of(ch * per + i * 8, 8), 8)
            at = pl.ds(pl.multiple_of(PAD + ch * per + i * 8, 8), 8)
            for t in range(NT):
                col = pl.ds(128 * t, 128)
                lb = lraw[raw, col]
                hat[t, at, :] = jnp.where(lb == 0, 0.5, jnp.where(lb == 1, 0.5 / 0.7, 0.125)).astype(F32)
                v0, v1, v2 = (v[c, t, at, :] for c in range(3))
                b0, b1, b2 = (braw[c, raw, col] for c in range(3))
                e[0, t, at, :] = v1 * b2 - v2 * b1
                e[1, t, at, :] = v2 * b0 - v0 * b2
                e[2, t, at, :] = v0 * b1 - v1 * b0

    sides = Sides()
    for out, rows, d in zip((oa, ob, ol, oh), sides.rows, sides.dims):
        out[0] = hat[:, rows, :]
        out[1] = e[d, :, rows, :]
        out[2] = v[0, :, rows, :]


def faces(w0, hat, e, f, src, inv, phi):
    zero = jnp.zeros(SHAPE, F32)
    sub = sublanes()

    def body(x, carry):
        fxm, qxm, hc, exc = carry
        r = row_of(x)
        fxo, qxo, hn, exn = [], [], [], []
        for y in range(2):
            base = r + 8 * y
            at, up, down = pl.ds(base, 8), pl.ds(base + 1, 8), pl.ds(base - 1, 8)
            ahead = pl.ds(base + NYL, 8)
            c = hc[y]
            hn.append(hat[:, ahead, :])
            exn.append(e[0, :, ahead, :])
            fx = recip(c + hn[y])
            qx = fx * (exc[y] + exn[y])
            fxo.append(fx)
            qxo.append(qx)
            ey = e[1, :, at, :]
            fy = recip(c + hat[:, up, :])
            fym = recip(c + hat[:, down, :])
            if y == 1:
                fy = jnp.where(sub == 7, 0.0, fy)
            else:
                fym = jnp.where(sub == 0, 0.0, fym)
            fz = recip(c + z_up(c, OUTSIDE))
            ez = e[2, :, at, :]
            qz = fz * (ez + z_up(ez))
            total = (qx - qxm[y]) + (fy * (ey + e[1, :, up, :]) - fym * (ey + e[1, :, down, :])) + (qz - z_down(qz))
            diag = ((fx + fxm[y]) + (fy + fym)) + (fz + z_down(fz)) + 0.025 * recip(c)
            source = 0.5 * total
            inverse = recip(diag)
            f[0, :, at, :] = fx
            f[1, :, at, :] = fy
            f[2, :, at, :] = fz
            src[:, at, :] = source
            inv[:, at, :] = inverse
            phi[:, at, :] = (-w0) * (source * inverse)
        return tuple(fxo), tuple(qxo), tuple(hn), tuple(exn)

    first = [pl.ds(PAD + 8 * y, 8) for y in range(2)]
    start = (
        (zero, zero),
        (zero, zero),
        tuple(hat[:, at, :] for at in first),
        tuple(e[0, :, at, :] for at in first),
    )
    lax.fori_loop(0, NXL, body, start, unroll=8)


def face_kernel(w0, planes, hat, e, v, visc, f, src, inv, phi, nu, vnew, sem):
    copies = [
        pltpu.make_async_copy(visc.at[:, pl.ds(128 * t, 128)], nu.at[t, pl.ds(PAD, CELLS)], sem.at[t])
        for t in range(NT)
    ]
    for copy in copies:
        copy.start()
    f[1, :, 0:PAD, :] = jnp.zeros((NT, PAD, 128), F32)
    fill_pads(phi)
    fill_pads(nu)
    faces(w0, hat, e, f, src, inv, phi)
    for copy in copies:
        copy.wait()
    predictor(v, nu, vnew, *planes)


def first_edge_kernel(w0, ha, hb, hl, hh, hat, e, v, src_in, inv_in, phi_in,
                      src, inv, phi, ca, cb, cl, ch, oa, ob, ol, oh):
    del src_in, inv_in, phi_in
    s = Sides()
    sides = tuple(zip((ha, hb, hl, hh), (ca, cb, cl, ch), (oa, ob, ol, oh), s.rows, s.dims, s.signs, s.masks))
    for halo, coef, _, rows, d, sign, mask in sides:
        g = mask * recip(hat[:, rows, :] + halo[0])
        coef[...] = g
        src[:, rows, :] = src[:, rows, :] + (0.5 * sign) * (g * (e[d, :, rows, :] + halo[1]))
        inv[:, rows, :] = recip(recip(inv[:, rows, :]) + g)
    for _, coef, _, rows, _, _, _ in sides:
        i = inv[:, rows, :]
        coef[...] = coef[...] * i
        phi[:, rows, :] = (-w0) * (src[:, rows, :] * i)
    for _, _, out, rows, _, _, _ in sides:
        out[0] = phi[:, rows, :]
        out[1] = v[1, :, rows, :]


def edge_kernel(w, comp, phi_in, ca, cb, cl, ch, ha, hb, hl, hh, *rest):
    del phi_in
    flow = rest[0] if comp is not None else None
    phi, *outs = rest[-5:]
    rows_of = Sides().rows
    for coef, halo, rows in zip((ca, cb, cl, ch), (ha, hb, hl, hh), rows_of):
        phi[:, rows, :] = phi[:, rows, :] + w * (coef[...] * halo[0])
    for out, rows in zip(outs, rows_of):
        out[0] = phi[:, rows, :]
        if comp is not None:
            out[1] = flow[comp, :, rows, :] if len(flow.shape) == 4 else flow[:, rows, :]


def predictor(v, nu, vnew, x0, x1):
    sub = sublanes()
    half = 0.5 * time_step

    @pl.loop(x0, x1, unroll=8)
    def _(x):
        r = row_of(x)
        for y in range(2):
            base = r + 8 * y
            at = pl.ds(base, 8)
            ups = (pl.ds(base + NYL, 8), pl.ds(base + 1, 8))
            downs = (pl.ds(base - NYL, 8), pl.ds(base - 1, 8))
            n = nu[:, at, :]
            vc = [v[c, :, at, :] for c in range(3)]
            coefs = []
            total = None
            for d in range(3):
                above = nu[:, ups[d], :] if d < 2 else z_up(n)
                below = nu[:, downs[d], :] if d < 2 else z_down(n)
                up = (n + above) - vc[d]
                down = (n + below) + vc[d]
                if d == 1 and y == 1:
                    up = jnp.where(sub == 7, 0.0, up)
                if d == 1 and y == 0:
                    down = jnp.where(sub == 0, 0.0, down)
                coefs.append((up, down))
                both = up + down
                total = both if total is None else total + both
            keep = 1.0 - half * total
            for c in range(3):
                acc = None
                for d in range(3):
                    above = v[c, :, ups[d], :] if d < 2 else z_up(vc[c])
                    below = v[c, :, downs[d], :] if d < 2 else z_down(vc[c])
                    term = coefs[d][0] * above + coefs[d][1] * below
                    acc = term if acc is None else acc + term
                vnew[c, :, at, :] = half * acc + keep * vc[c]


def sweep_kernel(w, planes, phi, f, src, inv, v, nu, vnew_in, out, vnew):
    del vnew_in
    fill_pads(out)
    zero = jnp.zeros(SHAPE, F32)

    def body(x, carry):
        pxm, pc = carry
        r = row_of(x)
        px, pn = [], []
        for y in range(2):
            base = r + 8 * y
            at, up, down = pl.ds(base, 8), pl.ds(base + 1, 8), pl.ds(base - 1, 8)
            pn.append(phi[:, pl.ds(base + NYL, 8), :])
            fx = f[0, :, at, :]
            c = pc[y]
            px.append(fx * c)
            t = fx * pn[y] + pxm[y]
            t = t + f[1, :, at, :] * phi[:, up, :]
            t = t + f[1, :, down, :] * phi[:, down, :]
            fz = f[2, :, at, :]
            t = t + fz * z_up(c)
            t = t + z_down(fz * c)
            out[:, at, :] = c + w * ((t - src[:, at, :]) * inv[:, at, :] - c)
        return tuple(px), tuple(pn)

    start = ((zero, zero), tuple(phi[:, pl.ds(PAD + 8 * y, 8), :] for y in range(2)))
    lax.fori_loop(0, NXL, body, start, unroll=16)
    predictor(v, nu, vnew, *planes)


def force_kernel(phi, hat, e, mag, v, nu, *rest):
    flows = [rest[4 * i : 4 * i + 4] for i in range(4)]
    potential, vnew, *edge_b = rest[17:23]
    bv, sem = rest[23:]
    per = CELLS // CHUNKS

    def magnetic(ch):
        src = pl.ds(ch * per, per)
        return [
            pltpu.make_async_copy(mag.at[:, src, pl.ds(128 * t, 128)], bv.at[:, t, src], sem.at[ch, t])
            for t in range(NT)
        ]

    copies = [
        pltpu.make_async_copy(
            phi.at[t, pl.ds(PAD, CELLS)], potential.at[:, pl.ds(128 * t, 128)], sem.at[CHUNKS, t]
        )
        for t in range(NT)
    ]
    for ch in range(CHUNKS):
        for copy in magnetic(ch):
            copy.start()
    for copy in copies:
        copy.start()

    s = Sides()
    half = 0.5 * time_step
    for i in range(4):
        rows, d, sign, mask = s.rows[i], s.dims[i], s.signs[i], s.masks[i]
        other = [mask * flows[0][i][2], mask * flows[1][i][1], mask * flows[2][i][1]]
        hn = mask * flows[3][i][1]
        coef = half * ((nu[:, rows, :] + hn) - sign * v[d, :, rows, :])
        gone = half * hn if d == 0 else coef
        for c in range(3):
            vnew[c, :, rows, :] = vnew[c, :, rows, :] + (coef * other[c] - gone * v[c, :, rows, :])

    sub = sublanes()
    for ch in range(CHUNKS):
        for copy in magnetic(ch):
            copy.wait()

        @pl.loop(ch * (NXL // CHUNKS), (ch + 1) * (NXL // CHUNKS), unroll=8)
        def _(x):
            r = row_of(x)
            for y in range(2):
                base = r + 8 * y
                at = pl.ds(base, 8)
                raw = pl.ds(pl.multiple_of(x * NYL + 8 * y, 8), 8)
                p = phi[:, at, :]
                yu = phi[:, pl.ds(base + 1, 8), :]
                yd = phi[:, pl.ds(base - 1, 8), :]
                if y == 1:
                    yu = jnp.where(sub == 7, 0.0, yu)
                else:
                    yd = jnp.where(sub == 0, 0.0, yd)
                diffs = (
                    phi[:, pl.ds(base + NYL, 8), :] - phi[:, pl.ds(base - NYL, 8), :],
                    yu - yd,
                    z_up(p) - z_down(p),
                )
                g = (0.5 * force_gain) * recip(hat[:, at, :])
                cur = [g * (e[d, :, at, :] - 0.5 * diffs[d]) for d in range(3)]
                b0, b1, b2 = (bv[c, :, raw, :] for c in range(3))
                c0, c1, c2 = cur
                vnew[0, :, at, :] = vnew[0, :, at, :] + (c1 * b2 - c2 * b1)
                vnew[1, :, at, :] = vnew[1, :, at, :] + (c2 * b0 - c0 * b2)
                vnew[2, :, at, :] = vnew[2, :, at, :] + (c0 * b1 - c1 * b0)

    for i in range(4):
        rows, d, sign = s.rows[i], s.dims[i], s.signs[i]
        inner = s.inner[i]
        n1, n2 = (d + 1) % 3, (d + 2) % 3
        g = (0.25 * force_gain * sign) * (s.masks[i] * recip(hat[:, rows, :]))
        edge_b[i][0] = g * bv[n2, :, inner, :]
        edge_b[i][1] = -g * bv[n1, :, inner, :]
    for copy in copies:
        copy.wait()


def last_kernel(ka, kb, kl, kh, ha, hb, hl, hh, vnew_in, result, vnew, sem):
    del vnew_in
    planes = NXL // CHUNKS
    copies = []
    for ch in range(CHUNKS):
        s = Sides(ch * planes, planes)
        some = pl.ds(ch * planes, planes)
        todo = [(ka, ha, 0, some), (kb, hb, 1, some)]
        if ch == 0:
            todo.append((kl, hl, 2, pl.ds(0, NYL)))
        if ch == CHUNKS - 1:
            todo.append((kh, hh, 3, pl.ds(0, NYL)))
        for k, h, i, part in todo:
            rows, d = s.rows[i], s.dims[i]
            halo = h[0, :, part, :]
            for j, c in enumerate(((d + 1) % 3, (d + 2) % 3)):
                vnew[c, :, rows, :] = vnew[c, :, rows, :] + k[j, :, part, :] * halo
        per = planes * NYL
        for t in range(NT):
            copy = pltpu.make_async_copy(
                vnew.at[:, t, pl.ds(PAD + ch * per, per)],
                result.at[:, pl.ds(ch * per, per), pl.ds(128 * t, 128)],
                sem.at[ch, t],
            )
            copy.start()
            copies.append(copy)
    for copy in copies:
        copy.wait()


def resident(*shape):
    return pltpu.VMEM(shape, F32)


def in_vmem(x):
    return pltpu.with_memory_space_constraint(x, pltpu.VMEM)


def in_hbm(x):
    return pltpu.with_memory_space_constraint(x, pltpu.HBM)


IN_VMEM = pl.BlockSpec(memory_space=pltpu.VMEM)
IN_HBM = pl.BlockSpec(memory_space=pl.ANY)

FIELD = (NT, ROWS, 128)


def run(kernel, name, ins, outs, aliases=None, scratch=(), flops=0, moved=0, limit=8 * MIB):
    args = [in_hbm(a) if hbm else in_vmem(a) for a, hbm in ins]
    return pl.pallas_call(
        kernel,
        out_shape=outs,
        in_specs=[IN_HBM if hbm else IN_VMEM for _, hbm in ins],
        out_specs=[IN_HBM if isinstance(o, jax.ShapeDtypeStruct) else IN_VMEM for o in outs],
        input_output_aliases=aliases or {},
        scratch_shapes=list(scratch),
        compiler_params=pltpu.CompilerParams(vmem_limit_bytes=limit),
        cost_estimate=pl.CostEstimate(flops=flops, bytes_accessed=moved, transcendentals=0),
        name=name,
    )(*args)


def vm(*arrays):
    return [(a, False) for a in arrays]


def ring(axis, step):
    n = lax.axis_size(axis)
    return [(i, (i + step) % n) for i in range(n)]


def exchange(a, b, low, high):
    n = lax.axis_size("width") * 2
    across = [(i, (((i + 1) ^ 1) - 1) % n) for i in range(n)]
    hb = lax.ppermute(b, WIDTH, across)
    hl = lax.ppermute(high, "cast", ring("cast", 1))
    hh = lax.ppermute(low, "cast", ring("cast", -1))
    ha = lax.ppermute(a, "thick", [(0, 1), (1, 0)])
    return ha, hb, hl, hh


def edge_planes(n):
    return [resident(n, NT, NXL, 128)] * 2 + [resident(n, NT, NYL, 128)] * 2


def local(velocity, magnetic, labels, viscosity):
    vel = velocity.reshape(3, CELLS, NT * 128)
    mag = magnetic.reshape(3, CELLS, NT * 128)
    lab = labels.reshape(CELLS, NT * 128)
    visc = viscosity.reshape(CELLS, NT * 128)
    dma = pltpu.SemaphoreType.DMA
    w = [sweep_weight(k) for k in range(ITERS)]
    field, fields = resident(*FIELD), resident(3, *FIELD)
    cuts = (0, 16, 32, 48, 64)

    v, hat, e, *edges = run(
        load_kernel, "load", [(vel, True), (mag, True), (lab, True)],
        [fields, field, fields] + edge_planes(3),
        scratch=[
            pltpu.VMEM((3, CELLS, NT * 128), F32),
            pltpu.VMEM((CELLS, NT * 128), jnp.int32),
            dma((CHUNKS, NT + 2)),
        ],
        limit=12 * MIB,
    )
    halos = exchange(*edges)
    flows = [halos]
    f, src, inv, phi, nu, vnew = run(
        functools.partial(face_kernel, w[0], cuts[:2]), "faces", vm(hat, e, v) + [(visc, True)],
        [fields, field, field, field, field, fields],
        scratch=[dma((NT,))], flops=10_000_000, moved=20 * MIB,
    )
    src, inv, phi, *rest = run(
        functools.partial(first_edge_kernel, w[0]), "edges1", vm(*halos, hat, e, v, src, inv, phi),
        [field] * 3 + [resident(*o.shape[1:]) for o in edge_planes(1)] + edge_planes(2),
        aliases={7: 0, 8: 1, 9: 2},
    )
    coefs, edges = rest[:4], rest[4:]
    for k in range(1, ITERS):
        halos = exchange(*edges)
        flows.append(halos)
        phi, vnew = run(
            functools.partial(sweep_kernel, w[k], cuts[k : k + 2]), f"sweep{k}", vm(phi, f, src, inv, v, nu, vnew),
            [field, fields], aliases={6: 1}, flops=10_000_000, moved=16 * MIB,
        )
        comp, flow = ((2, [v]), (0, [nu]), (None, []))[k - 1]
        phi, *edges = run(
            functools.partial(edge_kernel, w[k], comp), f"edges{k + 1}", vm(phi, *coefs, *halos, *flow),
            [field] + edge_planes(1 if comp is None else 2), aliases={0: 0},
        )
    halos = exchange(*edges)
    potential, vnew, *products = run(
        force_kernel, "force",
        vm(phi, hat, e) + [(mag, True)] + vm(v, nu, *[h for group in flows for h in group], vnew),
        [jax.ShapeDtypeStruct((CELLS, NT * 128), F32), fields] + edge_planes(2),
        aliases={22: 1}, scratch=[pltpu.VMEM((3, NT, CELLS, 128), F32), dma((CHUNKS + 1, NT))],
        flops=10_000_000, moved=16 * MIB, limit=12 * MIB,
    )
    result, _ = run(
        last_kernel, "last", vm(*products, *halos, vnew),
        [jax.ShapeDtypeStruct((3, CELLS, NT * 128), F32), fields],
        aliases={8: 1}, scratch=[dma((CHUNKS, NT))],
    )
    return result.reshape(velocity.shape), potential.reshape(labels.shape)


def solution(mesh):
    fields = P(None, "cast", WIDTH, None)
    scalar = P("cast", WIDTH, None)
    return jax.shard_map(
        local,
        mesh=mesh,
        in_specs=(fields, fields, scalar, scalar),
        out_specs=(fields, scalar),
        check_vma=False,
    )
```

time: 110 us -> 81.7 us (0.74)
  starting transfers between devices: 47.4 us -> 35.8 us
  waiting for transfers between devices: 16.8 us -> 9.18 us
  Pallas kernels: 40.7 us -> 34.7 us
  local copies, waits for them, and re-layouts: 2.75 us -> 0 us
    ppermute x24 -> x20, starting transfers between devices: 47.4 us -> 35.8 us  [the longest x5 21.5 us: exchange(): hh = lax.ppermute(low, 'cast', ring('cast', -1))]
    ppermute x24 -> x20, waiting for transfers between devices: 16.8 us -> 9.18 us  [the longest x5 7.95 us: exchange(): hl = lax.ppermute(high, 'cast', ring('cast', 1))]
    pallas_call x11, Pallas kernels: 40.7 us -> 34.7 us  [run(): pl.pallas_call(kernel, out_shape=outs, in_specs=[IN_HBM if hbm else IN_VM...]
    unnamed x14 -> x0, local copies, waits for them, and re-layouts: 2.75 us -> none
  transfers between devices with their start and end apart: 24 -> 20, of which waited for: 4 -> 6; matrix products, arithmetic and copies ran while one was open for 0% -> 0% of each run, Pallas kernels for 26% -> 28%
where the time goes in v2:
time: 81.7 us; the launch traced here: 80.7 us
  starting transfers between devices  35.8 us (44%)
  Pallas kernels  34.7 us (42%)
  waiting for transfers between devices  9.18 us (11%)
  between operations  0.96 us (1%)
    pallas_call x11, Pallas kernels, run(): pl.pallas_call(kernel, out_shape=outs, in_specs=[IN_HBM if hbm else IN_VM...  34.7 us
    ppermute x5, starting transfers between devices, exchange(): hh = lax.ppermute(low, 'cast', ring('cast', -1))  21.5 us
    ppermute x5, starting transfers between devices, exchange(): hb = lax.ppermute(b, WIDTH, across)  11.9 us
    ppermute x5, waiting for transfers between devices, exchange(): hl = lax.ppermute(high, 'cast', ring('cast', 1))  7.95 us
    ppermute x5, starting transfers between devices, exchange(): hl = lax.ppermute(high, 'cast', ring('cast', 1))  1.93 us
  transfers between devices with their start and end apart: 20, of which 6 were waited for; matrix products, arithmetic and copies ran while one was open for 0% of the time, Pallas kernels for 28%

profile of v2, /device:TPU:2, one launch (start us, length us, event | category | flops | bytes accessed | tf_op | source)
XLA Modules:
  0.0 80.7 jit_solution(17812726865821024524)
XLA Ops:
  0.6 6.2 %load.1 = (f32[3,4,1056,128]{3,2,1,0:T(8,128)S(1)}, f32[4,1056,128]{2,1,0:T(8,128)S(1)}, f32[3,4,1056,128]{3,2,1,0:T(8,128)S(1)}, f32[3,4,64,128]{3,2,1,0:T(8,12...) custom-call(f32[3,1024,512]{2,1,0:T(8,128)} %bitcast.8, ...), custom_call_target="tpu_custom_call" | custom-call | tf_op jit(solution)/shard_map/load/pallas_call | solution.py:439
  6.8 0.1 collective-permute-start
  6.9 4.7 %collective-permute-start.1 = (f32[3,4,64,128]{3,2,1,0:T(8,128)S(1)}, f32[3,4,64,128]{3,2,1,0:T(8,128)S(1)}, u32[]{:S(2)}, u32[]{:S(2)}) collective-permute-start(f32[3,4,64,128]{3,2,1,0:T(8,128)S(1)} %get-tuple-element.55), channel_id=1, source_target_pairs={{0,15},{1,2},{2,1},{3,4},{4,3},{5,6},{6,5},{7,8},{8,7},{9,10},{10,... | collective-permute-start | bytes 1179656 | tf_op jit(solution)/shard_map/ppermute | solution.py:464
  11.6 1.9 %collective-permute-start.2 = (f32[3,4,16,128]{3,2,1,0:T(8,128)S(1)}, f32[3,4,16,128]{3,2,1,0:T(8,128)S(1)}, u32[]{:S(2)}, u32[]{:S(2)}) collective-permute-start(f32[3,4,16,128]{3,2,1,0:T(8,128)S(1)} %get-tuple-element.56), channel_id=1, source_target_pairs={{0,16},{16,32},{32,48},{48,64},{64,80},{80,96},{96,112},{112,0},{1... | collective-permute-start | bytes 294920 | tf_op jit(solution)/shard_map/ppermute | solution.py:465
  13.5 3.0 %collective-permute-start.3 = (f32[3,4,16,128]{3,2,1,0:T(8,128)S(1)}, f32[3,4,16,128]{3,2,1,0:T(8,128)S(1)}, u32[]{:S(2)}, u32[]{:S(2)}) collective-permute-start(f32[3,4,16,128]{3,2,1,0:T(8,128)S(1)} %get-tuple-element.57), channel_id=1, source_target_pairs={{0,112},{16,0},{32,16},{48,32},{64,48},{80,64},{96,80},{112,96},{1... | collective-permute-start | bytes 294920 | tf_op jit(solution)/shard_map/ppermute | solution.py:466
  16.5 8.0 %faces.1 = (f32[3,4,1056,128]{3,2,1,0:T(8,128)S(1)}, f32[4,1056,128]{2,1,0:T(8,128)S(1)}, f32[4,1056,128]{2,1,0:T(8,128)S(1)}, f32[4,1056,128]{2,1,0:T(8,128)S(1...) custom-call(f32[4,1056,128]{2,1,0:T(8,128)S(1)} %get-tuple-element.58.hat, ...), custom_call_target="tpu_custom_call" | custom-call | flops 10000000 | bytes 20971520 | tf_op jit(solution)/shard_map/faces/pallas_call | solution.py:439
  24.6 1.0 %collective-permute-done.2.hl.rest_2_ = f32[3,4,16,128]{3,2,1,0:T(8,128)S(1)} collective-permute-done((f32[3,4,16,128]{3,2,1,0:T(8,128)S(1)}, f32[3,4,16,128]{3,2,1,0:T(8,128)S(1)}, u32[]{:S(2)}, u32[]{:S(2)}) %collective-permute-start.2) | collective-permute-done | bytes 98336 | tf_op jit(solution)/shard_map/ppermute | solution.py:465
  25.5 1.6 %edges1.1 = (f32[4,1056,128]{2,1,0:T(8,128)S(1)}, f32[4,1056,128]{2,1,0:T(8,128)S(1)}, f32[4,1056,128]{2,1,0:T(8,128)S(1)}, f32[4,64,128]{2,1,0:T(8,128)S(1)}, f...) custom-call(f32[3,4,64,128]{3,2,1,0:T(8,128)S(1)} %collective-permut, ...), custom_call_target="tpu_custom_call", output_to_operand_aliasing={{0}: (7, {}), {1}: (8, {}), {2}: (9, {})} | custom-call | tf_op jit(solution)/shard_map/edges1/pallas_call | solution.py:439
  27.2 0.1 collective-permute-start.4
  27.3 2.3 %collective-permute-start.5 = (f32[2,4,64,128]{3,2,1,0:T(8,128)S(1)}, f32[2,4,64,128]{3,2,1,0:T(8,128)S(1)}, u32[]{:S(2)}, u32[]{:S(2)}) collective-permute-start(f32[2,4,64,128]{3,2,1,0:T(8,128)S(1)} %get-tuple-element.76), channel_id=1, source_target_pairs={{0,15},{1,2},{2,1},{3,4},{4,3},{5,6},{6,5},{7,8},{8,7},{9,10},{10,... | collective-permute-start | bytes 786440 | tf_op jit(solution)/shard_map/ppermute | solution.py:464
  29.5 4.1 %collective-permute-start.7 = (f32[2,4,16,128]{3,2,1,0:T(8,128)S(1)}, f32[2,4,16,128]{3,2,1,0:T(8,128)S(1)}, u32[]{:S(2)}, u32[]{:S(2)}) collective-permute-start(f32[2,4,16,128]{3,2,1,0:T(8,128)S(1)} %get-tuple-element.78), channel_id=1, source_target_pairs={{0,112},{16,0},{32,16},{48,32},{64,48},{80,64},{96,80},{112,96},{1... | collective-permute-start | bytes 196616 | tf_op jit(solution)/shard_map/ppermute | solution.py:466
  33.6 3.1 %sweep1.1 = (f32[4,1056,128]{2,1,0:T(8,128)S(1)}, f32[3,4,1056,128]{3,2,1,0:T(8,128)S(1)}) custom-call(f32[4,1056,128]{2,1,0:T(8,128)S(1)} %get-tuple-element.64.phi, f32[3,4,1056,128]{3,2,1,0:T(8,128)S(1)} %get-tuple-element.65.f, f32[4,1056,128]{2,1,0:T(8,128)S(1)} %get-tuple-element.66.src, ...), custom_call_target="tpu_custom_call", output_to_operand_aliasing={{1}: (6, {})} | custom-call | flops 10000000 | bytes 16777216 | tf_op jit(solution)/shard_map/sweep1/pallas_call | solution.py:439
  36.7 1.1 %collective-permute-done.6.hl.rest_6_ = f32[2,4,16,128]{3,2,1,0:T(8,128)S(1)} collective-permute-done((f32[2,4,16,128]{3,2,1,0:T(8,128)S(1)}, f32[2,4,16,128]{3,2,1,0:T(8,128)S(1)}, u32[]{:S(2)}, u32[]{:S(2)}) %collective-permute-start.6) | collective-permute-done | bytes 65568 | tf_op jit(solution)/shard_map/ppermute | solution.py:465
  37.9 0.8 collective-permute-done.5.hb.rest_5_
  38.6 0.6 edges2.1
  39.2 0.1 collective-permute-start.8
  39.3 2.1 %collective-permute-start.9 = (f32[2,4,64,128]{3,2,1,0:T(8,128)S(1)}, f32[2,4,64,128]{3,2,1,0:T(8,128)S(1)}, u32[]{:S(2)}, u32[]{:S(2)}) collective-permute-start(f32[2,4,64,128]{3,2,1,0:T(8,128)S(1)} %get-tuple-element.83), channel_id=1, source_target_pairs={{0,15},{1,2},{2,1},{3,4},{4,3},{5,6},{6,5},{7,8},{8,7},{9,10},{10,... | collective-permute-start | bytes 786440 | tf_op jit(solution)/shard_map/ppermute | solution.py:464
  41.4 5.1 %collective-permute-start.11 = (f32[2,4,16,128]{3,2,1,0:T(8,128)S(1)}, f32[2,4,16,128]{3,2,1,0:T(8,128)S(1)}, u32[]{:S(2)}, u32[]{:S(2)}) collective-permute-start(f32[2,4,16,128]{3,2,1,0:T(8,128)S(1)} %get-tuple-element.85), channel_id=1, source_target_pairs={{0,112},{16,0},{32,16},{48,32},{64,48},{80,64},{96,80},{112,96},{1... | collective-permute-start | bytes 196616 | tf_op jit(solution)/shard_map/ppermute | solution.py:466
  46.5 3.1 %sweep2.1 = (f32[4,1056,128]{2,1,0:T(8,128)S(1)}, f32[3,4,1056,128]{3,2,1,0:T(8,128)S(1)}) custom-call(f32[4,1056,128]{2,1,0:T(8,128)S(1)} %get-tuple-element.79.phi, f32[3,4,1056,128]{3,2,1,0:T(8,128)S(1)} %get-tuple-element.65.f, f32[4,1056,128]{2,1,0:T(8,128)S(1)} %get-tuple-element.66.src, ...), custom_call_target="tpu_custom_call", output_to_operand_aliasing={{1}: (6, {})} | custom-call | flops 10000000 | bytes 16777216 | tf_op jit(solution)/shard_map/sweep2/pallas_call | solution.py:439
  49.6 3.1 %collective-permute-done.10.hl.rest_10_ = f32[2,4,16,128]{3,2,1,0:T(8,128)S(1)} collective-permute-done((f32[2,4,16,128]{3,2,1,0:T(8,128)S(1)}, f32[2,4,16,128]{3,2,1,0:T(8,128)S(1)}, u32[]{:S(2)}, u32[]{:S(2)}) %collective-permute-start.10) | collective-permute-done | bytes 65568 | tf_op jit(solution)/shard_map/ppermute | solution.py:465
  52.7 0.6 edges3.1
  53.3 0.1 collective-permute-start.12
  53.4 1.6 %collective-permute-start.13 = (f32[2,4,64,128]{3,2,1,0:T(8,128)S(1)}, f32[2,4,64,128]{3,2,1,0:T(8,128)S(1)}, u32[]{:S(2)}, u32[]{:S(2)}) collective-permute-start(f32[2,4,64,128]{3,2,1,0:T(8,128)S(1)} %get-tuple-element.90), channel_id=1, source_target_pairs={{0,15},{1,2},{2,1},{3,4},{4,3},{5,6},{6,5},{7,8},{8,7},{9,10},{10,... | collective-permute-start | bytes 786440 | tf_op jit(solution)/shard_map/ppermute | solution.py:464
  55.0 4.1 %collective-permute-start.15 = (f32[2,4,16,128]{3,2,1,0:T(8,128)S(1)}, f32[2,4,16,128]{3,2,1,0:T(8,128)S(1)}, u32[]{:S(2)}, u32[]{:S(2)}) collective-permute-start(f32[2,4,16,128]{3,2,1,0:T(8,128)S(1)} %get-tuple-element.92), channel_id=1, source_target_pairs={{0,112},{16,0},{32,16},{48,32},{64,48},{80,64},{96,80},{112,96},{1... | collective-permute-start | bytes 196616 | tf_op jit(solution)/shard_map/ppermute | solution.py:466
  59.1 3.1 %sweep3.1 = (f32[4,1056,128]{2,1,0:T(8,128)S(1)}, f32[3,4,1056,128]{3,2,1,0:T(8,128)S(1)}) custom-call(f32[4,1056,128]{2,1,0:T(8,128)S(1)} %get-tuple-element.86.phi, f32[3,4,1056,128]{3,2,1,0:T(8,128)S(1)} %get-tuple-element.65.f, f32[4,1056,128]{2,1,0:T(8,128)S(1)} %get-tuple-element.66.src, ...), custom_call_target="tpu_custom_call", output_to_operand_aliasing={{1}: (6, {})} | custom-call | flops 10000000 | bytes 16777216 | tf_op jit(solution)/shard_map/sweep3/pallas_call | solution.py:439
  62.2 2.8 %collective-permute-done.14.hl.rest_14_ = f32[2,4,16,128]{3,2,1,0:T(8,128)S(1)} collective-permute-done((f32[2,4,16,128]{3,2,1,0:T(8,128)S(1)}, f32[2,4,16,128]{3,2,1,0:T(8,128)S(1)}, u32[]{:S(2)}, u32[]{:S(2)}) %collective-permute-start.14) | collective-permute-done | bytes 65568 | tf_op jit(solution)/shard_map/ppermute | solution.py:465
  65.0 0.4 collective-permute-done.13.hb.rest_13_
  65.4 0.5 edges4.1
  66.0 1.3 %collective-permute-start.17 = (f32[1,4,64,128]{3,2,1,0:T(8,128)S(1)}, f32[1,4,64,128]{3,2,1,0:T(8,128)S(1)}, u32[]{:S(2)}, u32[]{:S(2)}) collective-permute-start(f32[1,4,64,128]{3,2,1,0:T(8,128)S(1)} %get-tuple-element.100), channel_id=1, source_target_pairs={{0,15},{1,2},{2,1},{3,4},{4,3},{5,6},{6,5},{7,8},{8,7},{9,10},{10,... | collective-permute-start | bytes 393224 | tf_op jit(solution)/shard_map/ppermute | solution.py:464
  67.3 5.2 %collective-permute-start.19 = (f32[1,4,16,128]{3,2,1,0:T(8,128)S(1)}, f32[1,4,16,128]{3,2,1,0:T(8,128)S(1)}, u32[]{:S(2)}, u32[]{:S(2)}) collective-permute-start(f32[1,4,16,128]{3,2,1,0:T(8,128)S(1)} %get-tuple-element.102), channel_id=1, source_target_pairs={{0,112},{16,0},{32,16},{48,32},{64,48},{80,64},{96,80},{112,96},{1... | collective-permute-start | bytes 98312 | tf_op jit(solution)/shard_map/ppermute | solution.py:466
  72.5 5.0 %force.1 = (f32[1024,512]{1,0:T(8,128)}, f32[3,4,1056,128]{3,2,1,0:T(8,128)S(1)}, f32[2,4,64,128]{3,2,1,0:T(8,128)S(1)}, f32[2,4,64,128]{3,2,1,0:T(8,128)S(1)}, ...) custom-call(f32[4,1056,128]{2,1,0:T(8,128)S(1)} %get-tuple-element.93.phi, ...), custom_call_target="tpu_custom_call", output_to_operand_aliasing={{1}: (22, {})} | custom-call | flops 10000000 | bytes 16777216 | tf_op jit(solution)/shard_map/force/pallas_call | solution.py:439
  77.6 2.9 %last.1 = (f32[3,1024,512]{2,1,0:T(8,128)}, f32[3,4,1056,128]{3,2,1,0:T(8,128)S(1)}) custom-call(f32[2,4,64,128]{3,2,1,0:T(8,128)S(1)} %get-tuple-element.95.ka, f32[2,4,64,128]{3,2,1,0:T(8,128)S(1)} %get-tuple-element.96.kb, f32[2,4,16,128]{3,2,1,0:T(8,128)S(1)} %get-tuple-element.97.kl, ...), custom_call_target="tpu_custom_call", output_to_operand_aliasing={{1}: (8, {})} | custom-call | tf_op jit(solution)/shard_map/last/pallas_call | solution.py:439
  (19 shorter events, 0.1 us)
Async XLA Ops:
  6.8 18.7 %collective-permute-start = (f32[3,4,64,128]{3,2,1,0:T(8,128)S(1)}, f32[3,4,64,128]{3,2,1,0:T(8,128)S(1)}, u32[]{:S(2)}, u32[]{:S(2)}) collective-permute-start(f32[3,4,64,128]{3,2,1,0:T(8,128)S(1)} %get-tuple-element.54), channel_id=1, source_target_pairs={{0,1},{1,0},{2,3},{3,2},{4,5},{5,4},{6,7},{7,6},{8,9},{9,8},{10,11... | collective-permute-start | bytes 1179656 | tf_op jit(solution)/shard_map/ppermute | solution.py:467
  6.9 18.6 %collective-permute-start.1 = (f32[3,4,64,128]{3,2,1,0:T(8,128)S(1)}, f32[3,4,64,128]{3,2,1,0:T(8,128)S(1)}, u32[]{:S(2)}, u32[]{:S(2)}) collective-permute-start(f32[3,4,64,128]{3,2,1,0:T(8,128)S(1)} %get-tuple-element.55), channel_id=1, source_target_pairs={{0,15},{1,2},{2,1},{3,4},{4,3},{5,6},{6,5},{7,8},{8,7},{9,10},{10,... | collective-permute-start | bytes 1179656 | tf_op jit(solution)/shard_map/ppermute | solution.py:464
  11.6 13.9 %collective-permute-start.2 = (f32[3,4,16,128]{3,2,1,0:T(8,128)S(1)}, f32[3,4,16,128]{3,2,1,0:T(8,128)S(1)}, u32[]{:S(2)}, u32[]{:S(2)}) collective-permute-start(f32[3,4,16,128]{3,2,1,0:T(8,128)S(1)} %get-tuple-element.56), channel_id=1, source_target_pairs={{0,16},{16,32},{32,48},{48,64},{64,80},{80,96},{96,112},{112,0},{1... | collective-permute-start | bytes 294920 | tf_op jit(solution)/shard_map/ppermute | solution.py:465
  13.5 12.0 %collective-permute-start.3 = (f32[3,4,16,128]{3,2,1,0:T(8,128)S(1)}, f32[3,4,16,128]{3,2,1,0:T(8,128)S(1)}, u32[]{:S(2)}, u32[]{:S(2)}) collective-permute-start(f32[3,4,16,128]{3,2,1,0:T(8,128)S(1)} %get-tuple-element.57), channel_id=1, source_target_pairs={{0,112},{16,0},{32,16},{48,32},{64,48},{80,64},{96,80},{112,96},{1... | collective-permute-start | bytes 294920 | tf_op jit(solution)/shard_map/ppermute | solution.py:466
  27.2 10.7 %collective-permute-start.4 = (f32[2,4,64,128]{3,2,1,0:T(8,128)S(1)}, f32[2,4,64,128]{3,2,1,0:T(8,128)S(1)}, u32[]{:S(2)}, u32[]{:S(2)}) collective-permute-start(f32[2,4,64,128]{3,2,1,0:T(8,128)S(1)} %get-tuple-element.75), channel_id=1, source_target_pairs={{0,1},{1,0},{2,3},{3,2},{4,5},{5,4},{6,7},{7,6},{8,9},{9,8},{10,11... | collective-permute-start | bytes 786440 | tf_op jit(solution)/shard_map/ppermute | solution.py:467
  27.3 11.4 %collective-permute-start.5 = (f32[2,4,64,128]{3,2,1,0:T(8,128)S(1)}, f32[2,4,64,128]{3,2,1,0:T(8,128)S(1)}, u32[]{:S(2)}, u32[]{:S(2)}) collective-permute-start(f32[2,4,64,128]{3,2,1,0:T(8,128)S(1)} %get-tuple-element.76), channel_id=1, source_target_pairs={{0,15},{1,2},{2,1},{3,4},{4,3},{5,6},{6,5},{7,8},{8,7},{9,10},{10,... | collective-permute-start | bytes 786440 | tf_op jit(solution)/shard_map/ppermute | solution.py:464
  29.5 8.3 %collective-permute-start.6 = (f32[2,4,16,128]{3,2,1,0:T(8,128)S(1)}, f32[2,4,16,128]{3,2,1,0:T(8,128)S(1)}, u32[]{:S(2)}, u32[]{:S(2)}) collective-permute-start(f32[2,4,16,128]{3,2,1,0:T(8,128)S(1)} %get-tuple-element.77), channel_id=1, source_target_pairs={{0,16},{16,32},{32,48},{48,64},{64,80},{80,96},{96,112},{112,0},{1... | collective-permute-start | bytes 196616 | tf_op jit(solution)/shard_map/ppermute | solution.py:465
  29.5 8.3 %collective-permute-start.7 = (f32[2,4,16,128]{3,2,1,0:T(8,128)S(1)}, f32[2,4,16,128]{3,2,1,0:T(8,128)S(1)}, u32[]{:S(2)}, u32[]{:S(2)}) collective-permute-start(f32[2,4,16,128]{3,2,1,0:T(8,128)S(1)} %get-tuple-element.78), channel_id=1, source_target_pairs={{0,112},{16,0},{32,16},{48,32},{64,48},{80,64},{96,80},{112,96},{1... | collective-permute-start | bytes 196616 | tf_op jit(solution)/shard_map/ppermute | solution.py:466
  39.2 13.5 %collective-permute-start.8 = (f32[2,4,64,128]{3,2,1,0:T(8,128)S(1)}, f32[2,4,64,128]{3,2,1,0:T(8,128)S(1)}, u32[]{:S(2)}, u32[]{:S(2)}) collective-permute-start(f32[2,4,64,128]{3,2,1,0:T(8,128)S(1)} %get-tuple-element.82), channel_id=1, source_target_pairs={{0,1},{1,0},{2,3},{3,2},{4,5},{5,4},{6,7},{7,6},{8,9},{9,8},{10,11... | collective-permute-start | bytes 786440 | tf_op jit(solution)/shard_map/ppermute | solution.py:467
  39.3 13.4 %collective-permute-start.9 = (f32[2,4,64,128]{3,2,1,0:T(8,128)S(1)}, f32[2,4,64,128]{3,2,1,0:T(8,128)S(1)}, u32[]{:S(2)}, u32[]{:S(2)}) collective-permute-start(f32[2,4,64,128]{3,2,1,0:T(8,128)S(1)} %get-tuple-element.83), channel_id=1, source_target_pairs={{0,15},{1,2},{2,1},{3,4},{4,3},{5,6},{6,5},{7,8},{8,7},{9,10},{10,... | collective-permute-start | bytes 786440 | tf_op jit(solution)/shard_map/ppermute | solution.py:464
  41.4 11.3 %collective-permute-start.10 = (f32[2,4,16,128]{3,2,1,0:T(8,128)S(1)}, f32[2,4,16,128]{3,2,1,0:T(8,128)S(1)}, u32[]{:S(2)}, u32[]{:S(2)}) collective-permute-start(f32[2,4,16,128]{3,2,1,0:T(8,128)S(1)} %get-tuple-element.84), channel_id=1, source_target_pairs={{0,16},{16,32},{32,48},{48,64},{64,80},{80,96},{96,112},{112,0},{1... | collective-permute-start | bytes 196616 | tf_op jit(solution)/shard_map/ppermute | solution.py:465
  41.4 11.3 %collective-permute-start.11 = (f32[2,4,16,128]{3,2,1,0:T(8,128)S(1)}, f32[2,4,16,128]{3,2,1,0:T(8,128)S(1)}, u32[]{:S(2)}, u32[]{:S(2)}) collective-permute-start(f32[2,4,16,128]{3,2,1,0:T(8,128)S(1)} %get-tuple-element.85), channel_id=1, source_target_pairs={{0,112},{16,0},{32,16},{48,32},{64,48},{80,64},{96,80},{112,96},{1... | collective-permute-start | bytes 196616 | tf_op jit(solution)/shard_map/ppermute | solution.py:466
  53.3 11.7 %collective-permute-start.12 = (f32[2,4,64,128]{3,2,1,0:T(8,128)S(1)}, f32[2,4,64,128]{3,2,1,0:T(8,128)S(1)}, u32[]{:S(2)}, u32[]{:S(2)}) collective-permute-start(f32[2,4,64,128]{3,2,1,0:T(8,128)S(1)} %get-tuple-element.89), channel_id=1, source_target_pairs={{0,1},{1,0},{2,3},{3,2},{4,5},{5,4},{6,7},{7,6},{8,9},{9,8},{10,11... | collective-permute-start | bytes 786440 | tf_op jit(solution)/shard_map/ppermute | solution.py:467
  53.4 12.0 %collective-permute-start.13 = (f32[2,4,64,128]{3,2,1,0:T(8,128)S(1)}, f32[2,4,64,128]{3,2,1,0:T(8,128)S(1)}, u32[]{:S(2)}, u32[]{:S(2)}) collective-permute-start(f32[2,4,64,128]{3,2,1,0:T(8,128)S(1)} %get-tuple-element.90), channel_id=1, source_target_pairs={{0,15},{1,2},{2,1},{3,4},{4,3},{5,6},{6,5},{7,8},{8,7},{9,10},{10,... | collective-permute-start | bytes 786440 | tf_op jit(solution)/shard_map/ppermute | solution.py:464
  55.0 10.0 %collective-permute-start.14 = (f32[2,4,16,128]{3,2,1,0:T(8,128)S(1)}, f32[2,4,16,128]{3,2,1,0:T(8,128)S(1)}, u32[]{:S(2)}, u32[]{:S(2)}) collective-permute-start(f32[2,4,16,128]{3,2,1,0:T(8,128)S(1)} %get-tuple-element.91), channel_id=1, source_target_pairs={{0,16},{16,32},{32,48},{48,64},{64,80},{80,96},{96,112},{112,0},{1... | collective-permute-start | bytes 196616 | tf_op jit(solution)/shard_map/ppermute | solution.py:465
  55.0 10.0 %collective-permute-start.15 = (f32[2,4,16,128]{3,2,1,0:T(8,128)S(1)}, f32[2,4,16,128]{3,2,1,0:T(8,128)S(1)}, u32[]{:S(2)}, u32[]{:S(2)}) collective-permute-start(f32[2,4,16,128]{3,2,1,0:T(8,128)S(1)} %get-tuple-element.92), channel_id=1, source_target_pairs={{0,112},{16,0},{32,16},{48,32},{64,48},{80,64},{96,80},{112,96},{1... | collective-permute-start | bytes 196616 | tf_op jit(solution)/shard_map/ppermute | solution.py:466
  65.9 11.7 %collective-permute-start.16 = (f32[1,4,64,128]{3,2,1,0:T(8,128)S(1)}, f32[1,4,64,128]{3,2,1,0:T(8,128)S(1)}, u32[]{:S(2)}, u32[]{:S(2)}) collective-permute-start(f32[1,4,64,128]{3,2,1,0:T(8,128)S(1)} %get-tuple-element.99), channel_id=1, source_target_pairs={{0,1},{1,0},{2,3},{3,2},{4,5},{5,4},{6,7},{7,6},{8,9},{9,8},{10,11... | collective-permute-start | bytes 393224 | tf_op jit(solution)/shard_map/ppermute | solution.py:467
  66.0 11.6 %collective-permute-start.17 = (f32[1,4,64,128]{3,2,1,0:T(8,128)S(1)}, f32[1,4,64,128]{3,2,1,0:T(8,128)S(1)}, u32[]{:S(2)}, u32[]{:S(2)}) collective-permute-start(f32[1,4,64,128]{3,2,1,0:T(8,128)S(1)} %get-tuple-element.100), channel_id=1, source_target_pairs={{0,15},{1,2},{2,1},{3,4},{4,3},{5,6},{6,5},{7,8},{8,7},{9,10},{10,... | collective-permute-start | bytes 393224 | tf_op jit(solution)/shard_map/ppermute | solution.py:464
  67.3 10.2 %collective-permute-start.18 = (f32[1,4,16,128]{3,2,1,0:T(8,128)S(1)}, f32[1,4,16,128]{3,2,1,0:T(8,128)S(1)}, u32[]{:S(2)}, u32[]{:S(2)}) collective-permute-start(f32[1,4,16,128]{3,2,1,0:T(8,128)S(1)} %get-tuple-element.101), channel_id=1, source_target_pairs={{0,16},{16,32},{32,48},{48,64},{64,80},{80,96},{96,112},{112,0},{1... | collective-permute-start | bytes 98312 | tf_op jit(solution)/shard_map/ppermute | solution.py:465
  67.3 10.2 %collective-permute-start.19 = (f32[1,4,16,128]{3,2,1,0:T(8,128)S(1)}, f32[1,4,16,128]{3,2,1,0:T(8,128)S(1)}, u32[]{:S(2)}, u32[]{:S(2)}) collective-permute-start(f32[1,4,16,128]{3,2,1,0:T(8,128)S(1)} %get-tuple-element.102), channel_id=1, source_target_pairs={{0,112},{16,0},{32,16},{48,32},{64,48},{80,64},{96,80},{112,96},{1... | collective-permute-start | bytes 98312 | tf_op jit(solution)/shard_map/ppermute | solution.py:466

commit v3 on v2

v3 whole, which is shorter than its diff:
```python
import functools
import math

import jax
import jax.numpy as jnp
from jax import lax
from jax.experimental import pallas as pl
from jax.experimental.pallas import tpu as pltpu
from jax.sharding import PartitionSpec as P

ITERS = 4
time_step = 0.1
force_gain = 0.3

NXL = 64
NYL = 16
NT = 4
PAD = 16
CELLS = NXL * NYL
ROWS = CELLS + 2 * PAD
F32 = jnp.float32
WIDTH = ("width", "thick")
MIB = 1024 * 1024
SHAPE = (NT, 8, 128)
OUTSIDE = 1e30


def sweep_weight(k):
    return 2.0 / (2.15 + 1.75 * math.cos(math.pi * (2 * k + 1) / (2 * ITERS)))


def z_up(a, fill=0.0):
    r = pltpu.roll(a, 127, 2)
    after = jnp.concatenate([r[1:], jnp.full_like(r[:1], fill)], axis=0)
    return jnp.where(lax.broadcasted_iota(jnp.int32, a.shape, 2) == 127, after, r)


def z_down(a):
    r = pltpu.roll(a, 1, 2)
    before = jnp.concatenate([jnp.zeros_like(r[:1]), r[:-1]], axis=0)
    return jnp.where(lax.broadcasted_iota(jnp.int32, a.shape, 2) == 0, before, r)


def recip(d):
    return pltpu.reciprocal(d, approx=True)


def sublanes():
    return lax.broadcasted_iota(jnp.int32, SHAPE, 1)


def row_of(x):
    return pl.multiple_of(PAD + x * NYL, NYL)


def fill_pads(ref, value=0.0):
    lead = (slice(None),) * (len(ref.shape) - 2)
    block = jnp.full(ref.shape[:-2] + (PAD, 128), value, F32)
    ref[lead + (pl.ds(0, PAD),)] = block
    ref[lead + (pl.ds(PAD + CELLS, PAD),)] = block


class Sides:
    def __init__(self, x0=0, planes=NXL):
        thick = lax.axis_index("thick")
        place = lax.axis_index("width") * 2 + thick
        cast = lax.axis_index("cast")
        last = lax.axis_size("width") * 2 - 1
        near = self.near = (NYL - 1) * (1 - thick)
        far = self.far = (NYL - 1) * thick

        def rows(pad):
            start = pad + x0 * NYL
            return (
                pl.ds(start + near, planes, stride=NYL),
                pl.ds(start + far, planes, stride=NYL),
                pl.ds(pad, NYL),
                pl.ds(pad + CELLS - NYL, NYL),
            )

        self.rows = rows(PAD)
        self.inner = rows(0)
        self.dims = (1, 1, 0, 0)
        high = jnp.where(thick == 0, 1.0, -1.0).astype(F32)
        self.signs = (high, -high, -1.0, 1.0)

        def inside(ok):
            return jnp.where(ok, 1.0, 0.0).astype(F32)

        self.masks = (
            1.0,
            inside(((thick == 0) & (place > 0)) | ((thick == 1) & (place < last))),
            inside(cast > 0),
            inside(cast < lax.axis_size("cast") - 1),
        )


CHUNKS = 8


def load_kernel(vel, mag, lab, v, hat, e, vnew, oa, ob, ol, oh, ka, kb, kl, kh, b, lraw, sem):
    per = CELLS // CHUNKS

    def copies(ch):
        src = pl.ds(ch * per, per)
        dst = pl.ds(PAD + ch * per, per)
        for t in range(NT):
            col = pl.ds(128 * t, 128)
            yield pltpu.make_async_copy(vel.at[:, src, col], v.at[:, t, dst], sem.at[ch, t])
            yield pltpu.make_async_copy(mag.at[:, src, col], b.at[:, t, src], sem.at[ch, NT + t])
        yield pltpu.make_async_copy(lab.at[src], lraw.at[src], sem.at[ch, 2 * NT])

    for ch in range(CHUNKS):
        for copy in copies(ch):
            copy.start()
    fill_pads(v)
    fill_pads(e)
    fill_pads(hat, OUTSIDE)
    for ch in range(CHUNKS):
        for copy in copies(ch):
            copy.wait()

        @pl.loop(0, per // 8, unroll=8)
        def _(i):
            raw = pl.ds(pl.multiple_of(ch * per + i * 8, 8), 8)
            at = pl.ds(pl.multiple_of(PAD + ch * per + i * 8, 8), 8)
            for t in range(NT):
                lb = lraw[raw, pl.ds(128 * t, 128)]
                melt, shell = lb == 0, lb == 1
                hat[t, at, :] = jnp.where(melt, 0.5, jnp.where(shell, 0.5 / 0.7, 0.125)).astype(F32)
                gain = jnp.where(melt, 1.0, jnp.where(shell, 0.7, 4.0)).astype(F32) * force_gain
                v0, v1, v2 = (v[c, t, at, :] for c in range(3))
                b0, b1, b2 = (b[c, t, raw, :] for c in range(3))
                e0, e1, e2 = v1 * b2 - v2 * b1, v2 * b0 - v0 * b2, v0 * b1 - v1 * b0
                e[0, t, at, :] = e0
                e[1, t, at, :] = e1
                e[2, t, at, :] = e2
                vnew[0, t, at, :] = gain * (e1 * b2 - e2 * b1)
                vnew[1, t, at, :] = gain * (e2 * b0 - e0 * b2)
                vnew[2, t, at, :] = gain * (e0 * b1 - e1 * b0)

    sides = Sides()
    for out, rows, d in zip((oa, ob, ol, oh), sides.rows, sides.dims):
        out[0] = hat[:, rows, :]
        out[1] = e[d, :, rows, :]
        for c in range(1 if d else 3):
            out[2 + c] = v[c, :, rows, :]

    for i, k in enumerate((ka, kb, kl, kh)):
        rows, at, d = sides.rows[i], sides.inner[i], sides.dims[i]
        n1, n2 = (d + 1) % 3, (d + 2) % 3
        g = (0.25 * force_gain * sides.signs[i]) * (sides.masks[i] * recip(hat[:, rows, :]))
        k[0] = g * b[n2, :, at, :]
        k[1] = -g * b[n1, :, at, :]


def faces(w0, hat, e, f, src, inv, phi):
    zero = jnp.zeros(SHAPE, F32)
    sub = sublanes()

    def body(x, carry):
        fxm, qxm, hc, exc = carry
        r = row_of(x)
        fxo, qxo, hn, exn = [], [], [], []
        for y in range(2):
            base = r + 8 * y
            at, up, down = pl.ds(base, 8), pl.ds(base + 1, 8), pl.ds(base - 1, 8)
            ahead = pl.ds(base + NYL, 8)
            c = hc[y]
            hn.append(hat[:, ahead, :])
            exn.append(e[0, :, ahead, :])
            fx = recip(c + hn[y])
            qx = fx * (exc[y] + exn[y])
            fxo.append(fx)
            qxo.append(qx)
            ey = e[1, :, at, :]
            fy = recip(c + hat[:, up, :])
            fym = recip(c + hat[:, down, :])
            if y == 1:
                fy = jnp.where(sub == 7, 0.0, fy)
            else:
                fym = jnp.where(sub == 0, 0.0, fym)
            fz = recip(c + z_up(c, OUTSIDE))
            ez = e[2, :, at, :]
            qz = fz * (ez + z_up(ez))
            total = (qx - qxm[y]) + (fy * (ey + e[1, :, up, :]) - fym * (ey + e[1, :, down, :])) + (qz - z_down(qz))
            diag = ((fx + fxm[y]) + (fy + fym)) + (fz + z_down(fz)) + 0.025 * recip(c)
            source = 0.5 * total
            inverse = recip(diag)
            f[0, :, at, :] = fx
            f[1, :, at, :] = fy
            f[2, :, at, :] = fz
            src[:, at, :] = source
            inv[:, at, :] = inverse
            phi[:, at, :] = (-w0) * (source * inverse)
        return tuple(fxo), tuple(qxo), tuple(hn), tuple(exn)

    first = [pl.ds(PAD + 8 * y, 8) for y in range(2)]
    start = (
        (zero, zero),
        (zero, zero),
        tuple(hat[:, at, :] for at in first),
        tuple(e[0, :, at, :] for at in first),
    )
    lax.fori_loop(0, NXL, body, start, unroll=8)


def face_kernel(w0, hat, e, v, vnew, f, src, inv, phi):
    del v, vnew
    f[1, :, 0:PAD, :] = jnp.zeros((NT, PAD, 128), F32)
    fill_pads(phi)
    faces(w0, hat, e, f, src, inv, phi)


PHI, BEHIND, SOURCE, INVERSE, FACE_Y, FACE_Z, LINES = range(7)
LOW, HIGH = 0, 1


def put_planes(outs, phi, f):
    for out, edge, behind, face in zip(outs, (0, NXL - 1), (1, NXL - 2), (0, NXL - 2)):
        out[PHI] = phi[:, pl.ds(PAD + edge * NYL, NYL), :]
        out[BEHIND] = f[0, :, pl.ds(PAD + face * NYL, NYL), :] * phi[:, pl.ds(PAD + behind * NYL, NYL), :]


def first_edge_kernel(w0, ha, hb, hl, hh, hat, e, v, f_in, src_in, inv_in, phi_in,
                      f, src, inv, phi, ca, cb, cl, ch, oa, ob, ol, oh):
    del f_in, src_in, inv_in, phi_in
    s = Sides()
    coefs = (ca, cb, cl, ch)
    for pair in ((0, 1), (2, 3)):
        got = []
        for i in pair:
            halo, rows, d = (ha, hb, hl, hh)[i], s.rows[i], s.dims[i]
            g = s.masks[i] * recip(hat[:, rows, :] + halo[0])
            q = (0.5 * s.signs[i]) * (g * (e[d, :, rows, :] + halo[1]))
            got.append((i, rows, g, src[:, rows, :] + q, recip(recip(inv[:, rows, :]) + g)))
        for i, rows, g, source, inverse in got:
            coefs[i][...] = g
            src[:, rows, :] = source
            inv[:, rows, :] = inverse
    f[0, :, pl.ds(0, PAD), :] = cl[...]
    f[0, :, s.rows[3], :] = ch[...]
    got = []
    for i in range(4):
        rows = s.rows[i]
        inverse = inv[:, rows, :]
        got.append((i, rows, coefs[i][...] * inverse, (-w0) * (src[:, rows, :] * inverse)))
    for i, rows, coef, value in got:
        coefs[i][...] = coef
        phi[:, rows, :] = value
    for out, rows in zip((oa, ob), s.rows):
        out[0] = phi[:, rows, :]
        out[1] = v[1, :, rows, :]
    put_planes((ol, oh), phi, f)
    for out, rows, line in zip((ol, oh), s.rows[2:], (0, NXL - 1)):
        out[SOURCE] = src[:, rows, :]
        out[INVERSE] = inv[:, rows, :]
        out[FACE_Y] = f[1, :, rows, :]
        out[FACE_Z] = f[2, :, rows, :]
        out[LINES] = jnp.zeros((NT, NYL, 128), F32)
        for j, coef in enumerate((ca, cb)):
            out[LINES, :, pl.ds(j, 1), :] = coef[:, pl.ds(line, 1), :]


def add_sides(w, phi, coefs, halos, rows):
    got = [phi[:, r, :] + w * (c[...] * h) for c, h, r in zip(coefs, halos, rows)]
    for r, value in zip(rows, got):
        phi[:, r, :] = value


def wide_edge_kernel(w, last, old, f, phi_in, ca, cb, cl, ch, kl, kh, ha, hb, hl, hh, *rest):
    del phi_in
    s = Sides()
    phi, *outs = rest[-3:]
    halves = ((ca, cb), (ha[0], hb[0])), ((cl, ch), (hl[PHI], hh[PHI]))
    for (coefs, halos), rows in zip(halves, (s.rows[:2], s.rows[2:])):
        add_sides(w, phi, coefs, halos, rows)
    beyond = (pl.ds(0, PAD), pl.ds(PAD + CELLS, PAD))
    for side, (k, h) in enumerate(((kl, hl), (kh, hh))):
        c = h[PHI]
        face = f[0, :, beyond[0], :] if side == LOW else f[0, :, s.rows[3], :]
        fy, fz = k[FACE_Y], k[FACE_Z]
        t = face * old[:, s.rows[2 + side], :] + h[BEHIND]
        t = t + fy * pltpu.roll(c, NYL - 1, 1) + pltpu.roll(fy * c, 1, 1)
        t = t + fz * z_up(c) + z_down(fz * c)
        phi[:, beyond[side], :] = s.masks[2 + side] * (c + w * ((t - k[SOURCE]) * k[INVERSE] - c))
    for out, rows, at in zip(outs, s.rows, (s.near, s.far)):
        out[0, :, pl.ds(0, NXL), :] = phi[:, rows, :]
        out[0, :, pl.ds(NXL, 8), :] = jnp.zeros(SHAPE, F32)
        for side, h in enumerate((hl, hh)):
            out[0, :, pl.ds(NXL + side, 1), :] = h[PHI, :, pl.ds(at, 1), :]
        if not last:
            v = rest[0]
            out[1, :, pl.ds(0, NXL), :] = v[2, :, rows, :]
            out[1, :, pl.ds(NXL, 8), :] = jnp.zeros(SHAPE, F32)


def narrow_edge_kernel(w, w_before, f, nu, phi_in, ca, cb, cl, ch, kl, kh, ha, hb, phi, oa, ob, ol, oh):
    del phi_in
    s = Sides()
    inner = pl.ds(0, NXL)
    add_sides(w, phi, (ca, cb), (ha[0, :, inner, :], hb[0, :, inner, :]), s.rows[:2])
    for j, (h, at) in enumerate(((ha, s.near), (hb, s.far))):
        for side, (k, c, plane) in enumerate(((kl, cl, 0), (kh, ch, NXL - 1))):
            missing = w_before * (k[LINES, :, pl.ds(j, 1), :] * h[0, :, pl.ds(NXL + side, 1), :])
            row = pl.ds(PAD + plane * NYL + at, 1)
            phi[:, row, :] = phi[:, row, :] + w * (c[:, pl.ds(at, 1), :] * missing)
    for out, rows in zip((oa, ob), s.rows):
        out[0] = phi[:, rows, :]
        out[1] = nu[:, rows, :]
    put_planes((ol, oh), phi, f)
    for out, rows in zip((ol, oh), s.rows[2:]):
        out[2] = nu[:, rows, :]


def predictor(v, nu, vnew, x0, x1):
    sub = sublanes()
    half = 0.5 * time_step

    @pl.loop(x0, x1, unroll=8)
    def _(x):
        r = row_of(x)
        for y in range(2):
            base = r + 8 * y
            at = pl.ds(base, 8)
            ups = (pl.ds(base + NYL, 8), pl.ds(base + 1, 8))
            downs = (pl.ds(base - NYL, 8), pl.ds(base - 1, 8))
            n = nu[:, at, :]
            vc = [v[c, :, at, :] for c in range(3)]
            coefs = []
            total = None
            for d in range(3):
                above = nu[:, ups[d], :] if d < 2 else z_up(n)
                below = nu[:, downs[d], :] if d < 2 else z_down(n)
                up = (n + above) - vc[d]
                down = (n + below) + vc[d]
                if d == 1 and y == 1:
                    up = jnp.where(sub == 7, 0.0, up)
                if d == 1 and y == 0:
                    down = jnp.where(sub == 0, 0.0, down)
                coefs.append((up, down))
                both = up + down
                total = both if total is None else total + both
            keep = 1.0 - half * total
            for c in range(3):
                acc = None
                for d in range(3):
                    above = v[c, :, ups[d], :] if d < 2 else z_up(vc[c])
                    below = v[c, :, downs[d], :] if d < 2 else z_down(vc[c])
                    term = coefs[d][0] * above + coefs[d][1] * below
                    acc = term if acc is None else acc + term
                vnew[c, :, at, :] = vnew[c, :, at, :] + (half * acc + keep * vc[c])


def sweep_kernel(w, phi, f, src, inv, out):
    fill_pads(out)

    def body(x, carry):
        pxm, pc = carry
        r = row_of(x)
        px, pn = [], []
        for y in range(2):
            base = r + 8 * y
            at, up, down = pl.ds(base, 8), pl.ds(base + 1, 8), pl.ds(base - 1, 8)
            pn.append(phi[:, pl.ds(base + NYL, 8), :])
            fx = f[0, :, at, :]
            c = pc[y]
            px.append(fx * c)
            t = fx * pn[y] + pxm[y]
            t = t + f[1, :, at, :] * phi[:, up, :]
            t = t + f[1, :, down, :] * phi[:, down, :]
            fz = f[2, :, at, :]
            t = t + fz * z_up(c)
            t = t + z_down(fz * c)
            out[:, at, :] = c + w * ((t - src[:, at, :]) * inv[:, at, :] - c)
        return tuple(px), tuple(pn)

    before = tuple(f[0, :, pl.ds(8 * y, 8), :] * phi[:, pl.ds(8 * y, 8), :] for y in range(2))
    start = (before, tuple(phi[:, pl.ds(PAD + 8 * y, 8), :] for y in range(2)))
    lax.fori_loop(0, NXL, body, start, unroll=16)


def sweep_predict_kernel(w, planes, phi, f, src, inv, v, nu, vnew_in, out, vnew):
    del vnew_in
    sweep_kernel(w, phi, f, src, inv, out)
    predictor(v, nu, vnew, *planes)


def sweep_load_kernel(w, planes, phi, f, src, inv, v, visc, vnew_in, out, nu, vnew, sem):
    del vnew_in
    copies = [
        pltpu.make_async_copy(visc.at[:, pl.ds(128 * t, 128)], nu.at[t, pl.ds(PAD, CELLS)], sem.at[t])
        for t in range(NT)
    ]
    for copy in copies:
        copy.start()
    fill_pads(nu)
    sweep_kernel(w, phi, f, src, inv, out)
    for copy in copies:
        copy.wait()
    predictor(v, nu, vnew, *planes)


def force_kernel(phi, hat, b, v, nu, *rest):
    flows = [rest[0:4], rest[4:6], rest[6:8], rest[8:12]]
    potential, vnew, sem = rest[13:]
    copies = [
        pltpu.make_async_copy(phi.at[t, pl.ds(PAD, CELLS)], potential.at[:, pl.ds(128 * t, 128)], sem.at[t])
        for t in range(NT)
    ]
    for copy in copies:
        copy.start()

    s = Sides()
    half = 0.5 * time_step
    inner = pl.ds(0, NXL)
    for pair in ((0, 1), (2, 3)):
        got = []
        for i in pair:
            rows, d, sign, mask = s.rows[i], s.dims[i], s.signs[i], s.masks[i]
            if d:
                other = [flows[0][i][2], flows[1][i][1], flows[2][i][1, :, inner, :]]
                hn = mask * flows[3][i][1]
            else:
                other = [flows[0][i][2 + c] for c in range(3)]
                hn = mask * flows[3][i][2]
            vc = [v[c, :, rows, :] for c in range(3)]
            coef = half * ((nu[:, rows, :] + hn) - sign * vc[d])
            gone = half * hn if d == 0 else coef
            got.append([vnew[c, :, rows, :] + (coef * (mask * other[c]) - gone * vc[c]) for c in range(3)])
        for i, values in zip(pair, got):
            for c in range(3):
                vnew[c, :, s.rows[i], :] = values[c]

    sub = sublanes()
    @pl.loop(0, NXL, unroll=8)
    def _(x):
        r = row_of(x)
        for y in range(2):
            base = r + 8 * y
            at = pl.ds(base, 8)
            raw = pl.ds(pl.multiple_of(x * NYL + 8 * y, 8), 8)
            p = phi[:, at, :]
            yu = phi[:, pl.ds(base + 1, 8), :]
            yd = phi[:, pl.ds(base - 1, 8), :]
            if y == 1:
                yu = jnp.where(sub == 7, 0.0, yu)
            else:
                yd = jnp.where(sub == 0, 0.0, yd)
            diffs = (
                phi[:, pl.ds(base + NYL, 8), :] - phi[:, pl.ds(base - NYL, 8), :],
                yu - yd,
                z_up(p) - z_down(p),
            )
            g = (-0.25 * force_gain) * recip(hat[:, at, :])
            c0, c1, c2 = (g * diff for diff in diffs)
            for t in range(NT):
                b0, b1, b2 = (b[c, raw, pl.ds(128 * t, 128)] for c in range(3))
                vnew[0, t, at, :] = vnew[0, t, at, :] + (c1[t] * b2 - c2[t] * b1)
                vnew[1, t, at, :] = vnew[1, t, at, :] + (c2[t] * b0 - c0[t] * b2)
                vnew[2, t, at, :] = vnew[2, t, at, :] + (c0[t] * b1 - c1[t] * b0)

    for copy in copies:
        copy.wait()


PARTS = 4


def last_kernel(w, ka, kb, kl, kh, cl, ch, ha, hb, vnew_in, result, vnew, sem):
    del vnew_in
    planes = NXL // PARTS
    copies = []
    for part in range(PARTS):
        s = Sides(part * planes, planes)
        some = pl.ds(part * planes, planes)
        got = []
        for k, h, rows in ((ka, ha, s.rows[0]), (kb, hb, s.rows[1])):
            halo = h[0, :, some, :]
            got += [(c, rows, vnew[c, :, rows, :] + k[j, :, some, :] * halo) for j, c in enumerate((2, 0))]
        for c, rows, value in got:
            vnew[c, :, rows, :] = value
        corners = ([(kl, cl, LOW, 0)] if part == 0 else []) + ([(kh, ch, HIGH, NXL - 1)] if part == PARTS - 1 else [])
        for k, lines, side, plane in corners:
            for j, (h, at) in enumerate(((ha, s.near), (hb, s.far))):
                missing = w * (lines[LINES, :, pl.ds(j, 1), :] * h[0, :, pl.ds(NXL + side, 1), :])
                row = pl.ds(PAD + plane * NYL + at, 1)
                for i, c in enumerate((1, 2)):
                    vnew[c, :, row, :] = vnew[c, :, row, :] + k[i, :, pl.ds(at, 1), :] * missing
        per = planes * NYL
        for t in range(NT):
            copy = pltpu.make_async_copy(
                vnew.at[:, t, pl.ds(PAD + part * per, per)],
                result.at[:, pl.ds(part * per, per), pl.ds(128 * t, 128)],
                sem.at[part, t],
            )
            copy.start()
            copies.append(copy)
    for copy in copies:
        copy.wait()


def resident(*shape):
    return pltpu.VMEM(shape, F32)


def in_vmem(x):
    return pltpu.with_memory_space_constraint(x, pltpu.VMEM)


def in_hbm(x):
    return pltpu.with_memory_space_constraint(x, pltpu.HBM)


IN_VMEM = pl.BlockSpec(memory_space=pltpu.VMEM)
IN_HBM = pl.BlockSpec(memory_space=pl.ANY)

FIELD = (NT, ROWS, 128)


def run(kernel, name, ins, outs, aliases=None, scratch=(), flops=0, moved=0, limit=6 * MIB):
    args = [in_hbm(a) if hbm else in_vmem(a) for a, hbm in ins]
    return pl.pallas_call(
        kernel,
        out_shape=outs,
        in_specs=[IN_HBM if hbm else IN_VMEM for _, hbm in ins],
        out_specs=[IN_HBM if isinstance(o, jax.ShapeDtypeStruct) else IN_VMEM for o in outs],
        input_output_aliases=aliases or {},
        scratch_shapes=list(scratch),
        compiler_params=pltpu.CompilerParams(vmem_limit_bytes=limit),
        cost_estimate=pl.CostEstimate(flops=flops, bytes_accessed=moved, transcendentals=0),
        name=name,
    )(*args)


def vm(*arrays):
    return [(a, False) for a in arrays]


def ring(axis, step):
    n = lax.axis_size(axis)
    return [(i, (i + step) % n) for i in range(n)]


def across(a, b):
    n = lax.axis_size("width") * 2
    return (
        lax.ppermute(a, "thick", [(0, 1), (1, 0)]),
        lax.ppermute(b, WIDTH, [(i, (((i + 1) ^ 1) - 1) % n) for i in range(n)]),
    )


def along(low, high):
    return lax.ppermute(high, "cast", ring("cast", 1)), lax.ppermute(low, "cast", ring("cast", -1))


def rows_of(n, planes=NXL):
    return [resident(n, NT, planes, 128)] * 2


def planes_of(n):
    return [resident(n, NT, NYL, 128)] * 2


def local(velocity, magnetic, labels, viscosity):
    vel = velocity.reshape(3, CELLS, NT * 128)
    mag = magnetic.reshape(3, CELLS, NT * 128)
    lab = labels.reshape(CELLS, NT * 128)
    visc = viscosity.reshape(CELLS, NT * 128)
    dma = pltpu.SemaphoreType.DMA
    w = [sweep_weight(k) for k in range(ITERS)]
    field, fields = resident(*FIELD), resident(3, *FIELD)
    work = dict(flops=10_000_000, moved=16 * MIB)

    v, hat, e, vnew, *edges = run(
        load_kernel, "load", [(vel, True), (mag, True), (lab, True)],
        [fields, field, fields, fields] + rows_of(3) + planes_of(5) + rows_of(2) + planes_of(2),
        scratch=[
            pltpu.VMEM((3, NT, CELLS, 128), F32),
            pltpu.VMEM((CELLS, NT * 128), jnp.int32),
            dma((CHUNKS, 2 * NT + 1)),
        ],
        limit=10 * MIB,
    )
    edges, products = edges[:4], edges[4:]
    h1 = (*across(*edges[:2]), *along(*edges[2:]))
    f, src, inv, phi = run(
        functools.partial(face_kernel, w[0]), "faces", vm(hat, e, v, vnew), [fields, field, field, field], **work
    )
    f, src, inv, phi, *rest = run(
        functools.partial(first_edge_kernel, w[0]), "edges1", vm(*h1, hat, e, v, f, src, inv, phi),
        [fields] + [field] * 3 + [resident(NT, NXL, 128)] * 2 + [resident(NT, NYL, 128)] * 2 + rows_of(2) + planes_of(7),
        aliases={7: 0, 8: 1, 9: 2, 10: 3},
    )
    coefs, edges = rest[:4], rest[4:]

    h2 = (*across(*edges[:2]), *along(*edges[2:]))
    lines = h2[2:]
    old = phi
    phi, nu, vnew = run(
        functools.partial(sweep_load_kernel, w[1], (0, 32)), "sweep1",
        vm(phi, f, src, inv, v) + [(visc, True)] + vm(vnew),
        [field, field, fields], aliases={6: 2}, scratch=[dma((NT,))], **work,
    )
    phi, *edges = run(
        functools.partial(wide_edge_kernel, w[1], False), "edges2", vm(old, f, phi, *coefs, *lines, *h2, v),
        [field] + rows_of(2, NXL + 8), aliases={2: 0},
    )

    h3 = across(*edges)
    phi, vnew = run(
        functools.partial(sweep_predict_kernel, w[2], (32, 64)), "sweep2", vm(phi, f, src, inv, v, nu, vnew),
        [field, fields], aliases={6: 1}, **work,
    )
    phi, *edges = run(
        functools.partial(narrow_edge_kernel, w[2], w[1]), "edges3", vm(f, nu, phi, *coefs, *lines, *h3),
        [field] + rows_of(2) + planes_of(3), aliases={2: 0},
    )

    h4 = (*across(*edges[:2]), *along(*edges[2:]))
    old = phi
    (phi,) = run(functools.partial(sweep_kernel, w[3]), "sweep3", vm(phi, f, src, inv), [field], **work)
    phi, *edges = run(
        functools.partial(wide_edge_kernel, w[3], True), "edges4", vm(old, f, phi, *coefs, *lines, *h4),
        [field] + rows_of(1, NXL + 8), aliases={2: 0},
    )

    h5 = across(*edges)
    potential, vnew = run(
        force_kernel, "force", vm(phi, hat, mag, v, nu, *h1, *h2[:2], *h3, *h4, vnew),
        [jax.ShapeDtypeStruct((CELLS, NT * 128), F32), fields],
        aliases={17: 1}, scratch=[dma((NT,))], **work,
    )
    result, _ = run(
        functools.partial(last_kernel, w[3]), "last", vm(*products, *lines, *h5, vnew),
        [jax.ShapeDtypeStruct((3, CELLS, NT * 128), F32), fields],
        aliases={8: 1}, scratch=[dma((PARTS, NT))],
    )
    return result.reshape(velocity.shape), potential.reshape(labels.shape)


def solution(mesh):
    fields = P(None, "cast", WIDTH, None)
    scalar = P("cast", WIDTH, None)
    return jax.shard_map(
        local,
        mesh=mesh,
        in_specs=(fields, fields, scalar, scalar),
        out_specs=(fields, scalar),
        check_vma=False,
    )
```

time: 81.7 us -> 85.1 us (1.042); the launches traced: 80.7 us -> 85 us
  waiting for transfers between devices: 9.18 us -> 20.3 us
  starting transfers between devices: 35.8 us -> 28.8 us
    ppermute x20 -> x16, waiting for transfers between devices: 9.18 us -> 20.3 us  [the longest x3 11.8 us: along(): lax.ppermute(high, 'cast', ring('cast', 1))]
    ppermute x20 -> x16, starting transfers between devices: 35.8 us -> 28.8 us  [the longest x5 14.4 us: across(): lax.ppermute(b, WIDTH, [(i, ((i + 1 ^ 1) - 1) % n) for i in range(n)])]
  transfers between devices with their start and end apart: 20 -> 16, of which waited for: 6 -> 5; matrix products, arithmetic and copies ran while one was open for 0% -> 0% of each run, Pallas kernels for 28% -> 25%
where the time goes in v3:
time: 85.1 us; the launch traced here: 85 us
  Pallas kernels  35 us (41%)
  starting transfers between devices  28.8 us (34%)
  waiting for transfers between devices  20.3 us (24%)
  between operations  0.95 us (1%)
    pallas_call x11, Pallas kernels, run(): pl.pallas_call(kernel, out_shape=outs, in_specs=[IN_HBM if hbm else IN_VM...  35 us
    ppermute x5, starting transfers between devices, across(): lax.ppermute(b, WIDTH, [(i, ((i + 1 ^ 1) - 1) % n) for i in range(n)])  14.4 us
    ppermute x3, starting transfers between devices, along(): lax.ppermute(low, 'cast', ring('cast', -1))  12 us
    ppermute x3, waiting for transfers between devices, along(): lax.ppermute(high, 'cast', ring('cast', 1))  11.8 us
    ppermute x5, waiting for transfers between devices, across(): lax.ppermute(b, WIDTH, [(i, ((i + 1 ^ 1) - 1) % n) for i in range(n)])  8.45 us
    ppermute x3, starting transfers between devices, along(): lax.ppermute(high, 'cast', ring('cast', 1))  1.92 us
  transfers between devices with their start and end apart: 16, of which 5 were waited for; matrix products, arithmetic and copies ran while one was open for 0% of the time, Pallas kernels for 25%

profile of v3, /device:TPU:2, one launch (start us, length us, event | category | flops | bytes accessed | tf_op | source)
XLA Modules:
  0.0 85.0 jit_solution(11274792919191342131)
XLA Ops:
  0.6 7.3 %load.1 = (f32[3,4,1056,128]{3,2,1,0:T(8,128)S(1)}, f32[4,1056,128]{2,1,0:T(8,128)S(1)}, f32[3,4,1056,128]{3,2,1,0:T(8,128)S(1)}, f32[3,4,1056,128]{3,2,1,0:T(8,...) custom-call(f32[3,1024,512]{2,1,0:T(8,128)} %bitcast.10, ...), custom_call_target="tpu_custom_call" | custom-call | tf_op jit(solution)/shard_map/load/pallas_call | solution.py:523
  7.9 0.1 collective-permute-start
  8.0 4.7 %collective-permute-start.1 = (f32[3,4,64,128]{3,2,1,0:T(8,128)S(1)}, f32[3,4,64,128]{3,2,1,0:T(8,128)S(1)}, u32[]{:S(2)}, u32[]{:S(2)}) collective-permute-start(f32[3,4,64,128]{3,2,1,0:T(8,128)S(1)} %get-tuple-element.54), channel_id=1, source_target_pairs={{0,15},{1,2},{2,1},{3,4},{4,3},{5,6},{6,5},{7,8},{8,7},{9,10},{10,... | collective-permute-start | bytes 1179656 | tf_op jit(solution)/shard_map/ppermute | solution.py:549
  12.7 1.9 %collective-permute-start.2 = (f32[5,4,16,128]{3,2,1,0:T(8,128)S(1)}, f32[5,4,16,128]{3,2,1,0:T(8,128)S(1)}, u32[]{:S(2)}, u32[]{:S(2)}) collective-permute-start(f32[5,4,16,128]{3,2,1,0:T(8,128)S(1)} %get-tuple-element.55), channel_id=1, source_target_pairs={{0,16},{16,32},{32,48},{48,64},{64,80},{80,96},{96,112},{112,0},{1... | collective-permute-start | bytes 491528 | tf_op jit(solution)/shard_map/ppermute | solution.py:554
  14.6 3.0 %collective-permute-start.3 = (f32[5,4,16,128]{3,2,1,0:T(8,128)S(1)}, f32[5,4,16,128]{3,2,1,0:T(8,128)S(1)}, u32[]{:S(2)}, u32[]{:S(2)}) collective-permute-start(f32[5,4,16,128]{3,2,1,0:T(8,128)S(1)} %get-tuple-element.56), channel_id=1, source_target_pairs={{0,112},{16,0},{32,16},{48,32},{64,48},{80,64},{96,80},{112,96},{1... | collective-permute-start | bytes 491528 | tf_op jit(solution)/shard_map/ppermute | solution.py:554
  17.6 6.7 %faces.1 = (f32[3,4,1056,128]{3,2,1,0:T(8,128)S(1)}, f32[4,1056,128]{2,1,0:T(8,128)S(1)}, f32[4,1056,128]{2,1,0:T(8,128)S(1)}, f32[4,1056,128]{2,1,0:T(8,128)S(1)}) custom-call(f32[4,1056,128]{2,1,0:T(8,128)S(1)} %get-tuple-element.57.hat, f32[3,4,1056,128]{3,2,1,0:T(8,128)S(1)} %get-tuple-element.58.e, f32[3,4,1056,128]{3,2,1,0:T(8,128)S(1)} %get-tuple-element.59.v.rest_0_, ...), custom_call_target="tpu_custom_call" | custom-call | flops 10000000 | bytes 16777216 | tf_op jit(solution)/shard_map/faces/pallas_call | solution.py:523
  24.3 3.7 %collective-permute-done.2.hl.rest_2_ = f32[5,4,16,128]{3,2,1,0:T(8,128)S(1)} collective-permute-done((f32[5,4,16,128]{3,2,1,0:T(8,128)S(1)}, f32[5,4,16,128]{3,2,1,0:T(8,128)S(1)}, u32[]{:S(2)}, u32[]{:S(2)}) %collective-permute-start.2) | collective-permute-done | bytes 163872 | tf_op jit(solution)/shard_map/ppermute | solution.py:554
  28.0 0.0 collective-permute-done.3.hh.rest_3_
  28.0 1.6 %edges1.1 = (f32[3,4,1056,128]{3,2,1,0:T(8,128)S(1)}, f32[4,1056,128]{2,1,0:T(8,128)S(1)}, f32[4,1056,128]{2,1,0:T(8,128)S(1)}, f32[4,1056,128]{2,1,0:T(8,128)S(...) custom-call(f32[3,4,64,128]{3,2,1,0:T(8,128)S(1)} %collective-permut, ...), custom_call_target="tpu_custom_call", output_to_operand_aliasing={{0}: (7, {}), {1}: (8, {}), {2}: (9, {}), {3}: (10, {})} | custom-call | tf_op jit(solution)/shard_map/edges1/pallas_call | solution.py:523
  29.7 0.1 collective-permute-start.6
  29.8 2.3 %collective-permute-start.7 = (f32[2,4,64,128]{3,2,1,0:T(8,128)S(1)}, f32[2,4,64,128]{3,2,1,0:T(8,128)S(1)}, u32[]{:S(2)}, u32[]{:S(2)}) collective-permute-start(f32[2,4,64,128]{3,2,1,0:T(8,128)S(1)} %get-tuple-element.78), channel_id=1, source_target_pairs={{0,15},{1,2},{2,1},{3,4},{4,3},{5,6},{6,5},{7,8},{8,7},{9,10},{10,... | collective-permute-start | bytes 786440 | tf_op jit(solution)/shard_map/ppermute | solution.py:549
  32.0 0.0 collective-permute-start.4
  32.0 4.1 %collective-permute-start.5 = (f32[7,4,16,128]{3,2,1,0:T(8,128)S(1)}, f32[7,4,16,128]{3,2,1,0:T(8,128)S(1)}, u32[]{:S(2)}, u32[]{:S(2)}) collective-permute-start(f32[7,4,16,128]{3,2,1,0:T(8,128)S(1)} %get-tuple-element.66), channel_id=1, source_target_pairs={{0,112},{16,0},{32,16},{48,32},{64,48},{80,64},{96,80},{112,96},{1... | collective-permute-start | bytes 688136 | tf_op jit(solution)/shard_map/ppermute | solution.py:554
  36.2 4.6 %sweep1.1 = (f32[4,1056,128]{2,1,0:T(8,128)S(1)}, f32[4,1056,128]{2,1,0:T(8,128)S(1)}, f32[3,4,1056,128]{3,2,1,0:T(8,128)S(1)}) custom-call(f32[4,1056,128]{2,1,0:T(8,128)S(1)} %get-tuple-element.68.phi.old, f32[3,4,1056,128]{3,2,1,0:T(8,128)S(1)} %get-tuple-element.67.f, ...), custom_call_target="tpu_custom_call", output_to_operand_aliasing={{2}: (6, {})} | custom-call | flops 10000000 | bytes 16777216 | tf_op jit(solution)/shard_map/sweep1/pallas_call | solution.py:523
  40.8 2.1 %collective-permute-done.4.kl.hl.cl = f32[7,4,16,128]{3,2,1,0:T(8,128)S(1)} collective-permute-done((f32[7,4,16,128]{3,2,1,0:T(8,128)S(1)}, f32[7,4,16,128]{3,2,1,0:T(8,128)S(1)}, u32[]{:S(2)}, u32[]{:S(2)}) %collective-permute-start.4) | collective-permute-done | bytes 229408 | tf_op jit(solution)/shard_map/ppermute | solution.py:554
  42.9 0.6 edges2.1
  43.6 0.1 collective-permute-start.8
  43.7 3.7 %collective-permute-start.9 = (f32[2,4,72,128]{3,2,1,0:T(8,128)S(1)}, f32[2,4,72,128]{3,2,1,0:T(8,128)S(1)}, u32[]{:S(2)}, u32[]{:S(2)}) collective-permute-start(f32[2,4,72,128]{3,2,1,0:T(8,128)S(1)} %get-tuple-element.83), channel_id=1, source_target_pairs={{0,15},{1,2},{2,1},{3,4},{4,3},{5,6},{6,5},{7,8},{8,7},{9,10},{10,... | collective-permute-start | bytes 884744 | tf_op jit(solution)/shard_map/ppermute | solution.py:549
  47.4 4.6 %sweep2.1 = (f32[4,1056,128]{2,1,0:T(8,128)S(1)}, f32[3,4,1056,128]{3,2,1,0:T(8,128)S(1)}) custom-call(f32[4,1056,128]{2,1,0:T(8,128)S(1)} %get-tuple-element.79.phi, f32[3,4,1056,128]{3,2,1,0:T(8,128)S(1)} %get-tuple-element.67.f, f32[4,1056,128]{2,1,0:T(8,128)S(1)} %get-tuple-element.69.src, ...), custom_call_target="tpu_custom_call", output_to_operand_aliasing={{1}: (6, {})} | custom-call | flops 10000000 | bytes 16777216 | tf_op jit(solution)/shard_map/sweep2/pallas_call | solution.py:523
  52.0 4.2 %collective-permute-done.9.hb.rest_7_ = f32[2,4,72,128]{3,2,1,0:T(8,128)S(1)} collective-permute-done((f32[2,4,72,128]{3,2,1,0:T(8,128)S(1)}, f32[2,4,72,128]{3,2,1,0:T(8,128)S(1)}, u32[]{:S(2)}, u32[]{:S(2)}) %collective-permute-start.9) | collective-permute-done | bytes 294944 | tf_op jit(solution)/shard_map/ppermute | solution.py:549
  56.2 0.6 edges3.1
  56.9 0.1 collective-permute-start.10
  56.9 2.3 %collective-permute-start.11 = (f32[2,4,64,128]{3,2,1,0:T(8,128)S(1)}, f32[2,4,64,128]{3,2,1,0:T(8,128)S(1)}, u32[]{:S(2)}, u32[]{:S(2)}) collective-permute-start(f32[2,4,64,128]{3,2,1,0:T(8,128)S(1)} %get-tuple-element.86), channel_id=1, source_target_pairs={{0,15},{1,2},{2,1},{3,4},{4,3},{5,6},{6,5},{7,8},{8,7},{9,10},{10,... | collective-permute-start | bytes 786440 | tf_op jit(solution)/shard_map/ppermute | solution.py:549
  59.2 4.9 %collective-permute-start.13 = (f32[3,4,16,128]{3,2,1,0:T(8,128)S(1)}, f32[3,4,16,128]{3,2,1,0:T(8,128)S(1)}, u32[]{:S(2)}, u32[]{:S(2)}) collective-permute-start(f32[3,4,16,128]{3,2,1,0:T(8,128)S(1)} %get-tuple-element.88), channel_id=1, source_target_pairs={{0,112},{16,0},{32,16},{48,32},{64,48},{80,64},{96,80},{112,96},{1... | collective-permute-start | bytes 294920 | tf_op jit(solution)/shard_map/ppermute | solution.py:554
  64.2 1.8 %sweep3.1.phi_in = f32[4,1056,128]{2,1,0:T(8,128)S(1)} custom-call(f32[4,1056,128]{2,1,0:T(8,128)S(1)} %get-tuple-element.84.phi.old, f32[3,4,1056,128]{3,2,1,0:T(8,128)S(1)} %get-tuple-element.67.f, f32[4,1056,128]{2,1,0:T(8,128)S(1)} %get-tuple-element.69.src, f32[4,1056,128]{2,1,0:T(8,128)S(1)} %get-tuple-element.70.inv), custom_call_target="tpu_custom_call" | custom-call | flops 10000000 | bytes 16777216 | tf_op jit(solution)/shard_map/sweep3/pallas_call | solution.py:523
  65.9 5.9 %collective-permute-done.12.hl.rest_10_ = f32[3,4,16,128]{3,2,1,0:T(8,128)S(1)} collective-permute-done((f32[3,4,16,128]{3,2,1,0:T(8,128)S(1)}, f32[3,4,16,128]{3,2,1,0:T(8,128)S(1)}, u32[]{:S(2)}, u32[]{:S(2)}) %collective-permute-start.12) | collective-permute-done | bytes 98336 | tf_op jit(solution)/shard_map/ppermute | solution.py:554
  71.9 0.5 edges4.1
  72.4 0.1 collective-permute-start.14
  72.5 1.5 %collective-permute-start.15 = (f32[1,4,72,128]{3,2,1,0:T(8,128)S(1)}, f32[1,4,72,128]{3,2,1,0:T(8,128)S(1)}, u32[]{:S(2)}, u32[]{:S(2)}) collective-permute-start(f32[1,4,72,128]{3,2,1,0:T(8,128)S(1)} %get-tuple-element.90), channel_id=1, source_target_pairs={{0,15},{1,2},{2,1},{3,4},{4,3},{5,6},{6,5},{7,8},{8,7},{9,10},{10,... | collective-permute-start | bytes 442376 | tf_op jit(solution)/shard_map/ppermute | solution.py:549
  74.0 3.7 %force.1 = (f32[1024,512]{1,0:T(8,128)}, f32[3,4,1056,128]{3,2,1,0:T(8,128)S(1)}) custom-call(f32[4,1056,128]{2,1,0:T(8,128)S(1)} %get-tuple-element.91.phi, f32[4,1056,128]{2,1,0:T(8,128)S(1)} %get-tuple-element.57.hat, f32[3,1024,512]{2,1,0:T(8,128)S(1)} %bitcast.9, ...), custom_call_target="tpu_custom_call", output_to_operand_aliasing={{1}: (17, {})} | custom-call | flops 10000000 | bytes 16777216 | tf_op jit(solution)/shard_map/force/pallas_call | solution.py:523
  77.7 4.2 %collective-permute-done.15.hb = f32[1,4,72,128]{3,2,1,0:T(8,128)S(1)} collective-permute-done((f32[1,4,72,128]{3,2,1,0:T(8,128)S(1)}, f32[1,4,72,128]{3,2,1,0:T(8,128)S(1)}, u32[]{:S(2)}, u32[]{:S(2)}) %collective-permute-start.15) | collective-permute-done | bytes 147488 | tf_op jit(solution)/shard_map/ppermute | solution.py:549
  81.9 2.9 %last.1 = (f32[3,1024,512]{2,1,0:T(8,128)}, f32[3,4,1056,128]{3,2,1,0:T(8,128)S(1)}) custom-call(f32[2,4,64,128]{3,2,1,0:T(8,128)S(1)} %get-tuple-element.49.ka, f32[2,4,64,128]{3,2,1,0:T(8,128)S(1)} %get-tuple-element.50.kb, f32[2,4,16,128]{3,2,1,0:T(8,128)S(1)} %get-tuple-element.51.kl, ...), custom_call_target="tpu_custom_call", output_to_operand_aliasing={{1}: (8, {})} | custom-call | tf_op jit(solution)/shard_map/last/pallas_call | solution.py:523
  (16 shorter events, 0.0 us)
Async XLA Ops:
  7.9 20.1 %collective-permute-start = (f32[3,4,64,128]{3,2,1,0:T(8,128)S(1)}, f32[3,4,64,128]{3,2,1,0:T(8,128)S(1)}, u32[]{:S(2)}, u32[]{:S(2)}) collective-permute-start(f32[3,4,64,128]{3,2,1,0:T(8,128)S(1)} %get-tuple-element.53), channel_id=1, source_target_pairs={{0,1},{1,0},{2,3},{3,2},{4,5},{5,4},{6,7},{7,6},{8,9},{9,8},{10,11... | collective-permute-start | bytes 1179656 | tf_op jit(solution)/shard_map/ppermute | solution.py:548
  8.0 20.0 %collective-permute-start.1 = (f32[3,4,64,128]{3,2,1,0:T(8,128)S(1)}, f32[3,4,64,128]{3,2,1,0:T(8,128)S(1)}, u32[]{:S(2)}, u32[]{:S(2)}) collective-permute-start(f32[3,4,64,128]{3,2,1,0:T(8,128)S(1)} %get-tuple-element.54), channel_id=1, source_target_pairs={{0,15},{1,2},{2,1},{3,4},{4,3},{5,6},{6,5},{7,8},{8,7},{9,10},{10,... | collective-permute-start | bytes 1179656 | tf_op jit(solution)/shard_map/ppermute | solution.py:549
  12.7 15.3 %collective-permute-start.2 = (f32[5,4,16,128]{3,2,1,0:T(8,128)S(1)}, f32[5,4,16,128]{3,2,1,0:T(8,128)S(1)}, u32[]{:S(2)}, u32[]{:S(2)}) collective-permute-start(f32[5,4,16,128]{3,2,1,0:T(8,128)S(1)} %get-tuple-element.55), channel_id=1, source_target_pairs={{0,16},{16,32},{32,48},{48,64},{64,80},{80,96},{96,112},{112,0},{1... | collective-permute-start | bytes 491528 | tf_op jit(solution)/shard_map/ppermute | solution.py:554
  14.6 13.4 %collective-permute-start.3 = (f32[5,4,16,128]{3,2,1,0:T(8,128)S(1)}, f32[5,4,16,128]{3,2,1,0:T(8,128)S(1)}, u32[]{:S(2)}, u32[]{:S(2)}) collective-permute-start(f32[5,4,16,128]{3,2,1,0:T(8,128)S(1)} %get-tuple-element.56), channel_id=1, source_target_pairs={{0,112},{16,0},{32,16},{48,32},{64,48},{80,64},{96,80},{112,96},{1... | collective-permute-start | bytes 491528 | tf_op jit(solution)/shard_map/ppermute | solution.py:554
  29.7 13.2 %collective-permute-start.6 = (f32[2,4,64,128]{3,2,1,0:T(8,128)S(1)}, f32[2,4,64,128]{3,2,1,0:T(8,128)S(1)}, u32[]{:S(2)}, u32[]{:S(2)}) collective-permute-start(f32[2,4,64,128]{3,2,1,0:T(8,128)S(1)} %get-tuple-element.77), channel_id=1, source_target_pairs={{0,1},{1,0},{2,3},{3,2},{4,5},{5,4},{6,7},{7,6},{8,9},{9,8},{10,11... | collective-permute-start | bytes 786440 | tf_op jit(solution)/shard_map/ppermute | solution.py:548
  29.8 13.2 %collective-permute-start.7 = (f32[2,4,64,128]{3,2,1,0:T(8,128)S(1)}, f32[2,4,64,128]{3,2,1,0:T(8,128)S(1)}, u32[]{:S(2)}, u32[]{:S(2)}) collective-permute-start(f32[2,4,64,128]{3,2,1,0:T(8,128)S(1)} %get-tuple-element.78), channel_id=1, source_target_pairs={{0,15},{1,2},{2,1},{3,4},{4,3},{5,6},{6,5},{7,8},{8,7},{9,10},{10,... | collective-permute-start | bytes 786440 | tf_op jit(solution)/shard_map/ppermute | solution.py:549
  32.0 10.9 %collective-permute-start.4 = (f32[7,4,16,128]{3,2,1,0:T(8,128)S(1)}, f32[7,4,16,128]{3,2,1,0:T(8,128)S(1)}, u32[]{:S(2)}, u32[]{:S(2)}) collective-permute-start(f32[7,4,16,128]{3,2,1,0:T(8,128)S(1)} %get-tuple-element.65), channel_id=1, source_target_pairs={{0,16},{16,32},{32,48},{48,64},{64,80},{80,96},{96,112},{112,0},{1... | collective-permute-start | bytes 688136 | tf_op jit(solution)/shard_map/ppermute | solution.py:554
  32.0 10.9 %collective-permute-start.5 = (f32[7,4,16,128]{3,2,1,0:T(8,128)S(1)}, f32[7,4,16,128]{3,2,1,0:T(8,128)S(1)}, u32[]{:S(2)}, u32[]{:S(2)}) collective-permute-start(f32[7,4,16,128]{3,2,1,0:T(8,128)S(1)} %get-tuple-element.66), channel_id=1, source_target_pairs={{0,112},{16,0},{32,16},{48,32},{64,48},{80,64},{96,80},{112,96},{1... | collective-permute-start | bytes 688136 | tf_op jit(solution)/shard_map/ppermute | solution.py:554
  43.6 8.4 %collective-permute-start.8 = (f32[2,4,72,128]{3,2,1,0:T(8,128)S(1)}, f32[2,4,72,128]{3,2,1,0:T(8,128)S(1)}, u32[]{:S(2)}, u32[]{:S(2)}) collective-permute-start(f32[2,4,72,128]{3,2,1,0:T(8,128)S(1)} %get-tuple-element.82), channel_id=1, source_target_pairs={{0,1},{1,0},{2,3},{3,2},{4,5},{5,4},{6,7},{7,6},{8,9},{9,8},{10,11... | collective-permute-start | bytes 884744 | tf_op jit(solution)/shard_map/ppermute | solution.py:548
  43.7 12.5 %collective-permute-start.9 = (f32[2,4,72,128]{3,2,1,0:T(8,128)S(1)}, f32[2,4,72,128]{3,2,1,0:T(8,128)S(1)}, u32[]{:S(2)}, u32[]{:S(2)}) collective-permute-start(f32[2,4,72,128]{3,2,1,0:T(8,128)S(1)} %get-tuple-element.83), channel_id=1, source_target_pairs={{0,15},{1,2},{2,1},{3,4},{4,3},{5,6},{6,5},{7,8},{8,7},{9,10},{10,... | collective-permute-start | bytes 884744 | tf_op jit(solution)/shard_map/ppermute | solution.py:549
  56.2 17.8 %slice-start = ((s8[6291456]{0:T(1024)(128)(4,1)}), s8[4194304]{0:T(1024)(128)(4,1)S(1)}, s32[]{:S(2)}) async-start(s8[6291456]{0:T(1024)(128)(4,1)} %bitcast.7), calls=%async_computation | async-start | bytes 8388608
  56.9 15.0 %collective-permute-start.10 = (f32[2,4,64,128]{3,2,1,0:T(8,128)S(1)}, f32[2,4,64,128]{3,2,1,0:T(8,128)S(1)}, u32[]{:S(2)}, u32[]{:S(2)}) collective-permute-start(f32[2,4,64,128]{3,2,1,0:T(8,128)S(1)} %get-tuple-element.85), channel_id=1, source_target_pairs={{0,1},{1,0},{2,3},{3,2},{4,5},{5,4},{6,7},{7,6},{8,9},{9,8},{10,11... | collective-permute-start | bytes 786440 | tf_op jit(solution)/shard_map/ppermute | solution.py:548
  56.9 14.9 %collective-permute-start.11 = (f32[2,4,64,128]{3,2,1,0:T(8,128)S(1)}, f32[2,4,64,128]{3,2,1,0:T(8,128)S(1)}, u32[]{:S(2)}, u32[]{:S(2)}) collective-permute-start(f32[2,4,64,128]{3,2,1,0:T(8,128)S(1)} %get-tuple-element.86), channel_id=1, source_target_pairs={{0,15},{1,2},{2,1},{3,4},{4,3},{5,6},{6,5},{7,8},{8,7},{9,10},{10,... | collective-permute-start | bytes 786440 | tf_op jit(solution)/shard_map/ppermute | solution.py:549
  59.2 12.6 %collective-permute-start.12 = (f32[3,4,16,128]{3,2,1,0:T(8,128)S(1)}, f32[3,4,16,128]{3,2,1,0:T(8,128)S(1)}, u32[]{:S(2)}, u32[]{:S(2)}) collective-permute-start(f32[3,4,16,128]{3,2,1,0:T(8,128)S(1)} %get-tuple-element.87), channel_id=1, source_target_pairs={{0,16},{16,32},{32,48},{48,64},{64,80},{80,96},{96,112},{112,0},{1... | collective-permute-start | bytes 294920 | tf_op jit(solution)/shard_map/ppermute | solution.py:554
  59.2 12.6 %collective-permute-start.13 = (f32[3,4,16,128]{3,2,1,0:T(8,128)S(1)}, f32[3,4,16,128]{3,2,1,0:T(8,128)S(1)}, u32[]{:S(2)}, u32[]{:S(2)}) collective-permute-start(f32[3,4,16,128]{3,2,1,0:T(8,128)S(1)} %get-tuple-element.88), channel_id=1, source_target_pairs={{0,112},{16,0},{32,16},{48,32},{64,48},{80,64},{96,80},{112,96},{1... | collective-permute-start | bytes 294920 | tf_op jit(solution)/shard_map/ppermute | solution.py:554
  64.1 9.8 %slice-start.1 = ((s8[6291456]{0:T(1024)(128)(4,1)}), s8[2097152]{0:T(1024)(128)(4,1)S(1)}, s32[]{:S(2)}) async-start(s8[6291456]{0:T(1024)(128)(4,1)} %bitcast.7), calls=%async_computation.1 | async-start | bytes 4194304
  72.4 5.3 %collective-permute-start.14 = (f32[1,4,72,128]{3,2,1,0:T(8,128)S(1)}, f32[1,4,72,128]{3,2,1,0:T(8,128)S(1)}, u32[]{:S(2)}, u32[]{:S(2)}) collective-permute-start(f32[1,4,72,128]{3,2,1,0:T(8,128)S(1)} %get-tuple-element.89), channel_id=1, source_target_pairs={{0,1},{1,0},{2,3},{3,2},{4,5},{5,4},{6,7},{7,6},{8,9},{9,8},{10,11... | collective-permute-start | bytes 442376 | tf_op jit(solution)/shard_map/ppermute | solution.py:548
  72.5 9.4 %collective-permute-start.15 = (f32[1,4,72,128]{3,2,1,0:T(8,128)S(1)}, f32[1,4,72,128]{3,2,1,0:T(8,128)S(1)}, u32[]{:S(2)}, u32[]{:S(2)}) collective-permute-start(f32[1,4,72,128]{3,2,1,0:T(8,128)S(1)} %get-tuple-element.90), channel_id=1, source_target_pairs={{0,15},{1,2},{2,1},{3,4},{4,3},{5,6},{6,5},{7,8},{8,7},{9,10},{10,... | collective-permute-start | bytes 442376 | tf_op jit(solution)/shard_map/ppermute | solution.py:549

commit v4 on v3

--- a/solution.py
+++ b/solution.py
@@ -64,34 +64,45 @@
     def __init__(self, x0=0, planes=NXL):
         thick = lax.axis_index("thick")
         place = lax.axis_index("width") * 2 + thick
+        last = lax.axis_size("width") * 2 - 1
         cast = lax.axis_index("cast")
-        last = lax.axis_size("width") * 2 - 1
-        near = self.near = (NYL - 1) * (1 - thick)
-        far = self.far = (NYL - 1) * thick
+        odd = lax.rem(cast, 2)
+        self.near = (NYL - 1) * (1 - thick)
+        self.far = (NYL - 1) * thick
+        self.high = (1 - odd, odd)
+        self.edge = tuple(h * (NXL - 1) for h in self.high)
+
+        def plane(x):
+            return pl.ds(pl.multiple_of(x * NYL, NYL), NYL)
+
+        self.beyond = tuple(plane(h * (NXL + 1)) for h in self.high)
+        self.face_in = tuple(plane(h * NXL) for h in self.high)
+        self.behind = tuple(plane(1 + 1 + h * (NXL - 3)) for h in self.high)
+        self.face_behind = tuple(plane(1 + h * (NXL - 2)) for h in self.high)
 
         def rows(pad):
             start = pad + x0 * NYL
             return (
-                pl.ds(start + near, planes, stride=NYL),
-                pl.ds(start + far, planes, stride=NYL),
-                pl.ds(pad, NYL),
-                pl.ds(pad + CELLS - NYL, NYL),
+                pl.ds(start + self.near, planes, stride=NYL),
+                pl.ds(start + self.far, planes, stride=NYL),
+                *(plane(pad // NYL + x) for x in self.edge),
             )
 
         self.rows = rows(PAD)
         self.inner = rows(0)
         self.dims = (1, 1, 0, 0)
-        high = jnp.where(thick == 0, 1.0, -1.0).astype(F32)
-        self.signs = (high, -high, -1.0, 1.0)
-
-        def inside(ok):
-            return jnp.where(ok, 1.0, 0.0).astype(F32)
-
+
+        def number(condition, yes, no):
+            return jnp.where(condition, yes, no).astype(F32)
+
+        up = number(thick == 0, 1.0, -1.0)
+        ahead = number(odd == 0, 1.0, -1.0)
+        self.signs = (up, -up, ahead, -ahead)
         self.masks = (
             1.0,
-            inside(((thick == 0) & (place > 0)) | ((thick == 1) & (place < last))),
-            inside(cast > 0),
-            inside(cast < lax.axis_size("cast") - 1),
+            number(((thick == 0) & (place > 0)) | ((thick == 1) & (place < last)), 1.0, 0.0),
+            1.0,
+            number((cast > 0) & (cast < lax.axis_size("cast") - 1), 1.0, 0.0),
         )
 
 
@@ -143,8 +154,8 @@
     for out, rows, d in zip((oa, ob, ol, oh), sides.rows, sides.dims):
         out[0] = hat[:, rows, :]
         out[1] = e[d, :, rows, :]
-        for c in range(1 if d else 3):
-            out[2 + c] = v[c, :, rows, :]
+        if d:
+            out[2] = v[0, :, rows, :]
 
     for i, k in enumerate((ka, kb, kl, kh)):
         rows, at, d = sides.rows[i], sides.inner[i], sides.dims[i]
@@ -212,14 +223,12 @@
     faces(w0, hat, e, f, src, inv, phi)
 
 
-PHI, BEHIND, SOURCE, INVERSE, FACE_Y, FACE_Z, LINES = range(7)
-LOW, HIGH = 0, 1
-
-
-def put_planes(outs, phi, f):
-    for out, edge, behind, face in zip(outs, (0, NXL - 1), (1, NXL - 2), (0, NXL - 2)):
-        out[PHI] = phi[:, pl.ds(PAD + edge * NYL, NYL), :]
-        out[BEHIND] = f[0, :, pl.ds(PAD + face * NYL, NYL), :] * phi[:, pl.ds(PAD + behind * NYL, NYL), :]
+SOURCE, INVERSE, BEHIND, FLOW = (pl.ds(i * NYL, NYL) for i in range(4))
+LINES = 4 * NYL
+
+
+def flux_behind(phi, f, s, side):
+    return f[0, :, s.face_behind[side], :] * phi[:, s.behind[side], :]
 
 
 def first_edge_kernel(w0, ha, hb, hl, hh, hat, e, v, f_in, src_in, inv_in, phi_in,
@@ -238,8 +247,8 @@
             coefs[i][...] = g
             src[:, rows, :] = source
             inv[:, rows, :] = inverse
-    f[0, :, pl.ds(0, PAD), :] = cl[...]
-    f[0, :, s.rows[3], :] = ch[...]
+    for rows, coef in zip(s.face_in, (cl, ch)):
+        f[0, :, rows, :] = coef[...]
     got = []
     for i in range(4):
         rows = s.rows[i]
@@ -250,16 +259,16 @@
         phi[:, rows, :] = value
     for out, rows in zip((oa, ob), s.rows):
         out[0] = phi[:, rows, :]
-        out[1] = v[1, :, rows, :]
-    put_planes((ol, oh), phi, f)
-    for out, rows, line in zip((ol, oh), s.rows[2:], (0, NXL - 1)):
-        out[SOURCE] = src[:, rows, :]
-        out[INVERSE] = inv[:, rows, :]
-        out[FACE_Y] = f[1, :, rows, :]
-        out[FACE_Z] = f[2, :, rows, :]
-        out[LINES] = jnp.zeros((NT, NYL, 128), F32)
+    for c in range(1, 3):
+        oa[c] = v[c, :, s.rows[0], :]
+    for i, (out, rows, x) in enumerate(zip((ol, oh), s.rows[2:], s.edge)):
+        out[:, SOURCE, :] = src[:, rows, :]
+        out[:, INVERSE, :] = inv[:, rows, :]
+        out[:, BEHIND, :] = flux_behind(phi, f, s, i)
+        out[:, FLOW, :] = v[0, :, rows, :]
+        out[:, pl.ds(LINES, 8), :] = jnp.zeros(SHAPE, F32)
         for j, coef in enumerate((ca, cb)):
-            out[LINES, :, pl.ds(j, 1), :] = coef[:, pl.ds(line, 1), :]
+            out[:, pl.ds(LINES + j, 1), :] = coef[:, pl.ds(x, 1), :]
 
 
 def add_sides(w, phi, coefs, halos, rows):
@@ -268,49 +277,54 @@
         phi[:, r, :] = value
 
 
-def wide_edge_kernel(w, last, old, f, phi_in, ca, cb, cl, ch, kl, kh, ha, hb, hl, hh, *rest):
+def wide_edge_kernel(w, w0, old, f, phi_in, ca, cb, cl, ch, rl, rh, kl, kh, ha, hb, *rest):
     del phi_in
     s = Sides()
     phi, *outs = rest[-3:]
-    halves = ((ca, cb), (ha[0], hb[0])), ((cl, ch), (hl[PHI], hh[PHI]))
+    ks = (kl, kh)
+    if w0 is None:
+        beyond = [(h[0], h[1]) for h in rest[:2]]
+    else:
+        beyond = [((-w0) * (k[:, SOURCE, :] * k[:, INVERSE, :]), k[:, BEHIND, :]) for k in ks]
+    halves = ((ca, cb), (ha[0], hb[0])), ((cl, ch), (beyond[0][0], beyond[1][0]))
     for (coefs, halos), rows in zip(halves, (s.rows[:2], s.rows[2:])):
         add_sides(w, phi, coefs, halos, rows)
-    beyond = (pl.ds(0, PAD), pl.ds(PAD + CELLS, PAD))
-    for side, (k, h) in enumerate(((kl, hl), (kh, hh))):
-        c = h[PHI]
-        face = f[0, :, beyond[0], :] if side == LOW else f[0, :, s.rows[3], :]
-        fy, fz = k[FACE_Y], k[FACE_Z]
-        t = face * old[:, s.rows[2 + side], :] + h[BEHIND]
+    row = lax.broadcasted_iota(jnp.int32, (NT, NYL, 128), 1)
+    for side, (r, k, (c, flux)) in enumerate(zip((rl, rh), ks, beyond)):
+        hat = r[0]
+        fy = jnp.where(row == NYL - 1, 0.0, recip(hat + pltpu.roll(hat, NYL - 1, 1)))
+        fz = recip(hat + z_up(hat, OUTSIDE))
+        t = f[0, :, s.face_in[side], :] * old[:, s.rows[2 + side], :] + flux
         t = t + fy * pltpu.roll(c, NYL - 1, 1) + pltpu.roll(fy * c, 1, 1)
         t = t + fz * z_up(c) + z_down(fz * c)
-        phi[:, beyond[side], :] = s.masks[2 + side] * (c + w * ((t - k[SOURCE]) * k[INVERSE] - c))
+        phi[:, s.beyond[side], :] = s.masks[2 + side] * (c + w * ((t - k[:, SOURCE, :]) * k[:, INVERSE, :] - c))
     for out, rows, at in zip(outs, s.rows, (s.near, s.far)):
         out[0, :, pl.ds(0, NXL), :] = phi[:, rows, :]
         out[0, :, pl.ds(NXL, 8), :] = jnp.zeros(SHAPE, F32)
-        for side, h in enumerate((hl, hh)):
-            out[0, :, pl.ds(NXL + side, 1), :] = h[PHI, :, pl.ds(at, 1), :]
-        if not last:
-            v = rest[0]
-            out[1, :, pl.ds(0, NXL), :] = v[2, :, rows, :]
-            out[1, :, pl.ds(NXL, 8), :] = jnp.zeros(SHAPE, F32)
-
-
-def narrow_edge_kernel(w, w_before, f, nu, phi_in, ca, cb, cl, ch, kl, kh, ha, hb, phi, oa, ob, ol, oh):
+        for side, (c, _) in enumerate(beyond):
+            line = jnp.sum(jnp.where(row == at, c, 0.0), axis=1, keepdims=True)
+            out[0, :, pl.ds(NXL + side, 1), :] = line
+
+
+def narrow_edge_kernel(w, w_before, f, v, nu, phi_in, ca, cb, cl, ch, kl, kh, ha, hb, phi, oa, ob, ol, oh):
     del phi_in
     s = Sides()
     inner = pl.ds(0, NXL)
     add_sides(w, phi, (ca, cb), (ha[0, :, inner, :], hb[0, :, inner, :]), s.rows[:2])
     for j, (h, at) in enumerate(((ha, s.near), (hb, s.far))):
-        for side, (k, c, plane) in enumerate(((kl, cl, 0), (kh, ch, NXL - 1))):
-            missing = w_before * (k[LINES, :, pl.ds(j, 1), :] * h[0, :, pl.ds(NXL + side, 1), :])
+        for side, (k, c, plane) in enumerate(zip((kl, kh), (cl, ch), s.edge)):
+            missing = w_before * (k[:, pl.ds(LINES + j, 1), :] * h[0, :, pl.ds(NXL + side, 1), :])
             row = pl.ds(PAD + plane * NYL + at, 1)
             phi[:, row, :] = phi[:, row, :] + w * (c[:, pl.ds(at, 1), :] * missing)
     for out, rows in zip((oa, ob), s.rows):
         out[0] = phi[:, rows, :]
-        out[1] = nu[:, rows, :]
-    put_planes((ol, oh), phi, f)
-    for out, rows in zip((ol, oh), s.rows[2:]):
-        out[2] = nu[:, rows, :]
+    oa[1] = nu[:, s.rows[0], :]
+    for i, (out, rows) in enumerate(zip((ol, oh), s.rows[2:])):
+        out[0] = phi[:, rows, :]
+        out[1] = flux_behind(phi, f, s, i)
+        out[2] = v[1, :, rows, :]
+        out[3] = v[2, :, rows, :]
+        out[4] = nu[:, rows, :]
 
 
 def predictor(v, nu, vnew, x0, x1):
@@ -380,6 +394,19 @@
     lax.fori_loop(0, NXL, body, start, unroll=16)
 
 
+def sweep_flow_kernel(w, phi, f, src, inv, v, nu, out, flow):
+    rows = Sides().rows[1]
+    flow[0] = v[1, :, rows, :]
+    flow[1] = v[2, :, rows, :]
+    flow[2] = nu[:, rows, :]
+    sweep_kernel(w, phi, f, src, inv, out)
+
+
+def predict_kernel(planes, v, nu, vnew_in, vnew):
+    del vnew_in
+    predictor(v, nu, vnew, *planes)
+
+
 def sweep_predict_kernel(w, planes, phi, f, src, inv, v, nu, vnew_in, out, vnew):
     del vnew_in
     sweep_kernel(w, phi, f, src, inv, out)
@@ -402,8 +429,14 @@
 
 
 def force_kernel(phi, hat, b, v, nu, *rest):
-    flows = [rest[0:4], rest[4:6], rest[6:8], rest[8:12]]
-    potential, vnew, sem = rest[13:]
+    near0, far0, near1, near2, far, first_l, first_h, low, high = rest[:9]
+    sent = (
+        (near0[2], near1[1], near1[2], near2[1]),
+        (far0[2], far[0], far[1], far[2]),
+        (first_l[:, FLOW, :], low[2], low[3], low[4]),
+        (first_h[:, FLOW, :], high[2], high[3], high[4]),
+    )
+    potential, vnew, sem = rest[10:]
     copies = [
         pltpu.make_async_copy(phi.at[t, pl.ds(PAD, CELLS)], potential.at[:, pl.ds(128 * t, 128)], sem.at[t])
         for t in range(NT)
@@ -413,17 +446,12 @@
 
     s = Sides()
     half = 0.5 * time_step
-    inner = pl.ds(0, NXL)
     for pair in ((0, 1), (2, 3)):
         got = []
         for i in pair:
             rows, d, sign, mask = s.rows[i], s.dims[i], s.signs[i], s.masks[i]
-            if d:
-                other = [flows[0][i][2], flows[1][i][1], flows[2][i][1, :, inner, :]]
-                hn = mask * flows[3][i][1]
-            else:
-                other = [flows[0][i][2 + c] for c in range(3)]
-                hn = mask * flows[3][i][2]
+            other = sent[i][:3]
+            hn = mask * sent[i][3]
             vc = [v[c, :, rows, :] for c in range(3)]
             coef = half * ((nu[:, rows, :] + hn) - sign * vc[d])
             gone = half * hn if d == 0 else coef
@@ -471,6 +499,13 @@
     del vnew_in
     planes = NXL // PARTS
     copies = []
+    s = Sides()
+    for side, (k, lines, plane) in enumerate(zip((kl, kh), (cl, ch), s.edge)):
+        for j, (h, at) in enumerate(((ha, s.near), (hb, s.far))):
+            missing = w * (lines[:, pl.ds(LINES + j, 1), :] * h[0, :, pl.ds(NXL + side, 1), :])
+            row = pl.ds(PAD + plane * NYL + at, 1)
+            for i, c in enumerate((1, 2)):
+                vnew[c, :, row, :] = vnew[c, :, row, :] + k[i, :, pl.ds(at, 1), :] * missing
     for part in range(PARTS):
         s = Sides(part * planes, planes)
         some = pl.ds(part * planes, planes)
@@ -480,13 +515,6 @@
             got += [(c, rows, vnew[c, :, rows, :] + k[j, :, some, :] * halo) for j, c in enumerate((2, 0))]
         for c, rows, value in got:
             vnew[c, :, rows, :] = value
-        corners = ([(kl, cl, LOW, 0)] if part == 0 else []) + ([(kh, ch, HIGH, NXL - 1)] if part == PARTS - 1 else [])
-        for k, lines, side, plane in corners:
-            for j, (h, at) in enumerate(((ha, s.near), (hb, s.far))):
-                missing = w * (lines[LINES, :, pl.ds(j, 1), :] * h[0, :, pl.ds(NXL + side, 1), :])
-                row = pl.ds(PAD + plane * NYL + at, 1)
-                for i, c in enumerate((1, 2)):
-                    vnew[c, :, row, :] = vnew[c, :, row, :] + k[i, :, pl.ds(at, 1), :] * missing
         per = planes * NYL
         for t in range(NT):
             copy = pltpu.make_async_copy(
@@ -537,21 +565,25 @@
     return [(a, False) for a in arrays]
 
 
-def ring(axis, step):
-    n = lax.axis_size(axis)
-    return [(i, (i + step) % n) for i in range(n)]
+def next_chip(b):
+    n = lax.axis_size("width") * 2
+    return lax.ppermute(b, WIDTH, [(i, (((i + 1) ^ 1) - 1) % n) for i in range(n)])
 
 
 def across(a, b):
-    n = lax.axis_size("width") * 2
+    return lax.ppermute(a, "thick", [(0, 1), (1, 0)]), next_chip(b)
+
+
+def along(a, b):
+    n, m = lax.axis_size("cast"), lax.axis_size("width") * 2
+    second = []
+    for i in range(n):
+        j = ((i + 1) ^ 1) - 1
+        second += [(i * m + k, j * m + k if 0 <= j < n else i * m + (k ^ 1)) for k in range(m)]
     return (
-        lax.ppermute(a, "thick", [(0, 1), (1, 0)]),
-        lax.ppermute(b, WIDTH, [(i, (((i + 1) ^ 1) - 1) % n) for i in range(n)]),
-    )
-
-
-def along(low, high):
-    return lax.ppermute(high, "cast", ring("cast", 1)), lax.ppermute(low, "cast", ring("cast", -1))
+        lax.ppermute(a, "cast", [(i, i ^ 1) for i in range(n)]),
+        lax.ppermute(b, ("cast", *WIDTH), second),
+    )
 
 
 def rows_of(n, planes=NXL):
@@ -574,7 +606,7 @@
 
     v, hat, e, vnew, *edges = run(
         load_kernel, "load", [(vel, True), (mag, True), (lab, True)],
-        [fields, field, fields, fields] + rows_of(3) + planes_of(5) + rows_of(2) + planes_of(2),
+        [fields, field, fields, fields] + rows_of(3) + planes_of(2) + rows_of(2) + planes_of(2),
         scratch=[
             pltpu.VMEM((3, NT, CELLS, 128), F32),
             pltpu.VMEM((CELLS, NT * 128), jnp.int32),
@@ -589,7 +621,8 @@
     )
     f, src, inv, phi, *rest = run(
         functools.partial(first_edge_kernel, w[0]), "edges1", vm(*h1, hat, e, v, f, src, inv, phi),
-        [fields] + [field] * 3 + [resident(NT, NXL, 128)] * 2 + [resident(NT, NYL, 128)] * 2 + rows_of(2) + planes_of(7),
+        [fields] + [field] * 3 + [resident(NT, NXL, 128)] * 2 + [resident(NT, NYL, 128)] * 2
+        + [resident(3, NT, NXL, 128), resident(1, NT, NXL, 128)] + [resident(NT, LINES + 8, 128)] * 2,
         aliases={7: 0, 8: 1, 9: 2, 10: 3},
     )
     coefs, edges = rest[:4], rest[4:]
@@ -598,38 +631,46 @@
     lines = h2[2:]
     old = phi
     phi, nu, vnew = run(
-        functools.partial(sweep_load_kernel, w[1], (0, 32)), "sweep1",
+        functools.partial(sweep_load_kernel, w[1], (0, 24)), "sweep1",
         vm(phi, f, src, inv, v) + [(visc, True)] + vm(vnew),
         [field, field, fields], aliases={6: 2}, scratch=[dma((NT,))], **work,
     )
     phi, *edges = run(
-        functools.partial(wide_edge_kernel, w[1], False), "edges2", vm(old, f, phi, *coefs, *lines, *h2, v),
-        [field] + rows_of(2, NXL + 8), aliases={2: 0},
+        functools.partial(wide_edge_kernel, w[1], w[0]), "edges2", vm(old, f, phi, *coefs, *h1[2:], *lines, *h2[:2]),
+        [field] + rows_of(1, NXL + 8), aliases={2: 0},
     )
 
     h3 = across(*edges)
-    phi, vnew = run(
-        functools.partial(sweep_predict_kernel, w[2], (32, 64)), "sweep2", vm(phi, f, src, inv, v, nu, vnew),
-        [field, fields], aliases={6: 1}, **work,
-    )
+    phi, flow = run(
+        functools.partial(sweep_flow_kernel, w[2]), "sweep2", vm(phi, f, src, inv, v, nu),
+        [field, resident(3, NT, NXL, 128)], **work,
+    )
+    (vnew,) = run(
+        functools.partial(predict_kernel, (24, 48)), "predict", vm(v, nu, vnew), [fields], aliases={2: 0}, **work
+    )
+    flow = next_chip(flow)
     phi, *edges = run(
-        functools.partial(narrow_edge_kernel, w[2], w[1]), "edges3", vm(f, nu, phi, *coefs, *lines, *h3),
-        [field] + rows_of(2) + planes_of(3), aliases={2: 0},
+        functools.partial(narrow_edge_kernel, w[2], w[1]), "edges3", vm(f, v, nu, phi, *coefs, *lines, *h3),
+        [field, resident(2, NT, NXL, 128), resident(1, NT, NXL, 128)] + planes_of(5), aliases={3: 0},
     )
 
     h4 = (*across(*edges[:2]), *along(*edges[2:]))
     old = phi
-    (phi,) = run(functools.partial(sweep_kernel, w[3]), "sweep3", vm(phi, f, src, inv), [field], **work)
+    phi, vnew = run(
+        functools.partial(sweep_predict_kernel, w[3], (48, 64)), "sweep3", vm(phi, f, src, inv, v, nu, vnew),
+        [field, fields], aliases={6: 1}, **work,
+    )
     phi, *edges = run(
-        functools.partial(wide_edge_kernel, w[3], True), "edges4", vm(old, f, phi, *coefs, *lines, *h4),
+        functools.partial(wide_edge_kernel, w[3], None), "edges4",
+        vm(old, f, phi, *coefs, *h1[2:], *lines, *h4, flow),
         [field] + rows_of(1, NXL + 8), aliases={2: 0},
     )
 
     h5 = across(*edges)
     potential, vnew = run(
-        force_kernel, "force", vm(phi, hat, mag, v, nu, *h1, *h2[:2], *h3, *h4, vnew),
+        force_kernel, "force", vm(phi, hat, mag, v, nu, *h1[:2], h2[0], h4[0], flow, *lines, *h4[2:], vnew),
         [jax.ShapeDtypeStruct((CELLS, NT * 128), F32), fields],
-        aliases={17: 1}, scratch=[dma((NT,))], **work,
+        aliases={14: 1}, scratch=[dma((NT,))], **work,
     )
     result, _ = run(
         functools.partial(last_kernel, w[3]), "last", vm(*products, *lines, *h5, vnew),

time: 85.1 us -> 76.3 us (0.90)
  waiting for transfers between devices: 20.3 us -> 13.8 us
  starting transfers between devices: 28.8 us -> 26.3 us
    ppermute x16 -> x17, waiting for transfers between devices: 20.3 us -> 13.8 us  [the longest x6 12.5 us: next_chip(): lax.ppermute(b, WIDTH, [(i, ((i + 1 ^ 1) - 1) % n) for i in range(n)])]
    ppermute x16 -> x17, starting transfers between devices: 28.8 us -> 26.3 us  [the longest x6 15.9 us: next_chip(): lax.ppermute(b, WIDTH, [(i, ((i + 1 ^ 1) - 1) % n) for i in range(n)])]
    pallas_call x11 -> x12, Pallas kernels: 35 us -> 35.2 us  [run(): pl.pallas_call(kernel, out_shape=outs, in_specs=[IN_HBM if hbm else IN_VM...]
  transfers between devices with their start and end apart: 16 -> 17, of which waited for: 5 -> 5; matrix products, arithmetic and copies ran while one was open for 0% -> 0% of each run, Pallas kernels for 25% -> 29%
where the time goes in v4:
time: 76.3 us; the launch traced here: 76.2 us
  Pallas kernels  35.2 us (46%)
  starting transfers between devices  26.3 us (34%)
  waiting for transfers between devices  13.8 us (18%)
  between operations  0.98 us (1%)
    pallas_call x12, Pallas kernels, run(): pl.pallas_call(kernel, out_shape=outs, in_specs=[IN_HBM if hbm else IN_VM...  35.2 us
    ppermute x6, starting transfers between devices, next_chip(): lax.ppermute(b, WIDTH, [(i, ((i + 1 ^ 1) - 1) % n) for i in range(n)])  15.9 us
    ppermute x6, waiting for transfers between devices, next_chip(): lax.ppermute(b, WIDTH, [(i, ((i + 1 ^ 1) - 1) % n) for i in range(n)])  12.5 us
    ppermute x3, starting transfers between devices, along(): lax.ppermute(b, ('cast', *WIDTH), second)  6.83 us
    ppermute x3, starting transfers between devices, along(): lax.ppermute(a, 'cast', [(i, i ^ 1) for i in range(n)])  3.1 us
  transfers between devices with their start and end apart: 17, of which 5 were waited for; matrix products, arithmetic and copies ran while one was open for 0% of the time, Pallas kernels for 29%

profile of v4, /device:TPU:2, one launch (start us, length us, event | category | flops | bytes accessed | tf_op | source)
XLA Modules:
  0.0 76.2 jit_solution(11849569177274769833)
XLA Ops:
  0.6 7.3 %load.1 = (f32[3,4,1056,128]{3,2,1,0:T(8,128)S(1)}, f32[4,1056,128]{2,1,0:T(8,128)S(1)}, f32[3,4,1056,128]{3,2,1,0:T(8,128)S(1)}, f32[3,4,1056,128]{3,2,1,0:T(8,...) custom-call(f32[3,1024,512]{2,1,0:T(8,128)} %bitcast.10, ...), custom_call_target="tpu_custom_call" | custom-call | tf_op jit(solution)/shard_map/load/pallas_call | solution.py:551
  7.9 0.1 collective-permute-start
  8.0 4.7 %collective-permute-start.1 = (f32[3,4,64,128]{3,2,1,0:T(8,128)S(1)}, f32[3,4,64,128]{3,2,1,0:T(8,128)S(1)}, u32[]{:S(2)}, u32[]{:S(2)}) collective-permute-start(f32[3,4,64,128]{3,2,1,0:T(8,128)S(1)} %get-tuple-element.56), channel_id=1, source_target_pairs={{0,15},{1,2},{2,1},{3,4},{4,3},{5,6},{6,5},{7,8},{8,7},{9,10},{10,... | collective-permute-start | bytes 1179656 | tf_op jit(solution)/shard_map/ppermute | solution.py:570
  12.7 1.9 %collective-permute-start.2 = (f32[2,4,16,128]{3,2,1,0:T(8,128)S(1)}, f32[2,4,16,128]{3,2,1,0:T(8,128)S(1)}, u32[]{:S(2)}, u32[]{:S(2)}) collective-permute-start(f32[2,4,16,128]{3,2,1,0:T(8,128)S(1)} %get-tuple-element.57), channel_id=1, source_target_pairs={{0,16},{16,0},{32,48},{48,32},{64,80},{80,64},{96,112},{112,96},{1... | collective-permute-start | bytes 196616 | tf_op jit(solution)/shard_map/ppermute | solution.py:584
  14.6 3.4 %collective-permute-start.3 = (f32[2,4,16,128]{3,2,1,0:T(8,128)S(1)}, f32[2,4,16,128]{3,2,1,0:T(8,128)S(1)}, u32[]{:S(2)}, u32[]{:S(2)}) collective-permute-start(f32[2,4,16,128]{3,2,1,0:T(8,128)S(1)} %get-tuple-element.58), channel_id=1, source_target_pairs={{0,1},{1,0},{2,3},{3,2},{4,5},{5,4},{6,7},{7,6},{8,9},{9,8},{10,11... | collective-permute-start | bytes 196616 | tf_op jit(solution)/shard_map/ppermute | solution.py:585
  18.0 6.7 %faces.1 = (f32[3,4,1056,128]{3,2,1,0:T(8,128)S(1)}, f32[4,1056,128]{2,1,0:T(8,128)S(1)}, f32[4,1056,128]{2,1,0:T(8,128)S(1)}, f32[4,1056,128]{2,1,0:T(8,128)S(1)}) custom-call(f32[4,1056,128]{2,1,0:T(8,128)S(1)} %get-tuple-element.59.hat, f32[3,4,1056,128]{3,2,1,0:T(8,128)S(1)} %get-tuple-element.60.e, f32[3,4,1056,128]{3,2,1,0:T(8,128)S(1)} %get-tuple-element.61.v, ...), custom_call_target="tpu_custom_call" | custom-call | flops 10000000 | bytes 16777216 | tf_op jit(solution)/shard_map/faces/pallas_call | solution.py:551
  24.7 1.2 %collective-permute-done.3.hh.rh = f32[2,4,16,128]{3,2,1,0:T(8,128)S(1)} collective-permute-done((f32[2,4,16,128]{3,2,1,0:T(8,128)S(1)}, f32[2,4,16,128]{3,2,1,0:T(8,128)S(1)}, u32[]{:S(2)}, u32[]{:S(2)}) %collective-permute-start.3) | collective-permute-done | bytes 65568 | tf_op jit(solution)/shard_map/ppermute | solution.py:585
  25.9 1.6 %edges1.1 = (f32[3,4,1056,128]{3,2,1,0:T(8,128)S(1)}, f32[4,1056,128]{2,1,0:T(8,128)S(1)}, f32[4,1056,128]{2,1,0:T(8,128)S(1)}, f32[4,1056,128]{2,1,0:T(8,128)S(...) custom-call(f32[3,4,64,128]{3,2,1,0:T(8,128)S(1)} %collective-permut, ...), custom_call_target="tpu_custom_call", output_to_operand_aliasing={{0}: (7, {}), {1}: (8, {}), {2}: (9, {}), {3}: (10, {})} | custom-call | tf_op jit(solution)/shard_map/edges1/pallas_call | solution.py:551
  27.6 0.1 collective-permute-start.6
  27.7 0.1 collective-permute-start.4
  27.8 1.0 %collective-permute-start.5 = (f32[4,72,128]{2,1,0:T(8,128)S(1)}, f32[4,72,128]{2,1,0:T(8,128)S(1)}, u32[]{:S(2)}, u32[]{:S(2)}) collective-permute-start(f32[4,72,128]{2,1,0:T(8,128)S(1)} %get-tuple-element.68), channel_id=1, source_target_pairs={{0,1},{1,0},{2,3},{3,2},{4,5},{5,4},{6,7},{7,6},{8,9},{9,8},{10,11... | collective-permute-start | bytes 442376 | tf_op jit(solution)/shard_map/ppermute | solution.py:585
  28.7 2.6 %collective-permute-start.7 = (f32[1,4,64,128]{3,2,1,0:T(8,128)S(1)}, f32[1,4,64,128]{3,2,1,0:T(8,128)S(1)}, u32[]{:S(2)}, u32[]{:S(2)}) collective-permute-start(f32[1,4,64,128]{3,2,1,0:T(8,128)S(1)} %get-tuple-element.80), channel_id=1, source_target_pairs={{0,15},{1,2},{2,1},{3,4},{4,3},{5,6},{6,5},{7,8},{8,7},{9,10},{10,... | collective-permute-start | bytes 393224 | tf_op jit(solution)/shard_map/ppermute | solution.py:570
  31.3 3.9 %sweep1.1 = (f32[4,1056,128]{2,1,0:T(8,128)S(1)}, f32[4,1056,128]{2,1,0:T(8,128)S(1)}, f32[3,4,1056,128]{3,2,1,0:T(8,128)S(1)}) custom-call(f32[4,1056,128]{2,1,0:T(8,128)S(1)} %get-tuple-element.70.phi.old, f32[3,4,1056,128]{3,2,1,0:T(8,128)S(1)} %get-tuple-element.69.f, ...), custom_call_target="tpu_custom_call", output_to_operand_aliasing={{2}: (6, {})} | custom-call | flops 10000000 | bytes 16777216 | tf_op jit(solution)/shard_map/sweep1/pallas_call | solution.py:551
  35.2 3.0 %collective-permute-done.7.hb = f32[1,4,64,128]{3,2,1,0:T(8,128)S(1)} collective-permute-done((f32[1,4,64,128]{3,2,1,0:T(8,128)S(1)}, f32[1,4,64,128]{3,2,1,0:T(8,128)S(1)}, u32[]{:S(2)}, u32[]{:S(2)}) %collective-permute-start.7) | collective-permute-done | bytes 131104 | tf_op jit(solution)/shard_map/ppermute | solution.py:570
  38.2 0.6 edges2.1
  38.8 0.1 collective-permute-start.8
  38.9 2.4 %collective-permute-start.9 = (f32[1,4,72,128]{3,2,1,0:T(8,128)S(1)}, f32[1,4,72,128]{3,2,1,0:T(8,128)S(1)}, u32[]{:S(2)}, u32[]{:S(2)}) collective-permute-start(f32[1,4,72,128]{3,2,1,0:T(8,128)S(1)} %get-tuple-element.84), channel_id=1, source_target_pairs={{0,15},{1,2},{2,1},{3,4},{4,3},{5,6},{6,5},{7,8},{8,7},{9,10},{10,... | collective-permute-start | bytes 442376 | tf_op jit(solution)/shard_map/ppermute | solution.py:570
  41.3 2.0 %sweep2.1 = (f32[4,1056,128]{2,1,0:T(8,128)S(1)}, f32[3,4,64,128]{3,2,1,0:T(8,128)S(1)}) custom-call(f32[4,1056,128]{2,1,0:T(8,128)S(1)} %get-tuple-element.81.phi, f32[3,4,1056,128]{3,2,1,0:T(8,128)S(1)} %get-tuple-element.69.f, f32[4,1056,128]{2,1,0:T(8,128)S(1)} %get-tuple-element.71.src, f32[4,1056,128]{2,1,0:T(8,128)S(1)} %get-tuple-element.72.inv, ...), custom_call_target="tpu_custom_call" | custom-call | flops 10000000 | bytes 16777216 | tf_op jit(solution)/shard_map/sweep2/pallas_call | solution.py:551
  43.3 3.1 %collective-permute-start.14 = (f32[3,4,64,128]{3,2,1,0:T(8,128)S(1)}, f32[3,4,64,128]{3,2,1,0:T(8,128)S(1)}, u32[]{:S(2)}, u32[]{:S(2)}) collective-permute-start(f32[3,4,64,128]{3,2,1,0:T(8,128)S(1)} %get-tuple-element.92), channel_id=1, source_target_pairs={{0,15},{1,2},{2,1},{3,4},{4,3},{5,6},{6,5},{7,8},{8,7},{9,10},{10,... | collective-permute-start | bytes 1179656 | tf_op jit(solution)/shard_map/ppermute | solution.py:570
  46.4 1.7 %collective-permute-done.9.hb = f32[1,4,72,128]{3,2,1,0:T(8,128)S(1)} collective-permute-done((f32[1,4,72,128]{3,2,1,0:T(8,128)S(1)}, f32[1,4,72,128]{3,2,1,0:T(8,128)S(1)}, u32[]{:S(2)}, u32[]{:S(2)}) %collective-permute-start.9) | collective-permute-done | bytes 147488 | tf_op jit(solution)/shard_map/ppermute | solution.py:570
  48.1 0.6 edges3.1
  48.8 1.1 %collective-permute-start.12 = (f32[5,4,16,128]{3,2,1,0:T(8,128)S(1)}, f32[5,4,16,128]{3,2,1,0:T(8,128)S(1)}, u32[]{:S(2)}, u32[]{:S(2)}) collective-permute-start(f32[5,4,16,128]{3,2,1,0:T(8,128)S(1)} %get-tuple-element.90), channel_id=1, source_target_pairs={{0,16},{16,0},{32,48},{48,32},{64,80},{80,64},{96,112},{112,96},{1... | collective-permute-start | bytes 491528 | tf_op jit(solution)/shard_map/ppermute | solution.py:584
  49.9 2.5 %collective-permute-start.13 = (f32[5,4,16,128]{3,2,1,0:T(8,128)S(1)}, f32[5,4,16,128]{3,2,1,0:T(8,128)S(1)}, u32[]{:S(2)}, u32[]{:S(2)}) collective-permute-start(f32[5,4,16,128]{3,2,1,0:T(8,128)S(1)} %get-tuple-element.91), channel_id=1, source_target_pairs={{0,1},{1,0},{2,3},{3,2},{4,5},{5,4},{6,7},{7,6},{8,9},{9,8},{10,11... | collective-permute-start | bytes 491528 | tf_op jit(solution)/shard_map/ppermute | solution.py:585
  52.3 0.8 %collective-permute-start.11 = (f32[1,4,64,128]{3,2,1,0:T(8,128)S(1)}, f32[1,4,64,128]{3,2,1,0:T(8,128)S(1)}, u32[]{:S(2)}, u32[]{:S(2)}) collective-permute-start(f32[1,4,64,128]{3,2,1,0:T(8,128)S(1)} %get-tuple-element.89), channel_id=1, source_target_pairs={{0,15},{1,2},{2,1},{3,4},{4,3},{5,6},{6,5},{7,8},{8,7},{9,10},{10,... | collective-permute-start | bytes 393224 | tf_op jit(solution)/shard_map/ppermute | solution.py:570
  53.2 2.1 %predict.1.vnew_in = f32[3,4,1056,128]{3,2,1,0:T(8,128)S(1)} custom-call(f32[3,4,1056,128]{3,2,1,0:T(8,128)S(1)} %get-tuple-element.61.v, f32[4,1056,128]{2,1,0:T(8,128)S(1)} %get-tuple-element.73.nu, f32[3,4,1056,128]{3,2,1,0:T(8,128)S(1)} %get-tuple-element.86.vnew_in), custom_call_target="tpu_custom_call", output_to_operand_aliasing={{}: (2, {})} | custom-call | flops 10000000 | bytes 16777216 | tf_op jit(solution)/shard_map/predict/pallas_call | solution.py:551
  55.3 3.2 %sweep3.1 = (f32[4,1056,128]{2,1,0:T(8,128)S(1)}, f32[3,4,1056,128]{3,2,1,0:T(8,128)S(1)}) custom-call(f32[4,1056,128]{2,1,0:T(8,128)S(1)} %get-tuple-element.85.phi.old, f32[3,4,1056,128]{3,2,1,0:T(8,128)S(1)} %get-tuple-element.69.f, f32[4,1056,128]{2,1,0:T(8,128)S(1)} %get-tuple-element.71.src, ...), custom_call_target="tpu_custom_call", output_to_operand_aliasing={{1}: (6, {})} | custom-call | flops 10000000 | bytes 16777216 | tf_op jit(solution)/shard_map/sweep3/pallas_call | solution.py:551
  58.4 4.8 %collective-permute-done.11.hb = f32[1,4,64,128]{3,2,1,0:T(8,128)S(1)} collective-permute-done((f32[1,4,64,128]{3,2,1,0:T(8,128)S(1)}, f32[1,4,64,128]{3,2,1,0:T(8,128)S(1)}, u32[]{:S(2)}, u32[]{:S(2)}) %collective-permute-start.11) | collective-permute-done | bytes 131104 | tf_op jit(solution)/shard_map/ppermute | solution.py:570
  63.2 0.6 edges4.1
  63.9 2.3 %collective-permute-start.16 = (f32[1,4,72,128]{3,2,1,0:T(8,128)S(1)}, f32[1,4,72,128]{3,2,1,0:T(8,128)S(1)}, u32[]{:S(2)}, u32[]{:S(2)}) collective-permute-start(f32[1,4,72,128]{3,2,1,0:T(8,128)S(1)} %get-tuple-element.94), channel_id=1, source_target_pairs={{0,15},{1,2},{2,1},{3,4},{4,3},{5,6},{6,5},{7,8},{8,7},{9,10},{10,... | collective-permute-start | bytes 442376 | tf_op jit(solution)/shard_map/ppermute | solution.py:570
  66.2 3.7 %force.1 = (f32[1024,512]{1,0:T(8,128)}, f32[3,4,1056,128]{3,2,1,0:T(8,128)S(1)}) custom-call(f32[4,1056,128]{2,1,0:T(8,128)S(1)} %get-tuple-element.95.phi, f32[4,1056,128]{2,1,0:T(8,128)S(1)} %get-tuple-element.59.hat, f32[3,1024,512]{2,1,0:T(8,128)S(1)} %bitcast.9, f32[3,4,1056,128]{3,2,1,0:T(8,128)S(1)} %get-tuple-element.61.v, ...), custom_call_target="tpu_custom_call", output_to_operand_aliasing={{1}: (14, {})} | custom-call | flops 10000000 | bytes 16777216 | tf_op jit(solution)/shard_map/force/pallas_call | solution.py:551
  70.0 3.1 %collective-permute-done.16.hb = f32[1,4,72,128]{3,2,1,0:T(8,128)S(1)} collective-permute-done((f32[1,4,72,128]{3,2,1,0:T(8,128)S(1)}, f32[1,4,72,128]{3,2,1,0:T(8,128)S(1)}, u32[]{:S(2)}, u32[]{:S(2)}) %collective-permute-start.16) | collective-permute-done | bytes 147488 | tf_op jit(solution)/shard_map/ppermute | solution.py:570
  73.1 2.9 %last.1 = (f32[3,1024,512]{2,1,0:T(8,128)}, f32[3,4,1056,128]{3,2,1,0:T(8,128)S(1)}) custom-call(f32[2,4,64,128]{3,2,1,0:T(8,128)S(1)} %get-tuple-element.51.ka, f32[2,4,64,128]{3,2,1,0:T(8,128)S(1)} %get-tuple-element.52.kb, f32[2,4,16,128]{3,2,1,0:T(8,128)S(1)} %get-tuple-element.53.kl, ...), custom_call_target="tpu_custom_call", output_to_operand_aliasing={{1}: (8, {})} | custom-call | tf_op jit(solution)/shard_map/last/pallas_call | solution.py:551
  (19 shorter events, 0.2 us)
Async XLA Ops:
  7.9 18.0 %collective-permute-start = (f32[3,4,64,128]{3,2,1,0:T(8,128)S(1)}, f32[3,4,64,128]{3,2,1,0:T(8,128)S(1)}, u32[]{:S(2)}, u32[]{:S(2)}) collective-permute-start(f32[3,4,64,128]{3,2,1,0:T(8,128)S(1)} %get-tuple-element.55), channel_id=1, source_target_pairs={{0,1},{1,0},{2,3},{3,2},{4,5},{5,4},{6,7},{7,6},{8,9},{9,8},{10,11... | collective-permute-start | bytes 1179656 | tf_op jit(solution)/shard_map/ppermute | solution.py:574
  8.0 17.9 %collective-permute-start.1 = (f32[3,4,64,128]{3,2,1,0:T(8,128)S(1)}, f32[3,4,64,128]{3,2,1,0:T(8,128)S(1)}, u32[]{:S(2)}, u32[]{:S(2)}) collective-permute-start(f32[3,4,64,128]{3,2,1,0:T(8,128)S(1)} %get-tuple-element.56), channel_id=1, source_target_pairs={{0,15},{1,2},{2,1},{3,4},{4,3},{5,6},{6,5},{7,8},{8,7},{9,10},{10,... | collective-permute-start | bytes 1179656 | tf_op jit(solution)/shard_map/ppermute | solution.py:570
  12.7 12.0 %collective-permute-start.2 = (f32[2,4,16,128]{3,2,1,0:T(8,128)S(1)}, f32[2,4,16,128]{3,2,1,0:T(8,128)S(1)}, u32[]{:S(2)}, u32[]{:S(2)}) collective-permute-start(f32[2,4,16,128]{3,2,1,0:T(8,128)S(1)} %get-tuple-element.57), channel_id=1, source_target_pairs={{0,16},{16,0},{32,48},{48,32},{64,80},{80,64},{96,112},{112,96},{1... | collective-permute-start | bytes 196616 | tf_op jit(solution)/shard_map/ppermute | solution.py:584
  14.6 11.3 %collective-permute-start.3 = (f32[2,4,16,128]{3,2,1,0:T(8,128)S(1)}, f32[2,4,16,128]{3,2,1,0:T(8,128)S(1)}, u32[]{:S(2)}, u32[]{:S(2)}) collective-permute-start(f32[2,4,16,128]{3,2,1,0:T(8,128)S(1)} %get-tuple-element.58), channel_id=1, source_target_pairs={{0,1},{1,0},{2,3},{3,2},{4,5},{5,4},{6,7},{7,6},{8,9},{9,8},{10,11... | collective-permute-start | bytes 196616 | tf_op jit(solution)/shard_map/ppermute | solution.py:585
  27.6 10.6 %collective-permute-start.6 = (f32[3,4,64,128]{3,2,1,0:T(8,128)S(1)}, f32[3,4,64,128]{3,2,1,0:T(8,128)S(1)}, u32[]{:S(2)}, u32[]{:S(2)}) collective-permute-start(f32[3,4,64,128]{3,2,1,0:T(8,128)S(1)} %get-tuple-element.79), channel_id=1, source_target_pairs={{0,1},{1,0},{2,3},{3,2},{4,5},{5,4},{6,7},{7,6},{8,9},{9,8},{10,11... | collective-permute-start | bytes 1179656 | tf_op jit(solution)/shard_map/ppermute | solution.py:574
  27.7 10.5 %collective-permute-start.4 = (f32[4,72,128]{2,1,0:T(8,128)S(1)}, f32[4,72,128]{2,1,0:T(8,128)S(1)}, u32[]{:S(2)}, u32[]{:S(2)}) collective-permute-start(f32[4,72,128]{2,1,0:T(8,128)S(1)} %get-tuple-element.67), channel_id=1, source_target_pairs={{0,16},{16,0},{32,48},{48,32},{64,80},{80,64},{96,112},{112,96},{1... | collective-permute-start | bytes 442376 | tf_op jit(solution)/shard_map/ppermute | solution.py:584
  27.8 10.4 %collective-permute-start.5 = (f32[4,72,128]{2,1,0:T(8,128)S(1)}, f32[4,72,128]{2,1,0:T(8,128)S(1)}, u32[]{:S(2)}, u32[]{:S(2)}) collective-permute-start(f32[4,72,128]{2,1,0:T(8,128)S(1)} %get-tuple-element.68), channel_id=1, source_target_pairs={{0,1},{1,0},{2,3},{3,2},{4,5},{5,4},{6,7},{7,6},{8,9},{9,8},{10,11... | collective-permute-start | bytes 442376 | tf_op jit(solution)/shard_map/ppermute | solution.py:585
  28.7 9.5 %collective-permute-start.7 = (f32[1,4,64,128]{3,2,1,0:T(8,128)S(1)}, f32[1,4,64,128]{3,2,1,0:T(8,128)S(1)}, u32[]{:S(2)}, u32[]{:S(2)}) collective-permute-start(f32[1,4,64,128]{3,2,1,0:T(8,128)S(1)} %get-tuple-element.80), channel_id=1, source_target_pairs={{0,15},{1,2},{2,1},{3,4},{4,3},{5,6},{6,5},{7,8},{8,7},{9,10},{10,... | collective-permute-start | bytes 393224 | tf_op jit(solution)/shard_map/ppermute | solution.py:570
  38.8 7.6 %collective-permute-start.8 = (f32[1,4,72,128]{3,2,1,0:T(8,128)S(1)}, f32[1,4,72,128]{3,2,1,0:T(8,128)S(1)}, u32[]{:S(2)}, u32[]{:S(2)}) collective-permute-start(f32[1,4,72,128]{3,2,1,0:T(8,128)S(1)} %get-tuple-element.83), channel_id=1, source_target_pairs={{0,1},{1,0},{2,3},{3,2},{4,5},{5,4},{6,7},{7,6},{8,9},{9,8},{10,11... | collective-permute-start | bytes 442376 | tf_op jit(solution)/shard_map/ppermute | solution.py:574
  38.9 9.2 %collective-permute-start.9 = (f32[1,4,72,128]{3,2,1,0:T(8,128)S(1)}, f32[1,4,72,128]{3,2,1,0:T(8,128)S(1)}, u32[]{:S(2)}, u32[]{:S(2)}) collective-permute-start(f32[1,4,72,128]{3,2,1,0:T(8,128)S(1)} %get-tuple-element.84), channel_id=1, source_target_pairs={{0,15},{1,2},{2,1},{3,4},{4,3},{5,6},{6,5},{7,8},{8,7},{9,10},{10,... | collective-permute-start | bytes 442376 | tf_op jit(solution)/shard_map/ppermute | solution.py:570
  43.3 19.9 %collective-permute-start.14 = (f32[3,4,64,128]{3,2,1,0:T(8,128)S(1)}, f32[3,4,64,128]{3,2,1,0:T(8,128)S(1)}, u32[]{:S(2)}, u32[]{:S(2)}) collective-permute-start(f32[3,4,64,128]{3,2,1,0:T(8,128)S(1)} %get-tuple-element.92), channel_id=1, source_target_pairs={{0,15},{1,2},{2,1},{3,4},{4,3},{5,6},{6,5},{7,8},{8,7},{9,10},{10,... | collective-permute-start | bytes 1179656 | tf_op jit(solution)/shard_map/ppermute | solution.py:570
  48.7 14.6 %collective-permute-start.10 = (f32[2,4,64,128]{3,2,1,0:T(8,128)S(1)}, f32[2,4,64,128]{3,2,1,0:T(8,128)S(1)}, u32[]{:S(2)}, u32[]{:S(2)}) collective-permute-start(f32[2,4,64,128]{3,2,1,0:T(8,128)S(1)} %get-tuple-element.88), channel_id=1, source_target_pairs={{0,1},{1,0},{2,3},{3,2},{4,5},{5,4},{6,7},{7,6},{8,9},{9,8},{10,11... | collective-permute-start | bytes 786440 | tf_op jit(solution)/shard_map/ppermute | solution.py:574
  48.8 14.4 %collective-permute-start.12 = (f32[5,4,16,128]{3,2,1,0:T(8,128)S(1)}, f32[5,4,16,128]{3,2,1,0:T(8,128)S(1)}, u32[]{:S(2)}, u32[]{:S(2)}) collective-permute-start(f32[5,4,16,128]{3,2,1,0:T(8,128)S(1)} %get-tuple-element.90), channel_id=1, source_target_pairs={{0,16},{16,0},{32,48},{48,32},{64,80},{80,64},{96,112},{112,96},{1... | collective-permute-start | bytes 491528 | tf_op jit(solution)/shard_map/ppermute | solution.py:584
  49.9 13.4 %collective-permute-start.13 = (f32[5,4,16,128]{3,2,1,0:T(8,128)S(1)}, f32[5,4,16,128]{3,2,1,0:T(8,128)S(1)}, u32[]{:S(2)}, u32[]{:S(2)}) collective-permute-start(f32[5,4,16,128]{3,2,1,0:T(8,128)S(1)} %get-tuple-element.91), channel_id=1, source_target_pairs={{0,1},{1,0},{2,3},{3,2},{4,5},{5,4},{6,7},{7,6},{8,9},{9,8},{10,11... | collective-permute-start | bytes 491528 | tf_op jit(solution)/shard_map/ppermute | solution.py:585
  52.3 10.9 %collective-permute-start.11 = (f32[1,4,64,128]{3,2,1,0:T(8,128)S(1)}, f32[1,4,64,128]{3,2,1,0:T(8,128)S(1)}, u32[]{:S(2)}, u32[]{:S(2)}) collective-permute-start(f32[1,4,64,128]{3,2,1,0:T(8,128)S(1)} %get-tuple-element.89), channel_id=1, source_target_pairs={{0,15},{1,2},{2,1},{3,4},{4,3},{5,6},{6,5},{7,8},{8,7},{9,10},{10,... | collective-permute-start | bytes 393224 | tf_op jit(solution)/shard_map/ppermute | solution.py:570
  63.2 3.0 %slice-start = ((s8[6291456]{0:T(1024)(128)(4,1)}), s8[4194304]{0:T(1024)(128)(4,1)S(1)}, s32[]{:S(2)}) async-start(s8[6291456]{0:T(1024)(128)(4,1)} %bitcast.7), calls=%async_computation | async-start | bytes 8388608
  63.2 3.0 %slice-start.1 = ((s8[6291456]{0:T(1024)(128)(4,1)}), s8[2097152]{0:T(1024)(128)(4,1)S(1)}, s32[]{:S(2)}) async-start(s8[6291456]{0:T(1024)(128)(4,1)} %bitcast.7), calls=%async_computation.1 | async-start | bytes 4194304
  63.8 6.1 %collective-permute-start.15 = (f32[1,4,72,128]{3,2,1,0:T(8,128)S(1)}, f32[1,4,72,128]{3,2,1,0:T(8,128)S(1)}, u32[]{:S(2)}, u32[]{:S(2)}) collective-permute-start(f32[1,4,72,128]{3,2,1,0:T(8,128)S(1)} %get-tuple-element.93), channel_id=1, source_target_pairs={{0,1},{1,0},{2,3},{3,2},{4,5},{5,4},{6,7},{7,6},{8,9},{9,8},{10,11... | collective-permute-start | bytes 442376 | tf_op jit(solution)/shard_map/ppermute | solution.py:574
  63.9 9.1 %collective-permute-start.16 = (f32[1,4,72,128]{3,2,1,0:T(8,128)S(1)}, f32[1,4,72,128]{3,2,1,0:T(8,128)S(1)}, u32[]{:S(2)}, u32[]{:S(2)}) collective-permute-start(f32[1,4,72,128]{3,2,1,0:T(8,128)S(1)} %get-tuple-element.94), channel_id=1, source_target_pairs={{0,15},{1,2},{2,1},{3,4},{4,3},{5,6},{6,5},{7,8},{8,7},{9,10},{10,... | collective-permute-start | bytes 442376 | tf_op jit(solution)/shard_map/ppermute | solution.py:570

commit v5 on v4

--- a/solution.py
+++ b/solution.py
@@ -35,9 +35,9 @@
     return jnp.where(lax.broadcasted_iota(jnp.int32, a.shape, 2) == 127, after, r)
 
 
-def z_down(a):
+def z_down(a, fill=0.0):
     r = pltpu.roll(a, 1, 2)
-    before = jnp.concatenate([jnp.zeros_like(r[:1]), r[:-1]], axis=0)
+    before = jnp.concatenate([jnp.full_like(r[:1], fill), r[:-1]], axis=0)
     return jnp.where(lax.broadcasted_iota(jnp.int32, a.shape, 2) == 0, before, r)
 
 
@@ -106,63 +106,117 @@
         )
 
 
-CHUNKS = 8
-
-
-def load_kernel(vel, mag, lab, v, hat, e, vnew, oa, ob, ol, oh, ka, kb, kl, kh, b, lraw, sem):
-    per = CELLS // CHUNKS
+CHUNKS = 4
+PER = CELLS // CHUNKS
+
+
+def columns(source, chunk, target, sem, pad):
+    rows = pl.ds(chunk * PER, PER)
+    at = pl.ds(pad + chunk * PER, PER)
+    return [pltpu.make_async_copy(source.at[rows, pl.ds(128 * t, 128)], target.at[t, at], sem(t)) for t in range(NT)]
+
+
+def load_kernel(vel, mag, lab, v, b, hat, e, oa, ob, ol, oh, lraw, ve, be, sem, edge_sem):
+    s = Sides()
 
     def copies(ch):
-        src = pl.ds(ch * per, per)
-        dst = pl.ds(PAD + ch * per, per)
-        for t in range(NT):
-            col = pl.ds(128 * t, 128)
-            yield pltpu.make_async_copy(vel.at[:, src, col], v.at[:, t, dst], sem.at[ch, t])
-            yield pltpu.make_async_copy(mag.at[:, src, col], b.at[:, t, src], sem.at[ch, NT + t])
-        yield pltpu.make_async_copy(lab.at[src], lraw.at[src], sem.at[ch, 2 * NT])
-
-    for ch in range(CHUNKS):
-        for copy in copies(ch):
-            copy.start()
+        some = pl.ds(ch * PER, PER)
+        out = [pltpu.make_async_copy(lab.at[some], lraw.at[some], sem.at[ch, 4 * NT])]
+        for i, comp in enumerate((0, 2)):
+            out += columns(vel.at[comp], ch, v.at[comp], lambda t: sem.at[ch, i * NT + t], PAD)
+            out += columns(mag.at[comp], ch, b.at[i], lambda t: sem.at[ch, (2 + i) * NT + t], 0)
+        return out
+
+    outer = []
+    for i in range(2):
+        rows = s.inner[2 + i]
+        outer += [
+            pltpu.make_async_copy(vel.at[1, rows], ve.at[i], edge_sem.at[i, 0]),
+            pltpu.make_async_copy(mag.at[1, rows], be.at[i], edge_sem.at[i, 1]),
+        ]
+    chunks = [copies(ch) for ch in range(CHUNKS)]
+    for copy in chunks[0] + outer + [copy for chunk in chunks[1:] for copy in chunk]:
+        copy.start()
     fill_pads(v)
     fill_pads(e)
     fill_pads(hat, OUTSIDE)
     for ch in range(CHUNKS):
-        for copy in copies(ch):
+        for copy in chunks[ch]:
             copy.wait()
 
-        @pl.loop(0, per // 8, unroll=8)
+        @pl.loop(0, PER // 8, unroll=8)
         def _(i):
-            raw = pl.ds(pl.multiple_of(ch * per + i * 8, 8), 8)
-            at = pl.ds(pl.multiple_of(PAD + ch * per + i * 8, 8), 8)
+            raw = pl.ds(pl.multiple_of(ch * PER + i * 8, 8), 8)
+            at = pl.ds(pl.multiple_of(PAD + ch * PER + i * 8, 8), 8)
             for t in range(NT):
-                lb = lraw[raw, pl.ds(128 * t, 128)]
-                melt, shell = lb == 0, lb == 1
-                hat[t, at, :] = jnp.where(melt, 0.5, jnp.where(shell, 0.5 / 0.7, 0.125)).astype(F32)
-                gain = jnp.where(melt, 1.0, jnp.where(shell, 0.7, 4.0)).astype(F32) * force_gain
-                v0, v1, v2 = (v[c, t, at, :] for c in range(3))
-                b0, b1, b2 = (b[c, t, raw, :] for c in range(3))
-                e0, e1, e2 = v1 * b2 - v2 * b1, v2 * b0 - v0 * b2, v0 * b1 - v1 * b0
-                e[0, t, at, :] = e0
-                e[1, t, at, :] = e1
-                e[2, t, at, :] = e2
-                vnew[0, t, at, :] = gain * (e1 * b2 - e2 * b1)
-                vnew[1, t, at, :] = gain * (e2 * b0 - e0 * b2)
-                vnew[2, t, at, :] = gain * (e0 * b1 - e1 * b0)
-
-    sides = Sides()
-    for out, rows, d in zip((oa, ob, ol, oh), sides.rows, sides.dims):
+                label = lraw[raw, pl.ds(128 * t, 128)]
+                hat[t, at, :] = jnp.where(label == 0, 0.5, jnp.where(label == 1, 0.5 / 0.7, 0.125)).astype(F32)
+                e[1, t, at, :] = v[2, t, at, :] * b[0, t, raw, :] - v[0, t, at, :] * b[1, t, raw, :]
+
+    for copy in outer:
+        copy.wait()
+    for i, out in enumerate((ol, oh)):
+        rows, inner = s.rows[2 + i], s.inner[2 + i]
         out[0] = hat[:, rows, :]
-        out[1] = e[d, :, rows, :]
-        if d:
-            out[2] = v[0, :, rows, :]
-
+        for t in range(NT):
+            col = pl.ds(128 * t, 128)
+            out[1, t] = ve[i, :, col] * b[1, t, inner, :] - v[2, t, rows, :] * be[i, :, col]
+    for out, rows in zip((oa, ob), s.rows):
+        out[0] = hat[:, rows, :]
+        out[1] = e[1, :, rows, :]
+    ob[2] = v[0, :, s.rows[1], :]
+
+
+def rest_kernel(w0, vel, mag, visc, hat, b, v_in, e_in, v, e, vnew, f, src, inv, phi, nu, near,
+                ka, kb, kl, kh, mid, sem, visc_sem):
+    del v_in, e_in
+    chunks = [
+        columns(vel.at[1], ch, v.at[1], lambda t: sem.at[ch, t], PAD)
+        + columns(mag.at[1], ch, mid, lambda t: sem.at[ch, NT + t], 0)
+        for ch in range(CHUNKS)
+    ]
+    last = [
+        pltpu.make_async_copy(visc.at[:, pl.ds(128 * t, 128)], nu.at[t, pl.ds(PAD, CELLS)], visc_sem.at[t])
+        for t in range(NT)
+    ]
+    for copy in [copy for chunk in chunks for copy in chunk] + last:
+        copy.start()
+    f[1, :, 0:PAD, :] = jnp.zeros((NT, PAD, 128), F32)
+    fill_pads(phi)
+    fill_pads(nu)
+    for ch in range(CHUNKS):
+        for copy in chunks[ch]:
+            copy.wait()
+
+        @pl.loop(0, PER // 8, unroll=8)
+        def _(i):
+            raw = pl.ds(pl.multiple_of(ch * PER + i * 8, 8), 8)
+            at = pl.ds(pl.multiple_of(PAD + ch * PER + i * 8, 8), 8)
+            v0, v1, v2 = (v[c, :, at, :] for c in range(3))
+            b0, b1, b2 = b[0, :, raw, :], mid[:, raw, :], b[1, :, raw, :]
+            e1 = e[1, :, at, :]
+            e0, e2 = v1 * b2 - v2 * b1, v0 * b1 - v1 * b0
+            e[0, :, at, :] = e0
+            e[2, :, at, :] = e2
+            gain = (0.5 * force_gain) * recip(hat[:, at, :])
+            vnew[0, :, at, :] = gain * (e1 * b2 - e2 * b1)
+            vnew[1, :, at, :] = gain * (e2 * b0 - e0 * b2)
+            vnew[2, :, at, :] = gain * (e0 * b1 - e1 * b0)
+
+    faces(w0, hat, e, f, src, inv, phi)
+    s = Sides()
+    fields = [b.at[0], mid, b.at[1]]
     for i, k in enumerate((ka, kb, kl, kh)):
-        rows, at, d = sides.rows[i], sides.inner[i], sides.dims[i]
+        rows, at, d = s.rows[i], s.inner[i], s.dims[i]
         n1, n2 = (d + 1) % 3, (d + 2) % 3
-        g = (0.25 * force_gain * sides.signs[i]) * (sides.masks[i] * recip(hat[:, rows, :]))
-        k[0] = g * b[n2, :, at, :]
-        k[1] = -g * b[n1, :, at, :]
+        g = (0.25 * force_gain * s.signs[i]) * (s.masks[i] * recip(hat[:, rows, :]))
+        k[0] = g * fields[n2][:, at, :]
+        k[1] = -g * fields[n1][:, at, :]
+    for copy in last:
+        copy.wait()
+    for c in range(3):
+        near[c] = v[c, :, s.rows[0], :]
+    near[3] = nu[:, s.rows[0], :]
 
 
 def faces(w0, hat, e, f, src, inv, phi):
@@ -191,13 +245,13 @@
                 fy = jnp.where(sub == 7, 0.0, fy)
             else:
                 fym = jnp.where(sub == 0, 0.0, fym)
+            ez = e[2, :, at, :]
             fz = recip(c + z_up(c, OUTSIDE))
-            ez = e[2, :, at, :]
-            qz = fz * (ez + z_up(ez))
-            total = (qx - qxm[y]) + (fy * (ey + e[1, :, up, :]) - fym * (ey + e[1, :, down, :])) + (qz - z_down(qz))
-            diag = ((fx + fxm[y]) + (fy + fym)) + (fz + z_down(fz)) + 0.025 * recip(c)
-            source = 0.5 * total
-            inverse = recip(diag)
+            fzm = recip(c + z_down(c, OUTSIDE))
+            qy = fy * (ey + e[1, :, up, :]) - fym * (ey + e[1, :, down, :])
+            qz = fz * (ez + z_up(ez)) - fzm * (ez + z_down(ez))
+            source = 0.5 * (((qx - qxm[y]) + qy) + qz)
+            inverse = recip((((fx + fxm[y]) + (fy + fym)) + (fz + fzm)) + 0.025 * recip(c))
             f[0, :, at, :] = fx
             f[1, :, at, :] = fy
             f[2, :, at, :] = fz
@@ -216,56 +270,53 @@
     lax.fori_loop(0, NXL, body, start, unroll=8)
 
 
-def face_kernel(w0, hat, e, v, vnew, f, src, inv, phi):
-    del v, vnew
-    f[1, :, 0:PAD, :] = jnp.zeros((NT, PAD, 128), F32)
-    fill_pads(phi)
-    faces(w0, hat, e, f, src, inv, phi)
-
-
-SOURCE, INVERSE, BEHIND, FLOW = (pl.ds(i * NYL, NYL) for i in range(4))
-LINES = 4 * NYL
+SOURCE, INVERSE, BEHIND, *FLOW = (pl.ds(i * NYL, NYL) for i in range(6))
+LINES = 6 * NYL
 
 
 def flux_behind(phi, f, s, side):
     return f[0, :, s.face_behind[side], :] * phi[:, s.behind[side], :]
 
 
-def first_edge_kernel(w0, ha, hb, hl, hh, hat, e, v, f_in, src_in, inv_in, phi_in,
+def first_edge_kernel(w0, ha, hb, hl, hh, sa, sb, sl, sh, v, near, f_in, src_in, inv_in, phi_in,
                       f, src, inv, phi, ca, cb, cl, ch, oa, ob, ol, oh):
     del f_in, src_in, inv_in, phi_in
     s = Sides()
-    coefs = (ca, cb, cl, ch)
-    for pair in ((0, 1), (2, 3)):
-        got = []
-        for i in pair:
-            halo, rows, d = (ha, hb, hl, hh)[i], s.rows[i], s.dims[i]
-            g = s.masks[i] * recip(hat[:, rows, :] + halo[0])
-            q = (0.5 * s.signs[i]) * (g * (e[d, :, rows, :] + halo[1]))
-            got.append((i, rows, g, src[:, rows, :] + q, recip(recip(inv[:, rows, :]) + g)))
-        for i, rows, g, source, inverse in got:
-            coefs[i][...] = g
-            src[:, rows, :] = source
-            inv[:, rows, :] = inverse
-    for rows, coef in zip(s.face_in, (cl, ch)):
-        f[0, :, rows, :] = coef[...]
-    got = []
-    for i in range(4):
+    halos, sent, coefs = (ha, hb, hl, hh), (sa, sb, sl, sh), (ca, cb, cl, ch)
+
+    def add(i):
         rows = s.rows[i]
+        g = s.masks[i] * recip(sent[i][0] + halos[i][0])
+        source = src[:, rows, :] + (0.5 * s.signs[i]) * (g * (sent[i][1] + halos[i][1]))
+        return g, source, recip(recip(inv[:, rows, :]) + g)
+
+    got = [add(i) for i in (2, 3)]
+    for i, (g, source, inverse) in zip((2, 3), got):
+        rows = s.rows[i]
+        f[0, :, s.face_in[i - 2], :] = g
+        coefs[i][...] = g
+        src[:, rows, :] = source
+        inv[:, rows, :] = inverse
+        phi[:, rows, :] = (-w0) * (source * inverse)
+    got = [add(i) for i in (0, 1)]
+    for i, (g, source, inverse) in zip((0, 1), got):
+        rows = s.rows[i]
+        value = (-w0) * (source * inverse)
+        coefs[i][...] = g * inverse
+        src[:, rows, :] = source
+        inv[:, rows, :] = inverse
+        phi[:, rows, :] = value
+        (oa, ob)[i][0] = value
+    for c in range(3):
+        oa[1 + c] = near[c]
+    for i, (out, rows, x) in enumerate(zip((ol, oh), s.rows[2:], s.edge)):
         inverse = inv[:, rows, :]
-        got.append((i, rows, coefs[i][...] * inverse, (-w0) * (src[:, rows, :] * inverse)))
-    for i, rows, coef, value in got:
-        coefs[i][...] = coef
-        phi[:, rows, :] = value
-    for out, rows in zip((oa, ob), s.rows):
-        out[0] = phi[:, rows, :]
-    for c in range(1, 3):
-        oa[c] = v[c, :, s.rows[0], :]
-    for i, (out, rows, x) in enumerate(zip((ol, oh), s.rows[2:], s.edge)):
+        coefs[2 + i][...] = coefs[2 + i][...] * inverse
         out[:, SOURCE, :] = src[:, rows, :]
-        out[:, INVERSE, :] = inv[:, rows, :]
+        out[:, INVERSE, :] = inverse
         out[:, BEHIND, :] = flux_behind(phi, f, s, i)
-        out[:, FLOW, :] = v[0, :, rows, :]
+        for c in range(3):
+            out[:, FLOW[c], :] = v[c, :, rows, :]
         out[:, pl.ds(LINES, 8), :] = jnp.zeros(SHAPE, F32)
         for j, coef in enumerate((ca, cb)):
             out[:, pl.ds(LINES + j, 1), :] = coef[:, pl.ds(x, 1), :]
@@ -275,6 +326,7 @@
     got = [phi[:, r, :] + w * (c[...] * h) for c, h, r in zip(coefs, halos, rows)]
     for r, value in zip(rows, got):
         phi[:, r, :] = value
+    return got
 
 
 def wide_edge_kernel(w, w0, old, f, phi_in, ca, cb, cl, ch, rl, rh, kl, kh, ha, hb, *rest):
@@ -286,9 +338,8 @@
         beyond = [(h[0], h[1]) for h in rest[:2]]
     else:
         beyond = [((-w0) * (k[:, SOURCE, :] * k[:, INVERSE, :]), k[:, BEHIND, :]) for k in ks]
-    halves = ((ca, cb), (ha[0], hb[0])), ((cl, ch), (beyond[0][0], beyond[1][0]))
-    for (coefs, halos), rows in zip(halves, (s.rows[:2], s.rows[2:])):
-        add_sides(w, phi, coefs, halos, rows)
+    add_sides(w, phi, (cl, ch), (beyond[0][0], beyond[1][0]), s.rows[2:])
+    edges = add_sides(w, phi, (ca, cb), (ha[0], hb[0]), s.rows[:2])
     row = lax.broadcasted_iota(jnp.int32, (NT, NYL, 128), 1)
     for side, (r, k, (c, flux)) in enumerate(zip((rl, rh), ks, beyond)):
         hat = r[0]
@@ -298,33 +349,30 @@
         t = t + fy * pltpu.roll(c, NYL - 1, 1) + pltpu.roll(fy * c, 1, 1)
         t = t + fz * z_up(c) + z_down(fz * c)
         phi[:, s.beyond[side], :] = s.masks[2 + side] * (c + w * ((t - k[:, SOURCE, :]) * k[:, INVERSE, :] - c))
-    for out, rows, at in zip(outs, s.rows, (s.near, s.far)):
-        out[0, :, pl.ds(0, NXL), :] = phi[:, rows, :]
-        out[0, :, pl.ds(NXL, 8), :] = jnp.zeros(SHAPE, F32)
+    for out, values, at in zip(outs, edges, (s.near, s.far)):
+        out[0, :, pl.ds(0, NXL), :] = values
+        more = out.shape[2] - NXL
+        out[0, :, pl.ds(NXL, more), :] = jnp.zeros((NT, more, 128), F32)
         for side, (c, _) in enumerate(beyond):
             line = jnp.sum(jnp.where(row == at, c, 0.0), axis=1, keepdims=True)
             out[0, :, pl.ds(NXL + side, 1), :] = line
 
 
-def narrow_edge_kernel(w, w_before, f, v, nu, phi_in, ca, cb, cl, ch, kl, kh, ha, hb, phi, oa, ob, ol, oh):
+def narrow_edge_kernel(w, w_before, f, nu, near, phi_in, ca, cb, cl, ch, kl, kh, ha, hb, phi, oa, ob, ol, oh):
     del phi_in
     s = Sides()
-    inner = pl.ds(0, NXL)
-    add_sides(w, phi, (ca, cb), (ha[0, :, inner, :], hb[0, :, inner, :]), s.rows[:2])
     for j, (h, at) in enumerate(((ha, s.near), (hb, s.far))):
         for side, (k, c, plane) in enumerate(zip((kl, kh), (cl, ch), s.edge)):
             missing = w_before * (k[:, pl.ds(LINES + j, 1), :] * h[0, :, pl.ds(NXL + side, 1), :])
             row = pl.ds(PAD + plane * NYL + at, 1)
             phi[:, row, :] = phi[:, row, :] + w * (c[:, pl.ds(at, 1), :] * missing)
-    for out, rows in zip((oa, ob), s.rows):
-        out[0] = phi[:, rows, :]
-    oa[1] = nu[:, s.rows[0], :]
+    inner = pl.ds(0, NXL)
+    oa[0], ob[0] = add_sides(w, phi, (ca, cb), (ha[0, :, inner, :], hb[0, :, inner, :]), s.rows[:2])
+    oa[1] = near[3]
     for i, (out, rows) in enumerate(zip((ol, oh), s.rows[2:])):
         out[0] = phi[:, rows, :]
         out[1] = flux_behind(phi, f, s, i)
-        out[2] = v[1, :, rows, :]
-        out[3] = v[2, :, rows, :]
-        out[4] = nu[:, rows, :]
+        out[2] = nu[:, rows, :]
 
 
 def predictor(v, nu, vnew, x0, x1):
@@ -402,41 +450,20 @@
     sweep_kernel(w, phi, f, src, inv, out)
 
 
-def predict_kernel(planes, v, nu, vnew_in, vnew):
-    del vnew_in
-    predictor(v, nu, vnew, *planes)
-
-
 def sweep_predict_kernel(w, planes, phi, f, src, inv, v, nu, vnew_in, out, vnew):
     del vnew_in
     sweep_kernel(w, phi, f, src, inv, out)
     predictor(v, nu, vnew, *planes)
 
 
-def sweep_load_kernel(w, planes, phi, f, src, inv, v, visc, vnew_in, out, nu, vnew, sem):
-    del vnew_in
-    copies = [
-        pltpu.make_async_copy(visc.at[:, pl.ds(128 * t, 128)], nu.at[t, pl.ds(PAD, CELLS)], sem.at[t])
-        for t in range(NT)
-    ]
-    for copy in copies:
-        copy.start()
-    fill_pads(nu)
-    sweep_kernel(w, phi, f, src, inv, out)
-    for copy in copies:
-        copy.wait()
-    predictor(v, nu, vnew, *planes)
-
-
 def force_kernel(phi, hat, b, v, nu, *rest):
-    near0, far0, near1, near2, far, first_l, first_h, low, high = rest[:9]
+    far0, near, near_nu, far, *along = rest[:8]
     sent = (
-        (near0[2], near1[1], near1[2], near2[1]),
+        (near[1], near[2], near[3], near_nu[1]),
         (far0[2], far[0], far[1], far[2]),
-        (first_l[:, FLOW, :], low[2], low[3], low[4]),
-        (first_h[:, FLOW, :], high[2], high[3], high[4]),
-    )
-    potential, vnew, sem = rest[10:]
+        *((*(along[i][:, rows, :] for rows in FLOW), along[2 + i][2]) for i in range(2)),
+    )
+    potential, vnew, sem = rest[9:]
     copies = [
         pltpu.make_async_copy(phi.at[t, pl.ds(PAD, CELLS)], potential.at[:, pl.ds(128 * t, 128)], sem.at[t])
         for t in range(NT)
@@ -546,7 +573,7 @@
 FIELD = (NT, ROWS, 128)
 
 
-def run(kernel, name, ins, outs, aliases=None, scratch=(), flops=0, moved=0, limit=6 * MIB):
+def run(kernel, name, ins, outs, aliases=None, scratch=(), flops=0, moved=0, limit=4 * MIB):
     args = [in_hbm(a) if hbm else in_vmem(a) for a, hbm in ins]
     return pl.pallas_call(
         kernel,
@@ -571,7 +598,8 @@
 
 
 def across(a, b):
-    return lax.ppermute(a, "thick", [(0, 1), (1, 0)]), next_chip(b)
+    hb = next_chip(b)
+    return lax.ppermute(a, "thick", [(0, 1), (1, 0)]), hb
 
 
 def along(a, b):
@@ -580,10 +608,8 @@
     for i in range(n):
         j = ((i + 1) ^ 1) - 1
         second += [(i * m + k, j * m + k if 0 <= j < n else i * m + (k ^ 1)) for k in range(m)]
-    return (
-        lax.ppermute(a, "cast", [(i, i ^ 1) for i in range(n)]),
-        lax.ppermute(b, ("cast", *WIDTH), second),
-    )
+    hb = lax.ppermute(b, ("cast", *WIDTH), second)
+    return lax.ppermute(a, "cast", [(i, i ^ 1) for i in range(n)]), hb
 
 
 def rows_of(n, planes=NXL):
@@ -604,40 +630,45 @@
     field, fields = resident(*FIELD), resident(3, *FIELD)
     work = dict(flops=10_000_000, moved=16 * MIB)
 
-    v, hat, e, vnew, *edges = run(
+    v, b, hat, e, *edges = run(
         load_kernel, "load", [(vel, True), (mag, True), (lab, True)],
-        [fields, field, fields, fields] + rows_of(3) + planes_of(2) + rows_of(2) + planes_of(2),
+        [fields, resident(2, NT, CELLS, 128), field, fields, resident(2, NT, NXL, 128), resident(3, NT, NXL, 128)] + planes_of(2),
         scratch=[
-            pltpu.VMEM((3, NT, CELLS, 128), F32),
             pltpu.VMEM((CELLS, NT * 128), jnp.int32),
-            dma((CHUNKS, 2 * NT + 1)),
+            pltpu.VMEM((2, NYL, NT * 128), F32),
+            pltpu.VMEM((2, NYL, NT * 128), F32),
+            dma((CHUNKS, 4 * NT + 1)),
+            dma((2, 2)),
         ],
-        limit=10 * MIB,
-    )
-    edges, products = edges[:4], edges[4:]
+    )
     h1 = (*across(*edges[:2]), *along(*edges[2:]))
-    f, src, inv, phi = run(
-        functools.partial(face_kernel, w[0]), "faces", vm(hat, e, v, vnew), [fields, field, field, field], **work
+    v, e, vnew, f, src, inv, phi, nu, near, *products = run(
+        functools.partial(rest_kernel, w[0]), "faces",
+        [(vel, True), (mag, True), (visc, True)] + vm(hat, b, v, e),
+        [fields, fields, fields, fields, field, field, field, field, resident(4, NT, NXL, 128)]
+        + rows_of(2) + planes_of(2),
+        aliases={5: 0, 6: 1},
+        scratch=[pltpu.VMEM((NT, CELLS, 128), F32), dma((CHUNKS, 2 * NT)), dma((NT,))], **work,
     )
     f, src, inv, phi, *rest = run(
-        functools.partial(first_edge_kernel, w[0]), "edges1", vm(*h1, hat, e, v, f, src, inv, phi),
+        functools.partial(first_edge_kernel, w[0]), "edges1", vm(*h1, *edges, v, near, f, src, inv, phi),
         [fields] + [field] * 3 + [resident(NT, NXL, 128)] * 2 + [resident(NT, NYL, 128)] * 2
-        + [resident(3, NT, NXL, 128), resident(1, NT, NXL, 128)] + [resident(NT, LINES + 8, 128)] * 2,
-        aliases={7: 0, 8: 1, 9: 2, 10: 3},
+        + [resident(4, NT, NXL, 128), resident(1, NT, NXL, 128)] + [resident(NT, LINES + 8, 128)] * 2,
+        aliases={10: 0, 11: 1, 12: 2, 13: 3},
     )
     coefs, edges = rest[:4], rest[4:]
 
     h2 = (*across(*edges[:2]), *along(*edges[2:]))
     lines = h2[2:]
     old = phi
-    phi, nu, vnew = run(
-        functools.partial(sweep_load_kernel, w[1], (0, 24)), "sweep1",
-        vm(phi, f, src, inv, v) + [(visc, True)] + vm(vnew),
-        [field, field, fields], aliases={6: 2}, scratch=[dma((NT,))], **work,
+    phi, vnew = run(
+        functools.partial(sweep_predict_kernel, w[1], (0, 24)), "sweep1", vm(phi, f, src, inv, v, nu, vnew),
+        [field, fields], aliases={6: 1}, **work,
     )
     phi, *edges = run(
-        functools.partial(wide_edge_kernel, w[1], w[0]), "edges2", vm(old, f, phi, *coefs, *h1[2:], *lines, *h2[:2]),
-        [field] + rows_of(1, NXL + 8), aliases={2: 0},
+        functools.partial(wide_edge_kernel, w[1], w[0]), "edges2",
+        vm(old, f, phi, *coefs, *h1[2:], *lines, *h2[:2]),
+        [field, resident(1, NT, NXL + 8, 128), resident(1, NT, NXL + 16, 128)], aliases={2: 0},
     )
 
     h3 = across(*edges)
@@ -645,32 +676,29 @@
         functools.partial(sweep_flow_kernel, w[2]), "sweep2", vm(phi, f, src, inv, v, nu),
         [field, resident(3, NT, NXL, 128)], **work,
     )
-    (vnew,) = run(
-        functools.partial(predict_kernel, (24, 48)), "predict", vm(v, nu, vnew), [fields], aliases={2: 0}, **work
-    )
     flow = next_chip(flow)
     phi, *edges = run(
-        functools.partial(narrow_edge_kernel, w[2], w[1]), "edges3", vm(f, v, nu, phi, *coefs, *lines, *h3),
-        [field, resident(2, NT, NXL, 128), resident(1, NT, NXL, 128)] + planes_of(5), aliases={3: 0},
+        functools.partial(narrow_edge_kernel, w[2], w[1]), "edges3", vm(f, nu, near, phi, *coefs, *lines, *h3),
+        [field, resident(2, NT, NXL, 128), resident(1, NT, NXL, 128)] + planes_of(3), aliases={3: 0},
     )
 
     h4 = (*across(*edges[:2]), *along(*edges[2:]))
     old = phi
     phi, vnew = run(
-        functools.partial(sweep_predict_kernel, w[3], (48, 64)), "sweep3", vm(phi, f, src, inv, v, nu, vnew),
+        functools.partial(sweep_predict_kernel, w[3], (24, 64)), "sweep3", vm(phi, f, src, inv, v, nu, vnew),
         [field, fields], aliases={6: 1}, **work,
     )
     phi, *edges = run(
         functools.partial(wide_edge_kernel, w[3], None), "edges4",
         vm(old, f, phi, *coefs, *h1[2:], *lines, *h4, flow),
-        [field] + rows_of(1, NXL + 8), aliases={2: 0},
+        [field, resident(1, NT, NXL + 8, 128), resident(1, NT, NXL + 16, 128)], aliases={2: 0},
     )
 
     h5 = across(*edges)
     potential, vnew = run(
-        force_kernel, "force", vm(phi, hat, mag, v, nu, *h1[:2], h2[0], h4[0], flow, *lines, *h4[2:], vnew),
+        force_kernel, "force", vm(phi, hat, mag, v, nu, h1[1], h2[0], h4[0], flow, *lines, *h4[2:], vnew),
         [jax.ShapeDtypeStruct((CELLS, NT * 128), F32), fields],
-        aliases={14: 1}, scratch=[dma((NT,))], **work,
+        aliases={13: 1}, scratch=[dma((NT,))], **work,
     )
     result, _ = run(
         functools.partial(last_kernel, w[3]), "last", vm(*products, *lines, *h5, vnew),

time: 76.3 us -> 73.3 us (0.961)
  waiting for transfers between devices: 13.8 us -> 10.9 us
  Pallas kernels: 35.2 us -> 33 us
  starting transfers between devices: 26.3 us -> 28.4 us
    ppermute x6, waiting for transfers between devices: 12.5 us -> 7.54 us  [next_chip(): lax.ppermute(b, WIDTH, [(i, ((i + 1 ^ 1) - 1) % n) for i in range(n)])]
    ppermute x6, starting transfers between devices: 15.9 us -> 18.4 us  [next_chip(): lax.ppermute(b, WIDTH, [(i, ((i + 1 ^ 1) - 1) % n) for i in range(n)])]
    pallas_call x12 -> x11, Pallas kernels: 35.2 us -> 33 us  [run(): pl.pallas_call(kernel, out_shape=outs, in_specs=[IN_HBM if hbm else IN_VM...]
    ppermute x11, waiting for transfers between devices: 1.25 us -> 3.38 us  [the longest x3 3.36 us: along(): hb = lax.ppermute(b, ('cast', *WIDTH), second)]
  transfers between devices with their start and end apart: 17 -> 17, of which waited for: 5 -> 5; matrix products, arithmetic and copies ran while one was open for 0% -> 0% of each run, Pallas kernels for 29% -> 31%
where the time goes in v5:
time: 73.3 us; the launch traced here: 73.2 us
  Pallas kernels  33 us (45%)
  starting transfers between devices  28.4 us (39%)
  waiting for transfers between devices  10.9 us (15%)
  between operations  0.96 us (1%)
    pallas_call x11, Pallas kernels, run(): pl.pallas_call(kernel, out_shape=outs, in_specs=[IN_HBM if hbm else IN_VM...  33 us
    ppermute x6, starting transfers between devices, next_chip(): lax.ppermute(b, WIDTH, [(i, ((i + 1 ^ 1) - 1) % n) for i in range(n)])  18.4 us
    ppermute x3, starting transfers between devices, along(): hb = lax.ppermute(b, ('cast', *WIDTH), second)  7.78 us
    ppermute x6, waiting for transfers between devices, next_chip(): lax.ppermute(b, WIDTH, [(i, ((i + 1 ^ 1) - 1) % n) for i in range(n)])  7.54 us
    ppermute x3, waiting for transfers between devices, along(): hb = lax.ppermute(b, ('cast', *WIDTH), second)  3.36 us
    ppermute x3, starting transfers between devices, along(): return (lax.ppermute(a, 'cast', [(i, i ^ 1) for i in range(n)]), hb)  2.01 us
  transfers between devices with their start and end apart: 17, of which 5 were waited for; matrix products, arithmetic and copies ran while one was open for 0% of the time, Pallas kernels for 31%

profile of v5, /device:TPU:2, one launch (start us, length us, event | category | flops | bytes accessed | tf_op | source)
XLA Modules:
  0.0 73.2 jit_solution(15643679239659449697)
XLA Ops:
  0.6 5.3 %load.1 = (f32[3,4,1056,128]{3,2,1,0:T(8,128)S(1)}, f32[2,4,1024,128]{3,2,1,0:T(8,128)S(1)}, f32[4,1056,128]{2,1,0:T(8,128)S(1)}, f32[3,4,1056,128]{3,2,1,0:T(8,...) custom-call(f32[3,1024,512]{2,1,0:T(8,128)} %bitcast.11, ...), custom_call_target="tpu_custom_call" | custom-call | tf_op jit(solution)/shard_map/load/pallas_call | solution.py:578
  5.9 4.1 %collective-permute-start.1 = (f32[3,4,64,128]{3,2,1,0:T(8,128)S(1)}, f32[3,4,64,128]{3,2,1,0:T(8,128)S(1)}, u32[]{:S(2)}, u32[]{:S(2)}) collective-permute-start(f32[3,4,64,128]{3,2,1,0:T(8,128)S(1)} %get-tuple-element.63.sb), channel_id=1, source_target_pairs={{0,15},{1,2},{2,1},{3,4},{4,3},{5,6},{6,5},{7,8},{8,7},{9,10},{10,... | collective-permute-start | bytes 1179656 | tf_op jit(solution)/shard_map/ppermute | solution.py:597
  10.0 0.0 collective-permute-start
  10.0 1.9 %collective-permute-start.2 = (f32[2,4,16,128]{3,2,1,0:T(8,128)S(1)}, f32[2,4,16,128]{3,2,1,0:T(8,128)S(1)}, u32[]{:S(2)}, u32[]{:S(2)}) collective-permute-start(f32[2,4,16,128]{3,2,1,0:T(8,128)S(1)} %get-tuple-element.64.sl), channel_id=1, source_target_pairs={{0,16},{16,0},{32,48},{48,32},{64,80},{80,64},{96,112},{112,96},{1... | collective-permute-start | bytes 196616 | tf_op jit(solution)/shard_map/ppermute | solution.py:612
  11.9 3.4 %collective-permute-start.3 = (f32[2,4,16,128]{3,2,1,0:T(8,128)S(1)}, f32[2,4,16,128]{3,2,1,0:T(8,128)S(1)}, u32[]{:S(2)}, u32[]{:S(2)}) collective-permute-start(f32[2,4,16,128]{3,2,1,0:T(8,128)S(1)} %get-tuple-element.65.sh), channel_id=1, source_target_pairs={{0,1},{1,0},{2,3},{3,2},{4,5},{5,4},{6,7},{7,6},{8,9},{9,8},{10,11... | collective-permute-start | bytes 196616 | tf_op jit(solution)/shard_map/ppermute | solution.py:611
  15.3 7.7 %faces.1 = (f32[3,4,1056,128]{3,2,1,0:T(8,128)S(1)}, f32[3,4,1056,128]{3,2,1,0:T(8,128)S(1)}, f32[3,4,1056,128]{3,2,1,0:T(8,128)S(1)}, f32[3,4,1056,128]{3,2,1,0...) custom-call(f32[3,1024,512]{2,1,0:T(8,128)} %bitcast.12, ...), custom_call_target="tpu_custom_call", output_to_operand_aliasing={{0}: (5, {}), {1}: (6, {})} | custom-call | flops 10000000 | bytes 16777216 | tf_op jit(solution)/shard_map/faces/pallas_call | solution.py:578
  23.1 0.0 collective-permute-done.2.hl.rl
  23.1 0.7 %collective-permute-done.3.hh.rh = f32[2,4,16,128]{3,2,1,0:T(8,128)S(1)} collective-permute-done((f32[2,4,16,128]{3,2,1,0:T(8,128)S(1)}, f32[2,4,16,128]{3,2,1,0:T(8,128)S(1)}, u32[]{:S(2)}, u32[]{:S(2)}) %collective-permute-start.3) | collective-permute-done | bytes 65568 | tf_op jit(solution)/shard_map/ppermute | solution.py:611
  23.8 0.9 %edges1.1 = (f32[3,4,1056,128]{3,2,1,0:T(8,128)S(1)}, f32[4,1056,128]{2,1,0:T(8,128)S(1)}, f32[4,1056,128]{2,1,0:T(8,128)S(1)}, f32[4,1056,128]{2,1,0:T(8,128)S(...) custom-call(f32[2,4,64,128]{3,2,1,0:T(8,128)S(1)} %collective-permut, ...), custom_call_target="tpu_custom_call", output_to_operand_aliasing={{0}: (10, {}), {1}: (11, {}), {2}: (12, {}), {3}: (13, {})} | custom-call | tf_op jit(solution)/shard_map/edges1/pallas_call | solution.py:578
  24.8 0.1 collective-permute-start.6
  24.9 0.1 collective-permute-start.4
  25.0 1.3 %collective-permute-start.5 = (f32[4,104,128]{2,1,0:T(8,128)S(1)}, f32[4,104,128]{2,1,0:T(8,128)S(1)}, u32[]{:S(2)}, u32[]{:S(2)}) collective-permute-start(f32[4,104,128]{2,1,0:T(8,128)S(1)} %get-tuple-element.73), channel_id=1, source_target_pairs={{0,1},{1,0},{2,3},{3,2},{4,5},{5,4},{6,7},{7,6},{8,9},{9,8},{10,11... | collective-permute-start | bytes 638984 | tf_op jit(solution)/shard_map/ppermute | solution.py:611
  26.2 2.4 %collective-permute-start.7 = (f32[1,4,64,128]{3,2,1,0:T(8,128)S(1)}, f32[1,4,64,128]{3,2,1,0:T(8,128)S(1)}, u32[]{:S(2)}, u32[]{:S(2)}) collective-permute-start(f32[1,4,64,128]{3,2,1,0:T(8,128)S(1)} %get-tuple-element.86), channel_id=1, source_target_pairs={{0,15},{1,2},{2,1},{3,4},{4,3},{5,6},{6,5},{7,8},{8,7},{9,10},{10,... | collective-permute-start | bytes 393224 | tf_op jit(solution)/shard_map/ppermute | solution.py:597
  28.6 3.9 %sweep1.1 = (f32[4,1056,128]{2,1,0:T(8,128)S(1)}, f32[3,4,1056,128]{3,2,1,0:T(8,128)S(1)}) custom-call(f32[4,1056,128]{2,1,0:T(8,128)S(1)} %get-tuple-element.76.phi.old, f32[3,4,1056,128]{3,2,1,0:T(8,128)S(1)} %get-tuple-element.74.f, f32[4,1056,128]{2,1,0:T(8,128)S(1)} %get-tuple-element.77.src, ...), custom_call_target="tpu_custom_call", output_to_operand_aliasing={{1}: (6, {})} | custom-call | flops 10000000 | bytes 16777216 | tf_op jit(solution)/shard_map/sweep1/pallas_call | solution.py:578
  32.5 3.9 %collective-permute-done.7.hb = f32[1,4,64,128]{3,2,1,0:T(8,128)S(1)} collective-permute-done((f32[1,4,64,128]{3,2,1,0:T(8,128)S(1)}, f32[1,4,64,128]{3,2,1,0:T(8,128)S(1)}, u32[]{:S(2)}, u32[]{:S(2)}) %collective-permute-start.7) | collective-permute-done | bytes 131104 | tf_op jit(solution)/shard_map/ppermute | solution.py:597
  36.4 0.4 edges2.1
  36.9 3.1 %collective-permute-start.9 = (f32[1,4,80,128]{3,2,1,0:T(8,128)S(1)}, f32[1,4,80,128]{3,2,1,0:T(8,128)S(1)}, u32[]{:S(2)}, u32[]{:S(2)}) collective-permute-start(f32[1,4,80,128]{3,2,1,0:T(8,128)S(1)} %get-tuple-element.90), channel_id=1, source_target_pairs={{0,15},{1,2},{2,1},{3,4},{4,3},{5,6},{6,5},{7,8},{8,7},{9,10},{10,... | collective-permute-start | bytes 491528 | tf_op jit(solution)/shard_map/ppermute | solution.py:597
  39.9 2.0 %sweep2.1 = (f32[4,1056,128]{2,1,0:T(8,128)S(1)}, f32[3,4,64,128]{3,2,1,0:T(8,128)S(1)}) custom-call(f32[4,1056,128]{2,1,0:T(8,128)S(1)} %get-tuple-element.87.phi, f32[3,4,1056,128]{3,2,1,0:T(8,128)S(1)} %get-tuple-element.74.f, f32[4,1056,128]{2,1,0:T(8,128)S(1)} %get-tuple-element.77.src, f32[4,1056,128]{2,1,0:T(8,128)S(1)} %get-tuple-element.78.inv, ...), custom_call_target="tpu_custom_call" | custom-call | flops 10000000 | bytes 16777216 | tf_op jit(solution)/shard_map/sweep2/pallas_call | solution.py:578
  41.9 2.5 %collective-permute-start.14 = (f32[3,4,64,128]{3,2,1,0:T(8,128)S(1)}, f32[3,4,64,128]{3,2,1,0:T(8,128)S(1)}, u32[]{:S(2)}, u32[]{:S(2)}) collective-permute-start(f32[3,4,64,128]{3,2,1,0:T(8,128)S(1)} %get-tuple-element.98), channel_id=1, source_target_pairs={{0,15},{1,2},{2,1},{3,4},{4,3},{5,6},{6,5},{7,8},{8,7},{9,10},{10,... | collective-permute-start | bytes 1179656 | tf_op jit(solution)/shard_map/ppermute | solution.py:597
  44.4 1.7 %collective-permute-done.9.hb = f32[1,4,80,128]{3,2,1,0:T(8,128)S(1)} collective-permute-done((f32[1,4,80,128]{3,2,1,0:T(8,128)S(1)}, f32[1,4,80,128]{3,2,1,0:T(8,128)S(1)}, u32[]{:S(2)}, u32[]{:S(2)}) %collective-permute-start.9) | collective-permute-done | bytes 163872 | tf_op jit(solution)/shard_map/ppermute | solution.py:597
  46.1 0.4 edges3.1
  46.4 0.1 collective-permute-start.10
  46.5 2.3 %collective-permute-start.11 = (f32[1,4,64,128]{3,2,1,0:T(8,128)S(1)}, f32[1,4,64,128]{3,2,1,0:T(8,128)S(1)}, u32[]{:S(2)}, u32[]{:S(2)}) collective-permute-start(f32[1,4,64,128]{3,2,1,0:T(8,128)S(1)} %get-tuple-element.95), channel_id=1, source_target_pairs={{0,15},{1,2},{2,1},{3,4},{4,3},{5,6},{6,5},{7,8},{8,7},{9,10},{10,... | collective-permute-start | bytes 393224 | tf_op jit(solution)/shard_map/ppermute | solution.py:597
  48.8 3.1 %collective-permute-start.13 = (f32[3,4,16,128]{3,2,1,0:T(8,128)S(1)}, f32[3,4,16,128]{3,2,1,0:T(8,128)S(1)}, u32[]{:S(2)}, u32[]{:S(2)}) collective-permute-start(f32[3,4,16,128]{3,2,1,0:T(8,128)S(1)} %get-tuple-element.97), channel_id=1, source_target_pairs={{0,1},{1,0},{2,3},{3,2},{4,5},{5,4},{6,7},{7,6},{8,9},{9,8},{10,11... | collective-permute-start | bytes 294920 | tf_op jit(solution)/shard_map/ppermute | solution.py:611
  52.0 5.2 %sweep3.1 = (f32[4,1056,128]{2,1,0:T(8,128)S(1)}, f32[3,4,1056,128]{3,2,1,0:T(8,128)S(1)}) custom-call(f32[4,1056,128]{2,1,0:T(8,128)S(1)} %get-tuple-element.91.phi.old, f32[3,4,1056,128]{3,2,1,0:T(8,128)S(1)} %get-tuple-element.74.f, f32[4,1056,128]{2,1,0:T(8,128)S(1)} %get-tuple-element.77.src, ...), custom_call_target="tpu_custom_call", output_to_operand_aliasing={{1}: (6, {})} | custom-call | flops 10000000 | bytes 16777216 | tf_op jit(solution)/shard_map/sweep3/pallas_call | solution.py:578
  57.2 2.6 %collective-permute-done.13.rest_1_.rest_7_ = f32[3,4,16,128]{3,2,1,0:T(8,128)S(1)} collective-permute-done((f32[3,4,16,128]{3,2,1,0:T(8,128)S(1)}, f32[3,4,16,128]{3,2,1,0:T(8,128)S(1)}, u32[]{:S(2)}, u32[]{:S(2)}) %collective-permute-start.13) | collective-permute-done | bytes 98336 | tf_op jit(solution)/shard_map/ppermute | solution.py:611
  59.9 0.0 slice-start
  59.9 0.4 edges4.1
  60.3 4.1 %collective-permute-start.16 = (f32[1,4,80,128]{3,2,1,0:T(8,128)S(1)}, f32[1,4,80,128]{3,2,1,0:T(8,128)S(1)}, u32[]{:S(2)}, u32[]{:S(2)}) collective-permute-start(f32[1,4,80,128]{3,2,1,0:T(8,128)S(1)} %get-tuple-element.100), channel_id=1, source_target_pairs={{0,15},{1,2},{2,1},{3,4},{4,3},{5,6},{6,5},{7,8},{8,7},{9,10},{10,... | collective-permute-start | bytes 491528 | tf_op jit(solution)/shard_map/ppermute | solution.py:597
  64.5 3.7 %force.1 = (f32[1024,512]{1,0:T(8,128)}, f32[3,4,1056,128]{3,2,1,0:T(8,128)S(1)}) custom-call(f32[4,1056,128]{2,1,0:T(8,128)S(1)} %get-tuple-element.101.phi, f32[4,1056,128]{2,1,0:T(8,128)S(1)} %get-tuple-element.54.hat, f32[3,1024,512]{2,1,0:T(8,128)S(1)} %bitcast.10, ...), custom_call_target="tpu_custom_call", output_to_operand_aliasing={{1}: (13, {})} | custom-call | flops 10000000 | bytes 16777216 | tf_op jit(solution)/shard_map/force/pallas_call | solution.py:578
  68.2 1.9 %collective-permute-done.16.hb = f32[1,4,80,128]{3,2,1,0:T(8,128)S(1)} collective-permute-done((f32[1,4,80,128]{3,2,1,0:T(8,128)S(1)}, f32[1,4,80,128]{3,2,1,0:T(8,128)S(1)}, u32[]{:S(2)}, u32[]{:S(2)}) %collective-permute-start.16) | collective-permute-done | bytes 163872 | tf_op jit(solution)/shard_map/ppermute | solution.py:597
  70.1 2.9 %last.1 = (f32[3,1024,512]{2,1,0:T(8,128)}, f32[3,4,1056,128]{3,2,1,0:T(8,128)S(1)}) custom-call(f32[2,4,64,128]{3,2,1,0:T(8,128)S(1)} %get-tuple-element.58.ka, f32[2,4,64,128]{3,2,1,0:T(8,128)S(1)} %get-tuple-element.59.kb, f32[2,4,16,128]{3,2,1,0:T(8,128)S(1)} %get-tuple-element.60.kl, ...), custom_call_target="tpu_custom_call", output_to_operand_aliasing={{1}: (8, {})} | custom-call | tf_op jit(solution)/shard_map/last/pallas_call | solution.py:578
  (18 shorter events, 0.0 us)
Async XLA Ops:
  5.9 17.9 %collective-permute-start.1 = (f32[3,4,64,128]{3,2,1,0:T(8,128)S(1)}, f32[3,4,64,128]{3,2,1,0:T(8,128)S(1)}, u32[]{:S(2)}, u32[]{:S(2)}) collective-permute-start(f32[3,4,64,128]{3,2,1,0:T(8,128)S(1)} %get-tuple-element.63.sb), channel_id=1, source_target_pairs={{0,15},{1,2},{2,1},{3,4},{4,3},{5,6},{6,5},{7,8},{8,7},{9,10},{10,... | collective-permute-start | bytes 1179656 | tf_op jit(solution)/shard_map/ppermute | solution.py:597
  10.0 13.8 %collective-permute-start = (f32[2,4,64,128]{3,2,1,0:T(8,128)S(1)}, f32[2,4,64,128]{3,2,1,0:T(8,128)S(1)}, u32[]{:S(2)}, u32[]{:S(2)}) collective-permute-start(f32[2,4,64,128]{3,2,1,0:T(8,128)S(1)} %get-tuple-element.62.sa), channel_id=1, source_target_pairs={{0,1},{1,0},{2,3},{3,2},{4,5},{5,4},{6,7},{7,6},{8,9},{9,8},{10,11... | collective-permute-start | bytes 786440 | tf_op jit(solution)/shard_map/ppermute | solution.py:602
  10.0 13.1 %collective-permute-start.2 = (f32[2,4,16,128]{3,2,1,0:T(8,128)S(1)}, f32[2,4,16,128]{3,2,1,0:T(8,128)S(1)}, u32[]{:S(2)}, u32[]{:S(2)}) collective-permute-start(f32[2,4,16,128]{3,2,1,0:T(8,128)S(1)} %get-tuple-element.64.sl), channel_id=1, source_target_pairs={{0,16},{16,0},{32,48},{48,32},{64,80},{80,64},{96,112},{112,96},{1... | collective-permute-start | bytes 196616 | tf_op jit(solution)/shard_map/ppermute | solution.py:612
  11.9 11.9 %collective-permute-start.3 = (f32[2,4,16,128]{3,2,1,0:T(8,128)S(1)}, f32[2,4,16,128]{3,2,1,0:T(8,128)S(1)}, u32[]{:S(2)}, u32[]{:S(2)}) collective-permute-start(f32[2,4,16,128]{3,2,1,0:T(8,128)S(1)} %get-tuple-element.65.sh), channel_id=1, source_target_pairs={{0,1},{1,0},{2,3},{3,2},{4,5},{5,4},{6,7},{7,6},{8,9},{9,8},{10,11... | collective-permute-start | bytes 196616 | tf_op jit(solution)/shard_map/ppermute | solution.py:611
  24.8 11.6 %collective-permute-start.6 = (f32[4,4,64,128]{3,2,1,0:T(8,128)S(1)}, f32[4,4,64,128]{3,2,1,0:T(8,128)S(1)}, u32[]{:S(2)}, u32[]{:S(2)}) collective-permute-start(f32[4,4,64,128]{3,2,1,0:T(8,128)S(1)} %get-tuple-element.85), channel_id=1, source_target_pairs={{0,1},{1,0},{2,3},{3,2},{4,5},{5,4},{6,7},{7,6},{8,9},{9,8},{10,11... | collective-permute-start | bytes 1572872 | tf_op jit(solution)/shard_map/ppermute | solution.py:602
  24.9 11.5 %collective-permute-start.4 = (f32[4,104,128]{2,1,0:T(8,128)S(1)}, f32[4,104,128]{2,1,0:T(8,128)S(1)}, u32[]{:S(2)}, u32[]{:S(2)}) collective-permute-start(f32[4,104,128]{2,1,0:T(8,128)S(1)} %get-tuple-element.72), channel_id=1, source_target_pairs={{0,16},{16,0},{32,48},{48,32},{64,80},{80,64},{96,112},{112,96},{1... | collective-permute-start | bytes 638984 | tf_op jit(solution)/shard_map/ppermute | solution.py:612
  25.0 11.5 %collective-permute-start.5 = (f32[4,104,128]{2,1,0:T(8,128)S(1)}, f32[4,104,128]{2,1,0:T(8,128)S(1)}, u32[]{:S(2)}, u32[]{:S(2)}) collective-permute-start(f32[4,104,128]{2,1,0:T(8,128)S(1)} %get-tuple-element.73), channel_id=1, source_target_pairs={{0,1},{1,0},{2,3},{3,2},{4,5},{5,4},{6,7},{7,6},{8,9},{9,8},{10,11... | collective-permute-start | bytes 638984 | tf_op jit(solution)/shard_map/ppermute | solution.py:611
  26.2 10.2 %collective-permute-start.7 = (f32[1,4,64,128]{3,2,1,0:T(8,128)S(1)}, f32[1,4,64,128]{3,2,1,0:T(8,128)S(1)}, u32[]{:S(2)}, u32[]{:S(2)}) collective-permute-start(f32[1,4,64,128]{3,2,1,0:T(8,128)S(1)} %get-tuple-element.86), channel_id=1, source_target_pairs={{0,15},{1,2},{2,1},{3,4},{4,3},{5,6},{6,5},{7,8},{8,7},{9,10},{10,... | collective-permute-start | bytes 393224 | tf_op jit(solution)/shard_map/ppermute | solution.py:597
  36.9 9.2 %collective-permute-start.9 = (f32[1,4,80,128]{3,2,1,0:T(8,128)S(1)}, f32[1,4,80,128]{3,2,1,0:T(8,128)S(1)}, u32[]{:S(2)}, u32[]{:S(2)}) collective-permute-start(f32[1,4,80,128]{3,2,1,0:T(8,128)S(1)} %get-tuple-element.90), channel_id=1, source_target_pairs={{0,15},{1,2},{2,1},{3,4},{4,3},{5,6},{6,5},{7,8},{8,7},{9,10},{10,... | collective-permute-start | bytes 491528 | tf_op jit(solution)/shard_map/ppermute | solution.py:597
  39.9 4.5 %collective-permute-start.8 = (f32[1,4,72,128]{3,2,1,0:T(8,128)S(1)}, f32[1,4,72,128]{3,2,1,0:T(8,128)S(1)}, u32[]{:S(2)}, u32[]{:S(2)}) collective-permute-start(f32[1,4,72,128]{3,2,1,0:T(8,128)S(1)} %get-tuple-element.89), channel_id=1, source_target_pairs={{0,1},{1,0},{2,3},{3,2},{4,5},{5,4},{6,7},{7,6},{8,9},{9,8},{10,11... | collective-permute-start | bytes 442376 | tf_op jit(solution)/shard_map/ppermute | solution.py:602
  41.9 17.9 %collective-permute-start.14 = (f32[3,4,64,128]{3,2,1,0:T(8,128)S(1)}, f32[3,4,64,128]{3,2,1,0:T(8,128)S(1)}, u32[]{:S(2)}, u32[]{:S(2)}) collective-permute-start(f32[3,4,64,128]{3,2,1,0:T(8,128)S(1)} %get-tuple-element.98), channel_id=1, source_target_pairs={{0,15},{1,2},{2,1},{3,4},{4,3},{5,6},{6,5},{7,8},{8,7},{9,10},{10,... | collective-permute-start | bytes 1179656 | tf_op jit(solution)/shard_map/ppermute | solution.py:597
  46.4 13.4 %collective-permute-start.10 = (f32[2,4,64,128]{3,2,1,0:T(8,128)S(1)}, f32[2,4,64,128]{3,2,1,0:T(8,128)S(1)}, u32[]{:S(2)}, u32[]{:S(2)}) collective-permute-start(f32[2,4,64,128]{3,2,1,0:T(8,128)S(1)} %get-tuple-element.94), channel_id=1, source_target_pairs={{0,1},{1,0},{2,3},{3,2},{4,5},{5,4},{6,7},{7,6},{8,9},{9,8},{10,11... | collective-permute-start | bytes 786440 | tf_op jit(solution)/shard_map/ppermute | solution.py:602
  46.5 13.3 %collective-permute-start.11 = (f32[1,4,64,128]{3,2,1,0:T(8,128)S(1)}, f32[1,4,64,128]{3,2,1,0:T(8,128)S(1)}, u32[]{:S(2)}, u32[]{:S(2)}) collective-permute-start(f32[1,4,64,128]{3,2,1,0:T(8,128)S(1)} %get-tuple-element.95), channel_id=1, source_target_pairs={{0,15},{1,2},{2,1},{3,4},{4,3},{5,6},{6,5},{7,8},{8,7},{9,10},{10,... | collective-permute-start | bytes 393224 | tf_op jit(solution)/shard_map/ppermute | solution.py:597
  48.8 8.4 %collective-permute-start.12 = (f32[3,4,16,128]{3,2,1,0:T(8,128)S(1)}, f32[3,4,16,128]{3,2,1,0:T(8,128)S(1)}, u32[]{:S(2)}, u32[]{:S(2)}) collective-permute-start(f32[3,4,16,128]{3,2,1,0:T(8,128)S(1)} %get-tuple-element.96), channel_id=1, source_target_pairs={{0,16},{16,0},{32,48},{48,32},{64,80},{80,64},{96,112},{112,96},{1... | collective-permute-start | bytes 294920 | tf_op jit(solution)/shard_map/ppermute | solution.py:612
  48.8 11.0 %collective-permute-start.13 = (f32[3,4,16,128]{3,2,1,0:T(8,128)S(1)}, f32[3,4,16,128]{3,2,1,0:T(8,128)S(1)}, u32[]{:S(2)}, u32[]{:S(2)}) collective-permute-start(f32[3,4,16,128]{3,2,1,0:T(8,128)S(1)} %get-tuple-element.97), channel_id=1, source_target_pairs={{0,1},{1,0},{2,3},{3,2},{4,5},{5,4},{6,7},{7,6},{8,9},{9,8},{10,11... | collective-permute-start | bytes 294920 | tf_op jit(solution)/shard_map/ppermute | solution.py:611
  59.9 4.6 %slice-start = ((s8[6291456]{0:T(1024)(128)(4,1)}), s8[4194304]{0:T(1024)(128)(4,1)S(1)}, s32[]{:S(2)}) async-start(s8[6291456]{0:T(1024)(128)(4,1)} %bitcast.8), calls=%async_computation | async-start | bytes 8388608
  59.9 4.6 %slice-start.1 = ((s8[6291456]{0:T(1024)(128)(4,1)}), s8[2097152]{0:T(1024)(128)(4,1)S(1)}, s32[]{:S(2)}) async-start(s8[6291456]{0:T(1024)(128)(4,1)} %bitcast.8), calls=%async_computation.1 | async-start | bytes 4194304
  60.3 9.8 %collective-permute-start.16 = (f32[1,4,80,128]{3,2,1,0:T(8,128)S(1)}, f32[1,4,80,128]{3,2,1,0:T(8,128)S(1)}, u32[]{:S(2)}, u32[]{:S(2)}) collective-permute-start(f32[1,4,80,128]{3,2,1,0:T(8,128)S(1)} %get-tuple-element.100), channel_id=1, source_target_pairs={{0,15},{1,2},{2,1},{3,4},{4,3},{5,6},{6,5},{7,8},{8,7},{9,10},{10,... | collective-permute-start | bytes 491528 | tf_op jit(solution)/shard_map/ppermute | solution.py:597
  64.4 3.8 %collective-permute-start.15 = (f32[1,4,72,128]{3,2,1,0:T(8,128)S(1)}, f32[1,4,72,128]{3,2,1,0:T(8,128)S(1)}, u32[]{:S(2)}, u32[]{:S(2)}) collective-permute-start(f32[1,4,72,128]{3,2,1,0:T(8,128)S(1)} %get-tuple-element.99), channel_id=1, source_target_pairs={{0,1},{1,0},{2,3},{3,2},{4,5},{5,4},{6,7},{7,6},{8,9},{9,8},{10,11... | collective-permute-start | bytes 442376 | tf_op jit(solution)/shard_map/ppermute | solution.py:602

commit v6 on v5

--- a/solution.py
+++ b/solution.py
@@ -414,8 +414,9 @@
                 vnew[c, :, at, :] = vnew[c, :, at, :] + (half * acc + keep * vc[c])
 
 
-def sweep_kernel(w, phi, f, src, inv, out):
-    fill_pads(out)
+def sweep_kernel(w, phi, f, src, inv, out, x0=0, x1=NXL):
+    if x0 == 0:
+        fill_pads(out)
 
     def body(x, carry):
         pxm, pc = carry
@@ -437,9 +438,12 @@
             out[:, at, :] = c + w * ((t - src[:, at, :]) * inv[:, at, :] - c)
         return tuple(px), tuple(pn)
 
-    before = tuple(f[0, :, pl.ds(8 * y, 8), :] * phi[:, pl.ds(8 * y, 8), :] for y in range(2))
-    start = (before, tuple(phi[:, pl.ds(PAD + 8 * y, 8), :] for y in range(2)))
-    lax.fori_loop(0, NXL, body, start, unroll=16)
+    before = tuple(f[0, :, pl.ds(x0 * NYL + 8 * y, 8), :] * phi[:, pl.ds(x0 * NYL + 8 * y, 8), :] for y in range(2))
+    start = (before, tuple(phi[:, pl.ds(PAD + x0 * NYL + 8 * y, 8), :] for y in range(2)))
+    lax.fori_loop(x0, x1, body, start, unroll=min(16, x1 - x0))
+
+
+CUT = 16
 
 
 def sweep_flow_kernel(w, phi, f, src, inv, v, nu, out, flow):
@@ -447,7 +451,12 @@
     flow[0] = v[1, :, rows, :]
     flow[1] = v[2, :, rows, :]
     flow[2] = nu[:, rows, :]
-    sweep_kernel(w, phi, f, src, inv, out)
+    sweep_kernel(w, phi, f, src, inv, out, 0, CUT)
+
+
+def sweep_end_kernel(w, phi, f, src, inv, out_in, out):
+    del out_in
+    sweep_kernel(w, phi, f, src, inv, out, CUT, NXL)
 
 
 def sweep_predict_kernel(w, planes, phi, f, src, inv, v, nu, vnew_in, out, vnew):
@@ -463,7 +472,7 @@
         (far0[2], far[0], far[1], far[2]),
         *((*(along[i][:, rows, :] for rows in FLOW), along[2 + i][2]) for i in range(2)),
     )
-    potential, vnew, sem = rest[9:]
+    potential, result, vnew, sem, out_sem = rest[9:]
     copies = [
         pltpu.make_async_copy(phi.at[t, pl.ds(PAD, CELLS)], potential.at[:, pl.ds(128 * t, 128)], sem.at[t])
         for t in range(NT)
@@ -488,33 +497,47 @@
                 vnew[c, :, s.rows[i], :] = values[c]
 
     sub = sublanes()
-    @pl.loop(0, NXL, unroll=8)
-    def _(x):
-        r = row_of(x)
-        for y in range(2):
-            base = r + 8 * y
-            at = pl.ds(base, 8)
-            raw = pl.ds(pl.multiple_of(x * NYL + 8 * y, 8), 8)
-            p = phi[:, at, :]
-            yu = phi[:, pl.ds(base + 1, 8), :]
-            yd = phi[:, pl.ds(base - 1, 8), :]
-            if y == 1:
-                yu = jnp.where(sub == 7, 0.0, yu)
-            else:
-                yd = jnp.where(sub == 0, 0.0, yd)
-            diffs = (
-                phi[:, pl.ds(base + NYL, 8), :] - phi[:, pl.ds(base - NYL, 8), :],
-                yu - yd,
-                z_up(p) - z_down(p),
+    for ch in range(CHUNKS):
+
+        @pl.loop(ch * (NXL // CHUNKS), (ch + 1) * (NXL // CHUNKS), unroll=8)
+        def _(x):
+            r = row_of(x)
+            for y in range(2):
+                base = r + 8 * y
+                at = pl.ds(base, 8)
+                raw = pl.ds(pl.multiple_of(x * NYL + 8 * y, 8), 8)
+                p = phi[:, at, :]
+                yu = phi[:, pl.ds(base + 1, 8), :]
+                yd = phi[:, pl.ds(base - 1, 8), :]
+                if y == 1:
+                    yu = jnp.where(sub == 7, 0.0, yu)
+                else:
+                    yd = jnp.where(sub == 0, 0.0, yd)
+                diffs = (
+                    phi[:, pl.ds(base + NYL, 8), :] - phi[:, pl.ds(base - NYL, 8), :],
+                    yu - yd,
+                    z_up(p) - z_down(p),
+                )
+                g = (-0.25 * force_gain) * recip(hat[:, at, :])
+                c0, c1, c2 = (g * diff for diff in diffs)
+                for t in range(NT):
+                    b0, b1, b2 = (b[c, raw, pl.ds(128 * t, 128)] for c in range(3))
+                    vnew[0, t, at, :] = vnew[0, t, at, :] + (c1[t] * b2 - c2[t] * b1)
+                    vnew[1, t, at, :] = vnew[1, t, at, :] + (c2[t] * b0 - c0[t] * b2)
+                    vnew[2, t, at, :] = vnew[2, t, at, :] + (c0[t] * b1 - c1[t] * b0)
+
+        if ch == CHUNKS - 1:
+            break
+        low = ch * PER + (NYL if ch == 0 else 0)
+        some = (ch + 1) * PER - low
+        for t in range(NT):
+            copy = pltpu.make_async_copy(
+                vnew.at[1, t, pl.ds(PAD + low, some)],
+                result.at[1, pl.ds(low, some), pl.ds(128 * t, 128)],
+                out_sem.at[ch, t],
             )
-            g = (-0.25 * force_gain) * recip(hat[:, at, :])
-            c0, c1, c2 = (g * diff for diff in diffs)
-            for t in range(NT):
-                b0, b1, b2 = (b[c, raw, pl.ds(128 * t, 128)] for c in range(3))
-                vnew[0, t, at, :] = vnew[0, t, at, :] + (c1[t] * b2 - c2[t] * b1)
-                vnew[1, t, at, :] = vnew[1, t, at, :] + (c2[t] * b0 - c0[t] * b2)
-                vnew[2, t, at, :] = vnew[2, t, at, :] + (c0[t] * b1 - c1[t] * b0)
-
+            copy.start()
+            copies.append(copy)
     for copy in copies:
         copy.wait()
 
@@ -522,8 +545,8 @@
 PARTS = 4
 
 
-def last_kernel(w, ka, kb, kl, kh, cl, ch, ha, hb, vnew_in, result, vnew, sem):
-    del vnew_in
+def last_kernel(w, ka, kb, kl, kh, cl, ch, ha, hb, vnew_in, result_in, result, vnew, sem, edge_sem):
+    del vnew_in, result_in
     planes = NXL // PARTS
     copies = []
     s = Sides()
@@ -533,6 +556,15 @@
             row = pl.ds(PAD + plane * NYL + at, 1)
             for i, c in enumerate((1, 2)):
                 vnew[c, :, row, :] = vnew[c, :, row, :] + k[i, :, pl.ds(at, 1), :] * missing
+    for i, (low, some) in enumerate(((0, NYL), ((CHUNKS - 1) * PER, PER))):
+        for t in range(NT):
+            copy = pltpu.make_async_copy(
+                vnew.at[1, t, pl.ds(PAD + low, some)],
+                result.at[1, pl.ds(low, some), pl.ds(128 * t, 128)],
+                edge_sem.at[i, t],
+            )
+            copy.start()
+            copies.append(copy)
     for part in range(PARTS):
         s = Sides(part * planes, planes)
         some = pl.ds(part * planes, planes)
@@ -543,14 +575,15 @@
         for c, rows, value in got:
             vnew[c, :, rows, :] = value
         per = planes * NYL
-        for t in range(NT):
-            copy = pltpu.make_async_copy(
-                vnew.at[:, t, pl.ds(PAD + part * per, per)],
-                result.at[:, pl.ds(part * per, per), pl.ds(128 * t, 128)],
-                sem.at[part, t],
-            )
-            copy.start()
-            copies.append(copy)
+        for c in (0, 2):
+            for t in range(NT):
+                copy = pltpu.make_async_copy(
+                    vnew.at[c, t, pl.ds(PAD + part * per, per)],
+                    result.at[c, pl.ds(part * per, per), pl.ds(128 * t, 128)],
+                    sem.at[part, c // 2, t],
+                )
+                copy.start()
+                copies.append(copy)
     for copy in copies:
         copy.wait()
 
@@ -672,9 +705,12 @@
     )
 
     h3 = across(*edges)
-    phi, flow = run(
+    half, flow = run(
         functools.partial(sweep_flow_kernel, w[2]), "sweep2", vm(phi, f, src, inv, v, nu),
         [field, resident(3, NT, NXL, 128)], **work,
+    )
+    (phi,) = run(
+        functools.partial(sweep_end_kernel, w[2]), "rest2", vm(phi, f, src, inv, half), [field], aliases={4: 0}, **work
     )
     flow = next_chip(flow)
     phi, *edges = run(
@@ -695,15 +731,15 @@
     )
 
     h5 = across(*edges)
-    potential, vnew = run(
+    potential, result, vnew = run(
         force_kernel, "force", vm(phi, hat, mag, v, nu, h1[1], h2[0], h4[0], flow, *lines, *h4[2:], vnew),
-        [jax.ShapeDtypeStruct((CELLS, NT * 128), F32), fields],
-        aliases={13: 1}, scratch=[dma((NT,))], **work,
+        [jax.ShapeDtypeStruct((CELLS, NT * 128), F32), jax.ShapeDtypeStruct((3, CELLS, NT * 128), F32), fields],
+        aliases={13: 2}, scratch=[dma((NT,)), dma((CHUNKS - 1, NT))], **work,
     )
     result, _ = run(
-        functools.partial(last_kernel, w[3]), "last", vm(*products, *lines, *h5, vnew),
+        functools.partial(last_kernel, w[3]), "last", vm(*products, *lines, *h5, vnew) + [(result, True)],
         [jax.ShapeDtypeStruct((3, CELLS, NT * 128), F32), fields],
-        aliases={8: 1}, scratch=[dma((PARTS, NT))],
+        aliases={8: 1, 9: 0}, scratch=[dma((PARTS, 2, NT)), dma((2, NT))],
     )
     return result.reshape(velocity.shape), potential.reshape(labels.shape)
 

time: 73.3 us -> 72.6 us (level)
  waiting for transfers between devices: 10.9 us -> 9.97 us
    ppermute x3, waiting for transfers between devices: 3.36 us -> 1.94 us  [along(): hb = lax.ppermute(b, ('cast', *WIDTH), second)]
    pallas_call x11 -> x12, Pallas kernels: 33 us -> 32.9 us  [run(): pl.pallas_call(kernel, out_shape=outs, in_specs=[IN_HBM if hbm else IN_VM...]
  transfers between devices with their start and end apart: 17 -> 17, of which waited for: 5 -> 5; matrix products, arithmetic and copies ran while one was open for 0% -> 0% of each run, Pallas kernels for 31% -> 32%
where the time goes in v6:
time: 72.6 us; the launch traced here: 72.5 us
  Pallas kernels  32.9 us (45%)
  starting transfers between devices  28.4 us (39%)
  waiting for transfers between devices  9.97 us (14%)
  between operations  0.99 us (1%)
    pallas_call x12, Pallas kernels, run(): pl.pallas_call(kernel, out_shape=outs, in_specs=[IN_HBM if hbm else IN_VM...  32.9 us
    ppermute x6, starting transfers between devices, next_chip(): lax.ppermute(b, WIDTH, [(i, ((i + 1 ^ 1) - 1) % n) for i in range(n)])  18.4 us
    ppermute x6, waiting for transfers between devices, next_chip(): lax.ppermute(b, WIDTH, [(i, ((i + 1 ^ 1) - 1) % n) for i in range(n)])  8.01 us
    ppermute x3, starting transfers between devices, along(): hb = lax.ppermute(b, ('cast', *WIDTH), second)  7.79 us
    ppermute x3, starting transfers between devices, along(): return (lax.ppermute(a, 'cast', [(i, i ^ 1) for i in range(n)]), hb)  2.01 us
    ppermute x3, waiting for transfers between devices, along(): hb = lax.ppermute(b, ('cast', *WIDTH), second)  1.94 us
  transfers between devices with their start and end apart: 17, of which 5 were waited for; matrix products, arithmetic and copies ran while one was open for 0% of the time, Pallas kernels for 32%

profile of v6, /device:TPU:2, one launch (start us, length us, event | category | flops | bytes accessed | tf_op | source)
XLA Modules:
  0.0 72.5 jit_solution(3653459733797379291)
XLA Ops:
  0.6 5.3 %load.1 = (f32[3,4,1056,128]{3,2,1,0:T(8,128)S(1)}, f32[2,4,1024,128]{3,2,1,0:T(8,128)S(1)}, f32[4,1056,128]{2,1,0:T(8,128)S(1)}, f32[3,4,1056,128]{3,2,1,0:T(8,...) custom-call(f32[3,1024,512]{2,1,0:T(8,128)} %bitcast.11, ...), custom_call_target="tpu_custom_call" | custom-call | tf_op jit(solution)/shard_map/load/pallas_call | solution.py:611
  5.9 4.1 %collective-permute-start.1 = (f32[3,4,64,128]{3,2,1,0:T(8,128)S(1)}, f32[3,4,64,128]{3,2,1,0:T(8,128)S(1)}, u32[]{:S(2)}, u32[]{:S(2)}) collective-permute-start(f32[3,4,64,128]{3,2,1,0:T(8,128)S(1)} %get-tuple-element.64.sb), channel_id=1, source_target_pairs={{0,15},{1,2},{2,1},{3,4},{4,3},{5,6},{6,5},{7,8},{8,7},{9,10},{10,... | collective-permute-start | bytes 1179656 | tf_op jit(solution)/shard_map/ppermute | solution.py:630
  10.0 1.9 %collective-permute-start.2 = (f32[2,4,16,128]{3,2,1,0:T(8,128)S(1)}, f32[2,4,16,128]{3,2,1,0:T(8,128)S(1)}, u32[]{:S(2)}, u32[]{:S(2)}) collective-permute-start(f32[2,4,16,128]{3,2,1,0:T(8,128)S(1)} %get-tuple-element.65.sl), channel_id=1, source_target_pairs={{0,16},{16,0},{32,48},{48,32},{64,80},{80,64},{96,112},{112,96},{1... | collective-permute-start | bytes 196616 | tf_op jit(solution)/shard_map/ppermute | solution.py:645
  11.9 3.4 %collective-permute-start.3 = (f32[2,4,16,128]{3,2,1,0:T(8,128)S(1)}, f32[2,4,16,128]{3,2,1,0:T(8,128)S(1)}, u32[]{:S(2)}, u32[]{:S(2)}) collective-permute-start(f32[2,4,16,128]{3,2,1,0:T(8,128)S(1)} %get-tuple-element.66.sh), channel_id=1, source_target_pairs={{0,1},{1,0},{2,3},{3,2},{4,5},{5,4},{6,7},{7,6},{8,9},{9,8},{10,11... | collective-permute-start | bytes 196616 | tf_op jit(solution)/shard_map/ppermute | solution.py:644
  15.3 7.7 %faces.1 = (f32[3,4,1056,128]{3,2,1,0:T(8,128)S(1)}, f32[3,4,1056,128]{3,2,1,0:T(8,128)S(1)}, f32[3,4,1056,128]{3,2,1,0:T(8,128)S(1)}, f32[3,4,1056,128]{3,2,1,0...) custom-call(f32[3,1024,512]{2,1,0:T(8,128)} %bitcast.12, ...), custom_call_target="tpu_custom_call", output_to_operand_aliasing={{0}: (5, {}), {1}: (6, {})} | custom-call | flops 10000000 | bytes 16777216 | tf_op jit(solution)/shard_map/faces/pallas_call | solution.py:611
  23.1 0.7 %collective-permute-done.3.hh.rh = f32[2,4,16,128]{3,2,1,0:T(8,128)S(1)} collective-permute-done((f32[2,4,16,128]{3,2,1,0:T(8,128)S(1)}, f32[2,4,16,128]{3,2,1,0:T(8,128)S(1)}, u32[]{:S(2)}, u32[]{:S(2)}) %collective-permute-start.3) | collective-permute-done | bytes 65568 | tf_op jit(solution)/shard_map/ppermute | solution.py:644
  23.8 0.9 %edges1.1 = (f32[3,4,1056,128]{3,2,1,0:T(8,128)S(1)}, f32[4,1056,128]{2,1,0:T(8,128)S(1)}, f32[4,1056,128]{2,1,0:T(8,128)S(1)}, f32[4,1056,128]{2,1,0:T(8,128)S(...) custom-call(f32[2,4,64,128]{3,2,1,0:T(8,128)S(1)} %collective-permut, ...), custom_call_target="tpu_custom_call", output_to_operand_aliasing={{0}: (10, {}), {1}: (11, {}), {2}: (12, {}), {3}: (13, {})} | custom-call | tf_op jit(solution)/shard_map/edges1/pallas_call | solution.py:611
  24.8 0.1 collective-permute-start.6
  24.9 0.1 collective-permute-start.4
  25.0 1.3 %collective-permute-start.5 = (f32[4,104,128]{2,1,0:T(8,128)S(1)}, f32[4,104,128]{2,1,0:T(8,128)S(1)}, u32[]{:S(2)}, u32[]{:S(2)}) collective-permute-start(f32[4,104,128]{2,1,0:T(8,128)S(1)} %get-tuple-element.74), channel_id=1, source_target_pairs={{0,1},{1,0},{2,3},{3,2},{4,5},{5,4},{6,7},{7,6},{8,9},{9,8},{10,11... | collective-permute-start | bytes 638984 | tf_op jit(solution)/shard_map/ppermute | solution.py:644
  26.2 2.4 %collective-permute-start.7 = (f32[1,4,64,128]{3,2,1,0:T(8,128)S(1)}, f32[1,4,64,128]{3,2,1,0:T(8,128)S(1)}, u32[]{:S(2)}, u32[]{:S(2)}) collective-permute-start(f32[1,4,64,128]{3,2,1,0:T(8,128)S(1)} %get-tuple-element.87), channel_id=1, source_target_pairs={{0,15},{1,2},{2,1},{3,4},{4,3},{5,6},{6,5},{7,8},{8,7},{9,10},{10,... | collective-permute-start | bytes 393224 | tf_op jit(solution)/shard_map/ppermute | solution.py:630
  28.6 3.9 %sweep1.1 = (f32[4,1056,128]{2,1,0:T(8,128)S(1)}, f32[3,4,1056,128]{3,2,1,0:T(8,128)S(1)}) custom-call(f32[4,1056,128]{2,1,0:T(8,128)S(1)} %get-tuple-element.77.phi.old, f32[3,4,1056,128]{3,2,1,0:T(8,128)S(1)} %get-tuple-element.75.f, f32[4,1056,128]{2,1,0:T(8,128)S(1)} %get-tuple-element.78.src, ...), custom_call_target="tpu_custom_call", output_to_operand_aliasing={{1}: (6, {})} | custom-call | flops 10000000 | bytes 16777216 | tf_op jit(solution)/shard_map/sweep1/pallas_call | solution.py:611
  32.5 3.9 %collective-permute-done.7.hb = f32[1,4,64,128]{3,2,1,0:T(8,128)S(1)} collective-permute-done((f32[1,4,64,128]{3,2,1,0:T(8,128)S(1)}, f32[1,4,64,128]{3,2,1,0:T(8,128)S(1)}, u32[]{:S(2)}, u32[]{:S(2)}) %collective-permute-start.7) | collective-permute-done | bytes 131104 | tf_op jit(solution)/shard_map/ppermute | solution.py:630
  36.4 0.4 edges2.1
  36.9 3.1 %collective-permute-start.9 = (f32[1,4,80,128]{3,2,1,0:T(8,128)S(1)}, f32[1,4,80,128]{3,2,1,0:T(8,128)S(1)}, u32[]{:S(2)}, u32[]{:S(2)}) collective-permute-start(f32[1,4,80,128]{3,2,1,0:T(8,128)S(1)} %get-tuple-element.91), channel_id=1, source_target_pairs={{0,15},{1,2},{2,1},{3,4},{4,3},{5,6},{6,5},{7,8},{8,7},{9,10},{10,... | collective-permute-start | bytes 491528 | tf_op jit(solution)/shard_map/ppermute | solution.py:630
  39.9 0.6 sweep2.1
  40.6 2.5 %collective-permute-start.14 = (f32[3,4,64,128]{3,2,1,0:T(8,128)S(1)}, f32[3,4,64,128]{3,2,1,0:T(8,128)S(1)}, u32[]{:S(2)}, u32[]{:S(2)}) collective-permute-start(f32[3,4,64,128]{3,2,1,0:T(8,128)S(1)} %get-tuple-element.99), channel_id=1, source_target_pairs={{0,15},{1,2},{2,1},{3,4},{4,3},{5,6},{6,5},{7,8},{8,7},{9,10},{10,... | collective-permute-start | bytes 1179656 | tf_op jit(solution)/shard_map/ppermute | solution.py:630
  43.1 1.3 %rest2.1.phi_in = f32[4,1056,128]{2,1,0:T(8,128)S(1)} custom-call(f32[4,1056,128]{2,1,0:T(8,128)S(1)} %get-tuple-element.88.phi, f32[3,4,1056,128]{3,2,1,0:T(8,128)S(1)} %get-tuple-element.75.f, f32[4,1056,128]{2,1,0:T(8,128)S(1)} %get-tuple-element.78.src, f32[4,1056,128]{2,1,0:T(8,128)S(1)} %get-tuple-element.79.inv, ...), custom_call_target="tpu_custom_call", output_to_operand_aliasing={{}: (4, {})} | custom-call | flops 10000000 | bytes 16777216 | tf_op jit(solution)/shard_map/rest2/pallas_call | solution.py:611
  44.4 1.7 %collective-permute-done.9.hb = f32[1,4,80,128]{3,2,1,0:T(8,128)S(1)} collective-permute-done((f32[1,4,80,128]{3,2,1,0:T(8,128)S(1)}, f32[1,4,80,128]{3,2,1,0:T(8,128)S(1)}, u32[]{:S(2)}, u32[]{:S(2)}) %collective-permute-start.9) | collective-permute-done | bytes 163872 | tf_op jit(solution)/shard_map/ppermute | solution.py:630
  46.1 0.4 edges3.1
  46.4 0.1 collective-permute-start.10
  46.5 3.6 %collective-permute-start.11 = (f32[1,4,64,128]{3,2,1,0:T(8,128)S(1)}, f32[1,4,64,128]{3,2,1,0:T(8,128)S(1)}, u32[]{:S(2)}, u32[]{:S(2)}) collective-permute-start(f32[1,4,64,128]{3,2,1,0:T(8,128)S(1)} %get-tuple-element.96), channel_id=1, source_target_pairs={{0,15},{1,2},{2,1},{3,4},{4,3},{5,6},{6,5},{7,8},{8,7},{9,10},{10,... | collective-permute-start | bytes 393224 | tf_op jit(solution)/shard_map/ppermute | solution.py:630
  50.1 3.1 %collective-permute-start.13 = (f32[3,4,16,128]{3,2,1,0:T(8,128)S(1)}, f32[3,4,16,128]{3,2,1,0:T(8,128)S(1)}, u32[]{:S(2)}, u32[]{:S(2)}) collective-permute-start(f32[3,4,16,128]{3,2,1,0:T(8,128)S(1)} %get-tuple-element.98), channel_id=1, source_target_pairs={{0,1},{1,0},{2,3},{3,2},{4,5},{5,4},{6,7},{7,6},{8,9},{9,8},{10,11... | collective-permute-start | bytes 294920 | tf_op jit(solution)/shard_map/ppermute | solution.py:644
  53.2 5.2 %sweep3.1 = (f32[4,1056,128]{2,1,0:T(8,128)S(1)}, f32[3,4,1056,128]{3,2,1,0:T(8,128)S(1)}) custom-call(f32[4,1056,128]{2,1,0:T(8,128)S(1)} %get-tuple-element.92.phi.old, f32[3,4,1056,128]{3,2,1,0:T(8,128)S(1)} %get-tuple-element.75.f, f32[4,1056,128]{2,1,0:T(8,128)S(1)} %get-tuple-element.78.src, ...), custom_call_target="tpu_custom_call", output_to_operand_aliasing={{1}: (6, {})} | custom-call | flops 10000000 | bytes 16777216 | tf_op jit(solution)/shard_map/sweep3/pallas_call | solution.py:611
  58.5 1.2 %collective-permute-done.13.rest_1_.rest_7_ = f32[3,4,16,128]{3,2,1,0:T(8,128)S(1)} collective-permute-done((f32[3,4,16,128]{3,2,1,0:T(8,128)S(1)}, f32[3,4,16,128]{3,2,1,0:T(8,128)S(1)}, u32[]{:S(2)}, u32[]{:S(2)}) %collective-permute-start.13) | collective-permute-done | bytes 98336 | tf_op jit(solution)/shard_map/ppermute | solution.py:644
  59.7 0.0 slice-start
  59.8 0.4 edges4.1
  60.2 2.9 %collective-permute-start.16 = (f32[1,4,80,128]{3,2,1,0:T(8,128)S(1)}, f32[1,4,80,128]{3,2,1,0:T(8,128)S(1)}, u32[]{:S(2)}, u32[]{:S(2)}) collective-permute-start(f32[1,4,80,128]{3,2,1,0:T(8,128)S(1)} %get-tuple-element.101), channel_id=1, source_target_pairs={{0,15},{1,2},{2,1},{3,4},{4,3},{5,6},{6,5},{7,8},{8,7},{9,10},{10,... | collective-permute-start | bytes 491528 | tf_op jit(solution)/shard_map/ppermute | solution.py:630
  63.1 0.1 copy-done.1
  63.2 4.1 %force.1 = (f32[1024,512]{1,0:T(8,128)}, f32[3,1024,512]{2,1,0:T(8,128)}, f32[3,4,1056,128]{3,2,1,0:T(8,128)S(1)}) custom-call(f32[4,1056,128]{2,1,0:T(8,128)S(1)} %get-tuple-element.102.phi, f32[4,1056,128]{2,1,0:T(8,128)S(1)} %copy-done.1, f32[3,1024,512]{2,1,0:T(8,128)S(1)} %bitcast.10, ...), custom_call_target="tpu_custom_call", output_to_operand_aliasing={{2}: (13, {})} | custom-call | flops 10000000 | bytes 16777216 | tf_op jit(solution)/shard_map/force/pallas_call | solution.py:611
  67.4 2.4 %collective-permute-done.16.hb = f32[1,4,80,128]{3,2,1,0:T(8,128)S(1)} collective-permute-done((f32[1,4,80,128]{3,2,1,0:T(8,128)S(1)}, f32[1,4,80,128]{3,2,1,0:T(8,128)S(1)}, u32[]{:S(2)}, u32[]{:S(2)}) %collective-permute-start.16) | collective-permute-done | bytes 163872 | tf_op jit(solution)/shard_map/ppermute | solution.py:630
  69.8 2.5 %last.1 = (f32[3,1024,512]{2,1,0:T(8,128)}, f32[3,4,1056,128]{3,2,1,0:T(8,128)S(1)}) custom-call(f32[2,4,64,128]{3,2,1,0:T(8,128)S(1)} %get-tuple-element.59.ka, f32[2,4,64,128]{3,2,1,0:T(8,128)S(1)} %get-tuple-element.60.kb, f32[2,4,16,128]{3,2,1,0:T(8,128)S(1)} %get-tuple-element.61.kl, ...), custom_call_target="tpu_custom_call", output_to_operand_aliasing={{1}: (8, {}), {0}: (9, {})} | custom-call | tf_op jit(solution)/shard_map/last/pallas_call | solution.py:611
  (23 shorter events, 0.1 us)
Async XLA Ops:
  5.9 17.2 %copy-start = (f32[4,1056,128]{2,1,0:T(8,128)}, f32[4,1056,128]{2,1,0:T(8,128)S(1)}, u32[]{:S(2)}) copy-start(f32[4,1056,128]{2,1,0:T(8,128)S(1)} %get-tuple-element.55.hat) | copy-start | bytes 6488068
  5.9 17.9 %collective-permute-start.1 = (f32[3,4,64,128]{3,2,1,0:T(8,128)S(1)}, f32[3,4,64,128]{3,2,1,0:T(8,128)S(1)}, u32[]{:S(2)}, u32[]{:S(2)}) collective-permute-start(f32[3,4,64,128]{3,2,1,0:T(8,128)S(1)} %get-tuple-element.64.sb), channel_id=1, source_target_pairs={{0,15},{1,2},{2,1},{3,4},{4,3},{5,6},{6,5},{7,8},{8,7},{9,10},{10,... | collective-permute-start | bytes 1179656 | tf_op jit(solution)/shard_map/ppermute | solution.py:630
  10.0 13.8 %collective-permute-start = (f32[2,4,64,128]{3,2,1,0:T(8,128)S(1)}, f32[2,4,64,128]{3,2,1,0:T(8,128)S(1)}, u32[]{:S(2)}, u32[]{:S(2)}) collective-permute-start(f32[2,4,64,128]{3,2,1,0:T(8,128)S(1)} %get-tuple-element.63.sa), channel_id=1, source_target_pairs={{0,1},{1,0},{2,3},{3,2},{4,5},{5,4},{6,7},{7,6},{8,9},{9,8},{10,11... | collective-permute-start | bytes 786440 | tf_op jit(solution)/shard_map/ppermute | solution.py:635
  10.0 13.1 %collective-permute-start.2 = (f32[2,4,16,128]{3,2,1,0:T(8,128)S(1)}, f32[2,4,16,128]{3,2,1,0:T(8,128)S(1)}, u32[]{:S(2)}, u32[]{:S(2)}) collective-permute-start(f32[2,4,16,128]{3,2,1,0:T(8,128)S(1)} %get-tuple-element.65.sl), channel_id=1, source_target_pairs={{0,16},{16,0},{32,48},{48,32},{64,80},{80,64},{96,112},{112,96},{1... | collective-permute-start | bytes 196616 | tf_op jit(solution)/shard_map/ppermute | solution.py:645
  11.9 11.9 %collective-permute-start.3 = (f32[2,4,16,128]{3,2,1,0:T(8,128)S(1)}, f32[2,4,16,128]{3,2,1,0:T(8,128)S(1)}, u32[]{:S(2)}, u32[]{:S(2)}) collective-permute-start(f32[2,4,16,128]{3,2,1,0:T(8,128)S(1)} %get-tuple-element.66.sh), channel_id=1, source_target_pairs={{0,1},{1,0},{2,3},{3,2},{4,5},{5,4},{6,7},{7,6},{8,9},{9,8},{10,11... | collective-permute-start | bytes 196616 | tf_op jit(solution)/shard_map/ppermute | solution.py:644
  24.8 11.6 %collective-permute-start.6 = (f32[4,4,64,128]{3,2,1,0:T(8,128)S(1)}, f32[4,4,64,128]{3,2,1,0:T(8,128)S(1)}, u32[]{:S(2)}, u32[]{:S(2)}) collective-permute-start(f32[4,4,64,128]{3,2,1,0:T(8,128)S(1)} %get-tuple-element.86), channel_id=1, source_target_pairs={{0,1},{1,0},{2,3},{3,2},{4,5},{5,4},{6,7},{7,6},{8,9},{9,8},{10,11... | collective-permute-start | bytes 1572872 | tf_op jit(solution)/shard_map/ppermute | solution.py:635
  24.9 11.5 %collective-permute-start.4 = (f32[4,104,128]{2,1,0:T(8,128)S(1)}, f32[4,104,128]{2,1,0:T(8,128)S(1)}, u32[]{:S(2)}, u32[]{:S(2)}) collective-permute-start(f32[4,104,128]{2,1,0:T(8,128)S(1)} %get-tuple-element.73), channel_id=1, source_target_pairs={{0,16},{16,0},{32,48},{48,32},{64,80},{80,64},{96,112},{112,96},{1... | collective-permute-start | bytes 638984 | tf_op jit(solution)/shard_map/ppermute | solution.py:645
  25.0 11.5 %collective-permute-start.5 = (f32[4,104,128]{2,1,0:T(8,128)S(1)}, f32[4,104,128]{2,1,0:T(8,128)S(1)}, u32[]{:S(2)}, u32[]{:S(2)}) collective-permute-start(f32[4,104,128]{2,1,0:T(8,128)S(1)} %get-tuple-element.74), channel_id=1, source_target_pairs={{0,1},{1,0},{2,3},{3,2},{4,5},{5,4},{6,7},{7,6},{8,9},{9,8},{10,11... | collective-permute-start | bytes 638984 | tf_op jit(solution)/shard_map/ppermute | solution.py:644
  26.2 10.2 %collective-permute-start.7 = (f32[1,4,64,128]{3,2,1,0:T(8,128)S(1)}, f32[1,4,64,128]{3,2,1,0:T(8,128)S(1)}, u32[]{:S(2)}, u32[]{:S(2)}) collective-permute-start(f32[1,4,64,128]{3,2,1,0:T(8,128)S(1)} %get-tuple-element.87), channel_id=1, source_target_pairs={{0,15},{1,2},{2,1},{3,4},{4,3},{5,6},{6,5},{7,8},{8,7},{9,10},{10,... | collective-permute-start | bytes 393224 | tf_op jit(solution)/shard_map/ppermute | solution.py:630
  36.9 9.2 %collective-permute-start.9 = (f32[1,4,80,128]{3,2,1,0:T(8,128)S(1)}, f32[1,4,80,128]{3,2,1,0:T(8,128)S(1)}, u32[]{:S(2)}, u32[]{:S(2)}) collective-permute-start(f32[1,4,80,128]{3,2,1,0:T(8,128)S(1)} %get-tuple-element.91), channel_id=1, source_target_pairs={{0,15},{1,2},{2,1},{3,4},{4,3},{5,6},{6,5},{7,8},{8,7},{9,10},{10,... | collective-permute-start | bytes 491528 | tf_op jit(solution)/shard_map/ppermute | solution.py:630
  39.9 4.5 %collective-permute-start.8 = (f32[1,4,72,128]{3,2,1,0:T(8,128)S(1)}, f32[1,4,72,128]{3,2,1,0:T(8,128)S(1)}, u32[]{:S(2)}, u32[]{:S(2)}) collective-permute-start(f32[1,4,72,128]{3,2,1,0:T(8,128)S(1)} %get-tuple-element.90), channel_id=1, source_target_pairs={{0,1},{1,0},{2,3},{3,2},{4,5},{5,4},{6,7},{7,6},{8,9},{9,8},{10,11... | collective-permute-start | bytes 442376 | tf_op jit(solution)/shard_map/ppermute | solution.py:635
  40.6 19.1 %collective-permute-start.14 = (f32[3,4,64,128]{3,2,1,0:T(8,128)S(1)}, f32[3,4,64,128]{3,2,1,0:T(8,128)S(1)}, u32[]{:S(2)}, u32[]{:S(2)}) collective-permute-start(f32[3,4,64,128]{3,2,1,0:T(8,128)S(1)} %get-tuple-element.99), channel_id=1, source_target_pairs={{0,15},{1,2},{2,1},{3,4},{4,3},{5,6},{6,5},{7,8},{8,7},{9,10},{10,... | collective-permute-start | bytes 1179656 | tf_op jit(solution)/shard_map/ppermute | solution.py:630
  46.4 13.3 %collective-permute-start.10 = (f32[2,4,64,128]{3,2,1,0:T(8,128)S(1)}, f32[2,4,64,128]{3,2,1,0:T(8,128)S(1)}, u32[]{:S(2)}, u32[]{:S(2)}) collective-permute-start(f32[2,4,64,128]{3,2,1,0:T(8,128)S(1)} %get-tuple-element.95), channel_id=1, source_target_pairs={{0,1},{1,0},{2,3},{3,2},{4,5},{5,4},{6,7},{7,6},{8,9},{9,8},{10,11... | collective-permute-start | bytes 786440 | tf_op jit(solution)/shard_map/ppermute | solution.py:635
  46.5 13.2 %collective-permute-start.11 = (f32[1,4,64,128]{3,2,1,0:T(8,128)S(1)}, f32[1,4,64,128]{3,2,1,0:T(8,128)S(1)}, u32[]{:S(2)}, u32[]{:S(2)}) collective-permute-start(f32[1,4,64,128]{3,2,1,0:T(8,128)S(1)} %get-tuple-element.96), channel_id=1, source_target_pairs={{0,15},{1,2},{2,1},{3,4},{4,3},{5,6},{6,5},{7,8},{8,7},{9,10},{10,... | collective-permute-start | bytes 393224 | tf_op jit(solution)/shard_map/ppermute | solution.py:630
  50.1 8.4 %collective-permute-start.12 = (f32[3,4,16,128]{3,2,1,0:T(8,128)S(1)}, f32[3,4,16,128]{3,2,1,0:T(8,128)S(1)}, u32[]{:S(2)}, u32[]{:S(2)}) collective-permute-start(f32[3,4,16,128]{3,2,1,0:T(8,128)S(1)} %get-tuple-element.97), channel_id=1, source_target_pairs={{0,16},{16,0},{32,48},{48,32},{64,80},{80,64},{96,112},{112,96},{1... | collective-permute-start | bytes 294920 | tf_op jit(solution)/shard_map/ppermute | solution.py:645
  50.1 9.6 %collective-permute-start.13 = (f32[3,4,16,128]{3,2,1,0:T(8,128)S(1)}, f32[3,4,16,128]{3,2,1,0:T(8,128)S(1)}, u32[]{:S(2)}, u32[]{:S(2)}) collective-permute-start(f32[3,4,16,128]{3,2,1,0:T(8,128)S(1)} %get-tuple-element.98), channel_id=1, source_target_pairs={{0,1},{1,0},{2,3},{3,2},{4,5},{5,4},{6,7},{7,6},{8,9},{9,8},{10,11... | collective-permute-start | bytes 294920 | tf_op jit(solution)/shard_map/ppermute | solution.py:644
  59.7 3.4 %slice-start = ((s8[6291456]{0:T(1024)(128)(4,1)}), s8[4194304]{0:T(1024)(128)(4,1)S(1)}, s32[]{:S(2)}) async-start(s8[6291456]{0:T(1024)(128)(4,1)} %bitcast.8), calls=%async_computation | async-start | bytes 8388608
  59.7 3.4 %slice-start.1 = ((s8[6291456]{0:T(1024)(128)(4,1)}), s8[2097152]{0:T(1024)(128)(4,1)S(1)}, s32[]{:S(2)}) async-start(s8[6291456]{0:T(1024)(128)(4,1)} %bitcast.8), calls=%async_computation.1 | async-start | bytes 4194304
  59.7 3.5 %copy-start.1 = (f32[4,1056,128]{2,1,0:T(8,128)S(1)}, f32[4,1056,128]{2,1,0:T(8,128)}, u32[]{:S(2)}) copy-start(f32[4,1056,128]{2,1,0:T(8,128)} %copy-done) | copy-start | bytes 6488068
  60.2 9.6 %collective-permute-start.16 = (f32[1,4,80,128]{3,2,1,0:T(8,128)S(1)}, f32[1,4,80,128]{3,2,1,0:T(8,128)S(1)}, u32[]{:S(2)}, u32[]{:S(2)}) collective-permute-start(f32[1,4,80,128]{3,2,1,0:T(8,128)S(1)} %get-tuple-element.101), channel_id=1, source_target_pairs={{0,15},{1,2},{2,1},{3,4},{4,3},{5,6},{6,5},{7,8},{8,7},{9,10},{10,... | collective-permute-start | bytes 491528 | tf_op jit(solution)/shard_map/ppermute | solution.py:630
  63.1 4.3 %collective-permute-start.15 = (f32[1,4,72,128]{3,2,1,0:T(8,128)S(1)}, f32[1,4,72,128]{3,2,1,0:T(8,128)S(1)}, u32[]{:S(2)}, u32[]{:S(2)}) collective-permute-start(f32[1,4,72,128]{3,2,1,0:T(8,128)S(1)} %get-tuple-element.100), channel_id=1, source_target_pairs={{0,1},{1,0},{2,3},{3,2},{4,5},{5,4},{6,7},{7,6},{8,9},{9,8},{10,11... | collective-permute-start | bytes 442376 | tf_op jit(solution)/shard_map/ppermute | solution.py:635

commit v7 on v6

--- a/solution.py
+++ b/solution.py
@@ -443,7 +443,7 @@
     lax.fori_loop(x0, x1, body, start, unroll=min(16, x1 - x0))
 
 
-CUT = 16
+CUT = 8
 
 
 def sweep_flow_kernel(w, phi, f, src, inv, v, nu, out, flow):
@@ -695,7 +695,7 @@
     lines = h2[2:]
     old = phi
     phi, vnew = run(
-        functools.partial(sweep_predict_kernel, w[1], (0, 24)), "sweep1", vm(phi, f, src, inv, v, nu, vnew),
+        functools.partial(sweep_predict_kernel, w[1], (0, 40)), "sweep1", vm(phi, f, src, inv, v, nu, vnew),
         [field, fields], aliases={6: 1}, **work,
     )
     phi, *edges = run(
@@ -721,7 +721,7 @@
     h4 = (*across(*edges[:2]), *along(*edges[2:]))
     old = phi
     phi, vnew = run(
-        functools.partial(sweep_predict_kernel, w[3], (24, 64)), "sweep3", vm(phi, f, src, inv, v, nu, vnew),
+        functools.partial(sweep_predict_kernel, w[3], (40, 64)), "sweep3", vm(phi, f, src, inv, v, nu, vnew),
         [field, fields], aliases={6: 1}, **work,
     )
     phi, *edges = run(

time: 72.6 us -> 72.3 us (level)
  waiting for transfers between devices: 9.97 us -> 9.08 us
    ppermute x6, waiting for transfers between devices: 8.01 us -> 5.87 us  [next_chip(): lax.ppermute(b, WIDTH, [(i, ((i + 1 ^ 1) - 1) % n) for i in range(n)])]
    ppermute x3, waiting for transfers between devices: 1.94 us -> 3.18 us  [along(): hb = lax.ppermute(b, ('cast', *WIDTH), second)]
  transfers between devices with their start and end apart: 17 -> 17, of which waited for: 5 -> 5; matrix products, arithmetic and copies ran while one was open for 0% -> 0% of each run, Pallas kernels for 32% -> 33%
where the time goes in v7:
time: 72.3 us; the launch traced here: 72.2 us
  Pallas kernels  33.4 us (46%)
  starting transfers between devices  28.4 us (39%)
  waiting for transfers between devices  9.08 us (13%)
  between operations  0.99 us (1%)
    pallas_call x12, Pallas kernels, run(): pl.pallas_call(kernel, out_shape=outs, in_specs=[IN_HBM if hbm else IN_VM...  33.4 us
    ppermute x6, starting transfers between devices, next_chip(): lax.ppermute(b, WIDTH, [(i, ((i + 1 ^ 1) - 1) % n) for i in range(n)])  18.4 us
    ppermute x3, starting transfers between devices, along(): hb = lax.ppermute(b, ('cast', *WIDTH), second)  7.78 us
    ppermute x6, waiting for transfers between devices, next_chip(): lax.ppermute(b, WIDTH, [(i, ((i + 1 ^ 1) - 1) % n) for i in range(n)])  5.87 us
    ppermute x3, waiting for transfers between devices, along(): hb = lax.ppermute(b, ('cast', *WIDTH), second)  3.18 us
    ppermute x3, starting transfers between devices, along(): return (lax.ppermute(a, 'cast', [(i, i ^ 1) for i in range(n)]), hb)  2.01 us
  transfers between devices with their start and end apart: 17, of which 5 were waited for; matrix products, arithmetic and copies ran while one was open for 0% of the time, Pallas kernels for 33%

profile of v7, /device:TPU:2, one launch (start us, length us, event | category | flops | bytes accessed | tf_op | source)
XLA Modules:
  0.0 72.2 jit_solution(14649181357622266027)
XLA Ops:
  0.6 5.3 %load.1 = (f32[3,4,1056,128]{3,2,1,0:T(8,128)S(1)}, f32[2,4,1024,128]{3,2,1,0:T(8,128)S(1)}, f32[4,1056,128]{2,1,0:T(8,128)S(1)}, f32[3,4,1056,128]{3,2,1,0:T(8,...) custom-call(f32[3,1024,512]{2,1,0:T(8,128)} %bitcast.11, ...), custom_call_target="tpu_custom_call" | custom-call | tf_op jit(solution)/shard_map/load/pallas_call | solution.py:611
  5.9 4.1 %collective-permute-start.1 = (f32[3,4,64,128]{3,2,1,0:T(8,128)S(1)}, f32[3,4,64,128]{3,2,1,0:T(8,128)S(1)}, u32[]{:S(2)}, u32[]{:S(2)}) collective-permute-start(f32[3,4,64,128]{3,2,1,0:T(8,128)S(1)} %get-tuple-element.64.sb), channel_id=1, source_target_pairs={{0,15},{1,2},{2,1},{3,4},{4,3},{5,6},{6,5},{7,8},{8,7},{9,10},{10,... | collective-permute-start | bytes 1179656 | tf_op jit(solution)/shard_map/ppermute | solution.py:630
  10.0 1.9 %collective-permute-start.2 = (f32[2,4,16,128]{3,2,1,0:T(8,128)S(1)}, f32[2,4,16,128]{3,2,1,0:T(8,128)S(1)}, u32[]{:S(2)}, u32[]{:S(2)}) collective-permute-start(f32[2,4,16,128]{3,2,1,0:T(8,128)S(1)} %get-tuple-element.65.sl), channel_id=1, source_target_pairs={{0,16},{16,0},{32,48},{48,32},{64,80},{80,64},{96,112},{112,96},{1... | collective-permute-start | bytes 196616 | tf_op jit(solution)/shard_map/ppermute | solution.py:645
  11.9 3.4 %collective-permute-start.3 = (f32[2,4,16,128]{3,2,1,0:T(8,128)S(1)}, f32[2,4,16,128]{3,2,1,0:T(8,128)S(1)}, u32[]{:S(2)}, u32[]{:S(2)}) collective-permute-start(f32[2,4,16,128]{3,2,1,0:T(8,128)S(1)} %get-tuple-element.66.sh), channel_id=1, source_target_pairs={{0,1},{1,0},{2,3},{3,2},{4,5},{5,4},{6,7},{7,6},{8,9},{9,8},{10,11... | collective-permute-start | bytes 196616 | tf_op jit(solution)/shard_map/ppermute | solution.py:644
  15.3 7.7 %faces.1 = (f32[3,4,1056,128]{3,2,1,0:T(8,128)S(1)}, f32[3,4,1056,128]{3,2,1,0:T(8,128)S(1)}, f32[3,4,1056,128]{3,2,1,0:T(8,128)S(1)}, f32[3,4,1056,128]{3,2,1,0...) custom-call(f32[3,1024,512]{2,1,0:T(8,128)} %bitcast.12, ...), custom_call_target="tpu_custom_call", output_to_operand_aliasing={{0}: (5, {}), {1}: (6, {})} | custom-call | flops 10000000 | bytes 16777216 | tf_op jit(solution)/shard_map/faces/pallas_call | solution.py:611
  23.1 0.7 %collective-permute-done.3.hh.rh = f32[2,4,16,128]{3,2,1,0:T(8,128)S(1)} collective-permute-done((f32[2,4,16,128]{3,2,1,0:T(8,128)S(1)}, f32[2,4,16,128]{3,2,1,0:T(8,128)S(1)}, u32[]{:S(2)}, u32[]{:S(2)}) %collective-permute-start.3) | collective-permute-done | bytes 65568 | tf_op jit(solution)/shard_map/ppermute | solution.py:644
  23.8 0.9 %edges1.1 = (f32[3,4,1056,128]{3,2,1,0:T(8,128)S(1)}, f32[4,1056,128]{2,1,0:T(8,128)S(1)}, f32[4,1056,128]{2,1,0:T(8,128)S(1)}, f32[4,1056,128]{2,1,0:T(8,128)S(...) custom-call(f32[2,4,64,128]{3,2,1,0:T(8,128)S(1)} %collective-permut, ...), custom_call_target="tpu_custom_call", output_to_operand_aliasing={{0}: (10, {}), {1}: (11, {}), {2}: (12, {}), {3}: (13, {})} | custom-call | tf_op jit(solution)/shard_map/edges1/pallas_call | solution.py:611
  24.8 0.1 collective-permute-start.6
  24.9 0.1 collective-permute-start.4
  25.0 1.3 %collective-permute-start.5 = (f32[4,104,128]{2,1,0:T(8,128)S(1)}, f32[4,104,128]{2,1,0:T(8,128)S(1)}, u32[]{:S(2)}, u32[]{:S(2)}) collective-permute-start(f32[4,104,128]{2,1,0:T(8,128)S(1)} %get-tuple-element.74), channel_id=1, source_target_pairs={{0,1},{1,0},{2,3},{3,2},{4,5},{5,4},{6,7},{7,6},{8,9},{9,8},{10,11... | collective-permute-start | bytes 638984 | tf_op jit(solution)/shard_map/ppermute | solution.py:644
  26.2 2.4 %collective-permute-start.7 = (f32[1,4,64,128]{3,2,1,0:T(8,128)S(1)}, f32[1,4,64,128]{3,2,1,0:T(8,128)S(1)}, u32[]{:S(2)}, u32[]{:S(2)}) collective-permute-start(f32[1,4,64,128]{3,2,1,0:T(8,128)S(1)} %get-tuple-element.87), channel_id=1, source_target_pairs={{0,15},{1,2},{2,1},{3,4},{4,3},{5,6},{6,5},{7,8},{8,7},{9,10},{10,... | collective-permute-start | bytes 393224 | tf_op jit(solution)/shard_map/ppermute | solution.py:630
  28.6 5.3 %sweep1.1 = (f32[4,1056,128]{2,1,0:T(8,128)S(1)}, f32[3,4,1056,128]{3,2,1,0:T(8,128)S(1)}) custom-call(f32[4,1056,128]{2,1,0:T(8,128)S(1)} %get-tuple-element.77.phi.old, f32[3,4,1056,128]{3,2,1,0:T(8,128)S(1)} %get-tuple-element.75.f, f32[4,1056,128]{2,1,0:T(8,128)S(1)} %get-tuple-element.78.src, ...), custom_call_target="tpu_custom_call", output_to_operand_aliasing={{1}: (6, {})} | custom-call | flops 10000000 | bytes 16777216 | tf_op jit(solution)/shard_map/sweep1/pallas_call | solution.py:611
  33.9 2.6 %collective-permute-done.7.hb = f32[1,4,64,128]{3,2,1,0:T(8,128)S(1)} collective-permute-done((f32[1,4,64,128]{3,2,1,0:T(8,128)S(1)}, f32[1,4,64,128]{3,2,1,0:T(8,128)S(1)}, u32[]{:S(2)}, u32[]{:S(2)}) %collective-permute-start.7) | collective-permute-done | bytes 131104 | tf_op jit(solution)/shard_map/ppermute | solution.py:630
  36.4 0.4 edges2.1
  36.9 3.1 %collective-permute-start.9 = (f32[1,4,80,128]{3,2,1,0:T(8,128)S(1)}, f32[1,4,80,128]{3,2,1,0:T(8,128)S(1)}, u32[]{:S(2)}, u32[]{:S(2)}) collective-permute-start(f32[1,4,80,128]{3,2,1,0:T(8,128)S(1)} %get-tuple-element.91), channel_id=1, source_target_pairs={{0,15},{1,2},{2,1},{3,4},{4,3},{5,6},{6,5},{7,8},{8,7},{9,10},{10,... | collective-permute-start | bytes 491528 | tf_op jit(solution)/shard_map/ppermute | solution.py:630
  39.9 0.4 sweep2.1
  40.4 2.5 %collective-permute-start.14 = (f32[3,4,64,128]{3,2,1,0:T(8,128)S(1)}, f32[3,4,64,128]{3,2,1,0:T(8,128)S(1)}, u32[]{:S(2)}, u32[]{:S(2)}) collective-permute-start(f32[3,4,64,128]{3,2,1,0:T(8,128)S(1)} %get-tuple-element.99), channel_id=1, source_target_pairs={{0,15},{1,2},{2,1},{3,4},{4,3},{5,6},{6,5},{7,8},{8,7},{9,10},{10,... | collective-permute-start | bytes 1179656 | tf_op jit(solution)/shard_map/ppermute | solution.py:630
  42.9 2.1 %rest2.1.phi_in = f32[4,1056,128]{2,1,0:T(8,128)S(1)} custom-call(f32[4,1056,128]{2,1,0:T(8,128)S(1)} %get-tuple-element.88.phi, f32[3,4,1056,128]{3,2,1,0:T(8,128)S(1)} %get-tuple-element.75.f, f32[4,1056,128]{2,1,0:T(8,128)S(1)} %get-tuple-element.78.src, f32[4,1056,128]{2,1,0:T(8,128)S(1)} %get-tuple-element.79.inv, ...), custom_call_target="tpu_custom_call", output_to_operand_aliasing={{}: (4, {})} | custom-call | flops 10000000 | bytes 16777216 | tf_op jit(solution)/shard_map/rest2/pallas_call | solution.py:611
  44.9 1.1 %collective-permute-done.9.hb = f32[1,4,80,128]{3,2,1,0:T(8,128)S(1)} collective-permute-done((f32[1,4,80,128]{3,2,1,0:T(8,128)S(1)}, f32[1,4,80,128]{3,2,1,0:T(8,128)S(1)}, u32[]{:S(2)}, u32[]{:S(2)}) %collective-permute-start.9) | collective-permute-done | bytes 163872 | tf_op jit(solution)/shard_map/ppermute | solution.py:630
  46.1 0.4 edges3.1
  46.4 0.1 collective-permute-start.10
  46.5 3.7 %collective-permute-start.11 = (f32[1,4,64,128]{3,2,1,0:T(8,128)S(1)}, f32[1,4,64,128]{3,2,1,0:T(8,128)S(1)}, u32[]{:S(2)}, u32[]{:S(2)}) collective-permute-start(f32[1,4,64,128]{3,2,1,0:T(8,128)S(1)} %get-tuple-element.96), channel_id=1, source_target_pairs={{0,15},{1,2},{2,1},{3,4},{4,3},{5,6},{6,5},{7,8},{8,7},{9,10},{10,... | collective-permute-start | bytes 393224 | tf_op jit(solution)/shard_map/ppermute | solution.py:630
  50.2 3.1 %collective-permute-start.13 = (f32[3,4,16,128]{3,2,1,0:T(8,128)S(1)}, f32[3,4,16,128]{3,2,1,0:T(8,128)S(1)}, u32[]{:S(2)}, u32[]{:S(2)}) collective-permute-start(f32[3,4,16,128]{3,2,1,0:T(8,128)S(1)} %get-tuple-element.98), channel_id=1, source_target_pairs={{0,1},{1,0},{2,3},{3,2},{4,5},{5,4},{6,7},{7,6},{8,9},{9,8},{10,11... | collective-permute-start | bytes 294920 | tf_op jit(solution)/shard_map/ppermute | solution.py:644
  53.4 3.9 %sweep3.1 = (f32[4,1056,128]{2,1,0:T(8,128)S(1)}, f32[3,4,1056,128]{3,2,1,0:T(8,128)S(1)}) custom-call(f32[4,1056,128]{2,1,0:T(8,128)S(1)} %get-tuple-element.92.phi.old, f32[3,4,1056,128]{3,2,1,0:T(8,128)S(1)} %get-tuple-element.75.f, f32[4,1056,128]{2,1,0:T(8,128)S(1)} %get-tuple-element.78.src, ...), custom_call_target="tpu_custom_call", output_to_operand_aliasing={{1}: (6, {})} | custom-call | flops 10000000 | bytes 16777216 | tf_op jit(solution)/shard_map/sweep3/pallas_call | solution.py:611
  57.3 2.4 %collective-permute-done.13.rest_1_.rest_7_ = f32[3,4,16,128]{3,2,1,0:T(8,128)S(1)} collective-permute-done((f32[3,4,16,128]{3,2,1,0:T(8,128)S(1)}, f32[3,4,16,128]{3,2,1,0:T(8,128)S(1)}, u32[]{:S(2)}, u32[]{:S(2)}) %collective-permute-start.13) | collective-permute-done | bytes 98336 | tf_op jit(solution)/shard_map/ppermute | solution.py:644
  59.7 0.0 slice-start
  59.8 0.4 edges4.1
  60.2 2.7 %collective-permute-start.16 = (f32[1,4,80,128]{3,2,1,0:T(8,128)S(1)}, f32[1,4,80,128]{3,2,1,0:T(8,128)S(1)}, u32[]{:S(2)}, u32[]{:S(2)}) collective-permute-start(f32[1,4,80,128]{3,2,1,0:T(8,128)S(1)} %get-tuple-element.101), channel_id=1, source_target_pairs={{0,15},{1,2},{2,1},{3,4},{4,3},{5,6},{6,5},{7,8},{8,7},{9,10},{10,... | collective-permute-start | bytes 491528 | tf_op jit(solution)/shard_map/ppermute | solution.py:630
  62.9 0.3 copy-done.1
  63.2 4.1 %force.1 = (f32[1024,512]{1,0:T(8,128)}, f32[3,1024,512]{2,1,0:T(8,128)}, f32[3,4,1056,128]{3,2,1,0:T(8,128)S(1)}) custom-call(f32[4,1056,128]{2,1,0:T(8,128)S(1)} %get-tuple-element.102.phi, f32[4,1056,128]{2,1,0:T(8,128)S(1)} %copy-done.1, f32[3,1024,512]{2,1,0:T(8,128)S(1)} %bitcast.10, ...), custom_call_target="tpu_custom_call", output_to_operand_aliasing={{2}: (13, {})} | custom-call | flops 10000000 | bytes 16777216 | tf_op jit(solution)/shard_map/force/pallas_call | solution.py:611
  67.4 2.2 %collective-permute-done.16.hb = f32[1,4,80,128]{3,2,1,0:T(8,128)S(1)} collective-permute-done((f32[1,4,80,128]{3,2,1,0:T(8,128)S(1)}, f32[1,4,80,128]{3,2,1,0:T(8,128)S(1)}, u32[]{:S(2)}, u32[]{:S(2)}) %collective-permute-start.16) | collective-permute-done | bytes 163872 | tf_op jit(solution)/shard_map/ppermute | solution.py:630
  69.5 2.5 %last.1 = (f32[3,1024,512]{2,1,0:T(8,128)}, f32[3,4,1056,128]{3,2,1,0:T(8,128)S(1)}) custom-call(f32[2,4,64,128]{3,2,1,0:T(8,128)S(1)} %get-tuple-element.59.ka, f32[2,4,64,128]{3,2,1,0:T(8,128)S(1)} %get-tuple-element.60.kb, f32[2,4,16,128]{3,2,1,0:T(8,128)S(1)} %get-tuple-element.61.kl, ...), custom_call_target="tpu_custom_call", output_to_operand_aliasing={{1}: (8, {}), {0}: (9, {})} | custom-call | tf_op jit(solution)/shard_map/last/pallas_call | solution.py:611
  (23 shorter events, 0.1 us)
Async XLA Ops:
  5.9 17.2 %copy-start = (f32[4,1056,128]{2,1,0:T(8,128)}, f32[4,1056,128]{2,1,0:T(8,128)S(1)}, u32[]{:S(2)}) copy-start(f32[4,1056,128]{2,1,0:T(8,128)S(1)} %get-tuple-element.55.hat) | copy-start | bytes 6488068
  5.9 17.9 %collective-permute-start.1 = (f32[3,4,64,128]{3,2,1,0:T(8,128)S(1)}, f32[3,4,64,128]{3,2,1,0:T(8,128)S(1)}, u32[]{:S(2)}, u32[]{:S(2)}) collective-permute-start(f32[3,4,64,128]{3,2,1,0:T(8,128)S(1)} %get-tuple-element.64.sb), channel_id=1, source_target_pairs={{0,15},{1,2},{2,1},{3,4},{4,3},{5,6},{6,5},{7,8},{8,7},{9,10},{10,... | collective-permute-start | bytes 1179656 | tf_op jit(solution)/shard_map/ppermute | solution.py:630
  10.0 13.8 %collective-permute-start = (f32[2,4,64,128]{3,2,1,0:T(8,128)S(1)}, f32[2,4,64,128]{3,2,1,0:T(8,128)S(1)}, u32[]{:S(2)}, u32[]{:S(2)}) collective-permute-start(f32[2,4,64,128]{3,2,1,0:T(8,128)S(1)} %get-tuple-element.63.sa), channel_id=1, source_target_pairs={{0,1},{1,0},{2,3},{3,2},{4,5},{5,4},{6,7},{7,6},{8,9},{9,8},{10,11... | collective-permute-start | bytes 786440 | tf_op jit(solution)/shard_map/ppermute | solution.py:635
  10.0 13.1 %collective-permute-start.2 = (f32[2,4,16,128]{3,2,1,0:T(8,128)S(1)}, f32[2,4,16,128]{3,2,1,0:T(8,128)S(1)}, u32[]{:S(2)}, u32[]{:S(2)}) collective-permute-start(f32[2,4,16,128]{3,2,1,0:T(8,128)S(1)} %get-tuple-element.65.sl), channel_id=1, source_target_pairs={{0,16},{16,0},{32,48},{48,32},{64,80},{80,64},{96,112},{112,96},{1... | collective-permute-start | bytes 196616 | tf_op jit(solution)/shard_map/ppermute | solution.py:645
  11.9 11.9 %collective-permute-start.3 = (f32[2,4,16,128]{3,2,1,0:T(8,128)S(1)}, f32[2,4,16,128]{3,2,1,0:T(8,128)S(1)}, u32[]{:S(2)}, u32[]{:S(2)}) collective-permute-start(f32[2,4,16,128]{3,2,1,0:T(8,128)S(1)} %get-tuple-element.66.sh), channel_id=1, source_target_pairs={{0,1},{1,0},{2,3},{3,2},{4,5},{5,4},{6,7},{7,6},{8,9},{9,8},{10,11... | collective-permute-start | bytes 196616 | tf_op jit(solution)/shard_map/ppermute | solution.py:644
  24.8 11.6 %collective-permute-start.6 = (f32[4,4,64,128]{3,2,1,0:T(8,128)S(1)}, f32[4,4,64,128]{3,2,1,0:T(8,128)S(1)}, u32[]{:S(2)}, u32[]{:S(2)}) collective-permute-start(f32[4,4,64,128]{3,2,1,0:T(8,128)S(1)} %get-tuple-element.86), channel_id=1, source_target_pairs={{0,1},{1,0},{2,3},{3,2},{4,5},{5,4},{6,7},{7,6},{8,9},{9,8},{10,11... | collective-permute-start | bytes 1572872 | tf_op jit(solution)/shard_map/ppermute | solution.py:635
  24.9 11.5 %collective-permute-start.4 = (f32[4,104,128]{2,1,0:T(8,128)S(1)}, f32[4,104,128]{2,1,0:T(8,128)S(1)}, u32[]{:S(2)}, u32[]{:S(2)}) collective-permute-start(f32[4,104,128]{2,1,0:T(8,128)S(1)} %get-tuple-element.73), channel_id=1, source_target_pairs={{0,16},{16,0},{32,48},{48,32},{64,80},{80,64},{96,112},{112,96},{1... | collective-permute-start | bytes 638984 | tf_op jit(solution)/shard_map/ppermute | solution.py:645
  25.0 11.5 %collective-permute-start.5 = (f32[4,104,128]{2,1,0:T(8,128)S(1)}, f32[4,104,128]{2,1,0:T(8,128)S(1)}, u32[]{:S(2)}, u32[]{:S(2)}) collective-permute-start(f32[4,104,128]{2,1,0:T(8,128)S(1)} %get-tuple-element.74), channel_id=1, source_target_pairs={{0,1},{1,0},{2,3},{3,2},{4,5},{5,4},{6,7},{7,6},{8,9},{9,8},{10,11... | collective-permute-start | bytes 638984 | tf_op jit(solution)/shard_map/ppermute | solution.py:644
  26.2 10.2 %collective-permute-start.7 = (f32[1,4,64,128]{3,2,1,0:T(8,128)S(1)}, f32[1,4,64,128]{3,2,1,0:T(8,128)S(1)}, u32[]{:S(2)}, u32[]{:S(2)}) collective-permute-start(f32[1,4,64,128]{3,2,1,0:T(8,128)S(1)} %get-tuple-element.87), channel_id=1, source_target_pairs={{0,15},{1,2},{2,1},{3,4},{4,3},{5,6},{6,5},{7,8},{8,7},{9,10},{10,... | collective-permute-start | bytes 393224 | tf_op jit(solution)/shard_map/ppermute | solution.py:630
  36.9 9.2 %collective-permute-start.9 = (f32[1,4,80,128]{3,2,1,0:T(8,128)S(1)}, f32[1,4,80,128]{3,2,1,0:T(8,128)S(1)}, u32[]{:S(2)}, u32[]{:S(2)}) collective-permute-start(f32[1,4,80,128]{3,2,1,0:T(8,128)S(1)} %get-tuple-element.91), channel_id=1, source_target_pairs={{0,15},{1,2},{2,1},{3,4},{4,3},{5,6},{6,5},{7,8},{8,7},{9,10},{10,... | collective-permute-start | bytes 491528 | tf_op jit(solution)/shard_map/ppermute | solution.py:630
  39.9 5.0 %collective-permute-start.8 = (f32[1,4,72,128]{3,2,1,0:T(8,128)S(1)}, f32[1,4,72,128]{3,2,1,0:T(8,128)S(1)}, u32[]{:S(2)}, u32[]{:S(2)}) collective-permute-start(f32[1,4,72,128]{3,2,1,0:T(8,128)S(1)} %get-tuple-element.90), channel_id=1, source_target_pairs={{0,1},{1,0},{2,3},{3,2},{4,5},{5,4},{6,7},{7,6},{8,9},{9,8},{10,11... | collective-permute-start | bytes 442376 | tf_op jit(solution)/shard_map/ppermute | solution.py:635
  40.4 19.4 %collective-permute-start.14 = (f32[3,4,64,128]{3,2,1,0:T(8,128)S(1)}, f32[3,4,64,128]{3,2,1,0:T(8,128)S(1)}, u32[]{:S(2)}, u32[]{:S(2)}) collective-permute-start(f32[3,4,64,128]{3,2,1,0:T(8,128)S(1)} %get-tuple-element.99), channel_id=1, source_target_pairs={{0,15},{1,2},{2,1},{3,4},{4,3},{5,6},{6,5},{7,8},{8,7},{9,10},{10,... | collective-permute-start | bytes 1179656 | tf_op jit(solution)/shard_map/ppermute | solution.py:630
  46.4 13.3 %collective-permute-start.10 = (f32[2,4,64,128]{3,2,1,0:T(8,128)S(1)}, f32[2,4,64,128]{3,2,1,0:T(8,128)S(1)}, u32[]{:S(2)}, u32[]{:S(2)}) collective-permute-start(f32[2,4,64,128]{3,2,1,0:T(8,128)S(1)} %get-tuple-element.95), channel_id=1, source_target_pairs={{0,1},{1,0},{2,3},{3,2},{4,5},{5,4},{6,7},{7,6},{8,9},{9,8},{10,11... | collective-permute-start | bytes 786440 | tf_op jit(solution)/shard_map/ppermute | solution.py:635
  46.5 13.2 %collective-permute-start.11 = (f32[1,4,64,128]{3,2,1,0:T(8,128)S(1)}, f32[1,4,64,128]{3,2,1,0:T(8,128)S(1)}, u32[]{:S(2)}, u32[]{:S(2)}) collective-permute-start(f32[1,4,64,128]{3,2,1,0:T(8,128)S(1)} %get-tuple-element.96), channel_id=1, source_target_pairs={{0,15},{1,2},{2,1},{3,4},{4,3},{5,6},{6,5},{7,8},{8,7},{9,10},{10,... | collective-permute-start | bytes 393224 | tf_op jit(solution)/shard_map/ppermute | solution.py:630
  50.2 7.0 %collective-permute-start.12 = (f32[3,4,16,128]{3,2,1,0:T(8,128)S(1)}, f32[3,4,16,128]{3,2,1,0:T(8,128)S(1)}, u32[]{:S(2)}, u32[]{:S(2)}) collective-permute-start(f32[3,4,16,128]{3,2,1,0:T(8,128)S(1)} %get-tuple-element.97), channel_id=1, source_target_pairs={{0,16},{16,0},{32,48},{48,32},{64,80},{80,64},{96,112},{112,96},{1... | collective-permute-start | bytes 294920 | tf_op jit(solution)/shard_map/ppermute | solution.py:645
  50.2 9.5 %collective-permute-start.13 = (f32[3,4,16,128]{3,2,1,0:T(8,128)S(1)}, f32[3,4,16,128]{3,2,1,0:T(8,128)S(1)}, u32[]{:S(2)}, u32[]{:S(2)}) collective-permute-start(f32[3,4,16,128]{3,2,1,0:T(8,128)S(1)} %get-tuple-element.98), channel_id=1, source_target_pairs={{0,1},{1,0},{2,3},{3,2},{4,5},{5,4},{6,7},{7,6},{8,9},{9,8},{10,11... | collective-permute-start | bytes 294920 | tf_op jit(solution)/shard_map/ppermute | solution.py:644
  59.7 3.2 %slice-start = ((s8[6291456]{0:T(1024)(128)(4,1)}), s8[4194304]{0:T(1024)(128)(4,1)S(1)}, s32[]{:S(2)}) async-start(s8[6291456]{0:T(1024)(128)(4,1)} %bitcast.8), calls=%async_computation | async-start | bytes 8388608
  59.7 3.2 %slice-start.1 = ((s8[6291456]{0:T(1024)(128)(4,1)}), s8[2097152]{0:T(1024)(128)(4,1)S(1)}, s32[]{:S(2)}) async-start(s8[6291456]{0:T(1024)(128)(4,1)} %bitcast.8), calls=%async_computation.1 | async-start | bytes 4194304
  59.7 3.5 %copy-start.1 = (f32[4,1056,128]{2,1,0:T(8,128)S(1)}, f32[4,1056,128]{2,1,0:T(8,128)}, u32[]{:S(2)}) copy-start(f32[4,1056,128]{2,1,0:T(8,128)} %copy-done) | copy-start | bytes 6488068
  60.2 9.3 %collective-permute-start.16 = (f32[1,4,80,128]{3,2,1,0:T(8,128)S(1)}, f32[1,4,80,128]{3,2,1,0:T(8,128)S(1)}, u32[]{:S(2)}, u32[]{:S(2)}) collective-permute-start(f32[1,4,80,128]{3,2,1,0:T(8,128)S(1)} %get-tuple-element.101), channel_id=1, source_target_pairs={{0,15},{1,2},{2,1},{3,4},{4,3},{5,6},{6,5},{7,8},{8,7},{9,10},{10,... | collective-permute-start | bytes 491528 | tf_op jit(solution)/shard_map/ppermute | solution.py:630
  62.9 4.4 %collective-permute-start.15 = (f32[1,4,72,128]{3,2,1,0:T(8,128)S(1)}, f32[1,4,72,128]{3,2,1,0:T(8,128)S(1)}, u32[]{:S(2)}, u32[]{:S(2)}) collective-permute-start(f32[1,4,72,128]{3,2,1,0:T(8,128)S(1)} %get-tuple-element.100), channel_id=1, source_target_pairs={{0,1},{1,0},{2,3},{3,2},{4,5},{5,4},{6,7},{7,6},{8,9},{9,8},{10,11... | collective-permute-start | bytes 442376 | tf_op jit(solution)/shard_map/ppermute | solution.py:635
